TPU v7x, 32 devices: a whole 2x2x4 slice. The times are simulated.
32 devices in a mesh: seq: 4 (over y, x), fsdp: 8 (over z, core).
Axes of the slice: x: 2, y: 2, z: 4, core: 2. Of those that a mesh axis runs over, the one named last changes fastest.
Arguments:
- hidden_in: bfloat16 [16, 1024, 1024], P('fsdp', 'seq'), may hold values from -6 to 6
- segments: int32 [16, 1024], P('fsdp'), may hold values from 0 to 17, as said below
- q_weight: bfloat16 [1024, 1024], P('fsdp'), may hold values from -0.1875 to 0.1875
- k_weight: bfloat16 [1024, 1024], P('fsdp'), may hold values from -0.1875 to 0.1875
- v_weight: bfloat16 [1024, 1024], P('fsdp'), may hold values from -0.1875 to 0.1875
- out_weight: bfloat16 [1024, 1024], P('fsdp'), may hold values from -0.75 to 0.75
- q_bias: bfloat16 [1024], P('fsdp'), may hold values from -3 to 3
- v_bias: bfloat16 [1024], P('fsdp'), may hold values from -3 to 3
- out_bias: bfloat16 [1024], P('fsdp'), may hold values from -3 to 3
- up_weight: bfloat16 [1024, 4096], P('fsdp'), may hold values from -0.1875 to 0.1875
- up_bias: bfloat16 [4096], P('fsdp'), may hold values from -3 to 3
- down_weight: bfloat16 [4096, 1024], P('fsdp'), may hold values from -0.09375 to 0.09375
- down_bias: bfloat16 [1024], P('fsdp'), may hold values from -3 to 3
- norm1_gain: bfloat16 [1024], P('fsdp'), may hold values from 0.5 to 1.5
- norm1_bias: bfloat16 [1024], P('fsdp'), may hold values from -3 to 3
- norm2_gain: bfloat16 [1024], P('fsdp'), may hold values from 0.5 to 1.5
- norm2_bias: bfloat16 [1024], P('fsdp'), may hold values from -3 to 3
- out_grad: bfloat16 [16, 1024, 1024], P('fsdp', 'seq'), may hold values from -6 to 6
Outputs:
- layer_out: bfloat16 [16, 1024, 1024], P('fsdp', 'seq')
- input_grad: float32 [16, 1024, 1024], P('fsdp', 'seq')
- q_weight_grad: float32 [1024, 1024], P('fsdp')
- k_weight_grad: float32 [1024, 1024], P('fsdp')
- v_weight_grad: float32 [1024, 1024], P('fsdp')
- out_weight_grad: float32 [1024, 1024], P('fsdp')
- q_bias_grad: float32 [1024], P('fsdp')
- v_bias_grad: float32 [1024], P('fsdp')
- out_bias_grad: float32 [1024], P('fsdp')
- up_weight_grad: float32 [1024, 4096], P('fsdp')
- up_bias_grad: float32 [4096], P('fsdp')
- down_weight_grad: float32 [4096, 1024], P('fsdp')
- down_bias_grad: float32 [1024], P('fsdp')
- norm1_gain_grad: float32 [1024], P('fsdp')
- norm1_bias_grad: float32 [1024], P('fsdp')
- norm2_gain_grad: float32 [1024], P('fsdp')
- norm2_bias_grad: float32 [1024], P('fsdp')
Inputs may be any that keep to these rules, and one draw needn't show every extreme that they name: `segments`: along a sequence the numbers start at 1 and rise by one at each new document, then end in a tail of 0. Documents are at least max(60, 2) tokens long. In every aligned group of 2 sequences one sequence is a single document of all 1024 tokens and another holds the most documents; every sequence but the single document ends in 1 to 128 pad tokens.
All inputs are finite; a program needn't handle non-finite values.
Results may differ from a plain program's by a relative error of at most 0.02.
Values may be sent and summed in bfloat16 or wider, within the bound.
No kernel may reach another device: no remote copies, remote signals or barrier semaphores. Data moves between devices by JAX's collectives and lax.ppermute only.
A program may use at most 192 MiB of HBM per device.

v0:
```python
import functools

import jax
import jax.numpy as jnp
from jax import lax
from jax.experimental import pallas as pl
from jax.experimental.pallas import tpu as pltpu
from jax.sharding import Mesh
from jax.sharding import PartitionSpec as P

HEAD_DIM = 64
SPAN = 128
MASKED = -1e30


def dot(a,b,ca,cb):
    return lax.dot_general(a,b,(((ca,),(cb,)),((),())),preferred_element_type=jnp.float32)


TILE = 256


def run(kernel, name, grid, ins, outs, shapes, operands, prefetch=(), scratch=(), alias=None, waits=(), cost=10):
    known = len(prefetch) + len(ins)

    def waiting(*refs):
        kernel(*refs[:known], *refs[known + len(waits) :])

    ins = list(ins) + [pl.BlockSpec(memory_space=pl.ANY)] * len(waits)
    operands = list(operands) + list(waits)
    return pl.pallas_call(
        waiting,
        grid_spec=pltpu.PrefetchScalarGridSpec(
            num_scalar_prefetch=len(prefetch), grid=grid, in_specs=ins, out_specs=outs, scratch_shapes=scratch
        ),
        out_shape=shapes,
        input_output_aliases=alias or {},
        compiler_params=pltpu.CompilerParams(vmem_limit_bytes=28 << 20),
        cost_estimate=pl.CostEstimate(flops=cost * 1000000000, bytes_accessed=1000, transcendentals=0),
        name=name,
    )(*prefetch, *operands)


def fixed(array):
    rank = array.ndim
    return pl.BlockSpec(array.shape, lambda *_: (0,) * rank, pipeline_mode=pl.Buffered(buffer_count=1))


class View:
    def __init__(self, array, i=None):
        self.array, self.i = array, i
        self.shape = array.shape if i is None else array.shape[1:]

    def spec(self, block, place):
        i = self.i
        if i is None:
            return pl.BlockSpec(block, place)
        return pl.BlockSpec((None,) + tuple(block), lambda *a: (i,) + tuple(place(*a)))

    def whole(self):
        rank, i = len(self.shape), self.i
        once = pl.Buffered(buffer_count=1)
        if i is None:
            return pl.BlockSpec(self.shape, lambda *_: (0,) * rank, pipeline_mode=once)
        return pl.BlockSpec((None,) + tuple(self.shape), lambda *_: (i,) + (0,) * rank, pipeline_mode=once)

    def value(self):
        return self.array if self.i is None else self.array[self.i]


def arrays(views):
    return [v.array for v in views]


def kind_of(shape, dtype=jnp.bfloat16):
    return jax.ShapeDtypeStruct(tuple(shape), dtype)


def wide(tensor):
    return tensor.astype(jnp.float32)


def standardize(values):
    center = jnp.mean(values, axis=1, keepdims=True)
    offset = values - center
    inverse = lax.rsqrt(jnp.mean(offset * offset, axis=1, keepdims=True) + 1e-05)
    return offset * inverse, inverse


def standardize_back(upstream, normed, inverse, gain):
    scaled = upstream * gain
    return inverse * (
        scaled
        - jnp.mean(scaled, axis=1, keepdims=True)
        - normed * jnp.mean(scaled * normed, axis=1, keepdims=True)
    )


def column_sum(values):
    return jnp.sum(values, axis=0, keepdims=True)


OUT_BIAS, DOWN_BIAS, GAIN_ONE, SHIFT_ONE, GAIN_TWO, SHIFT_TWO = 2, 3, 4, 5, 6, 7


def project(places, blocks, weight, bias, scale):
    seqs, length, width = blocks[0].shape
    ranks = len(blocks)
    out_width = weight.shape[1]

    def kernel(place_ref, weight_ref, bias_ref, scale_ref, *refs):
        for q in range(ranks):

            @pl.when(pl.program_id(0) // seqs == q)
            def _(q=q):
                product = dot(refs[q][0], weight_ref[...], 1, 0) + bias_ref[...]
                refs[ranks][0] = (product * scale_ref[...]).astype(jnp.bfloat16)

    def source(q):
        return lambda i, p: (jnp.clip(i - q * seqs, 0, seqs - 1), 0, 0)

    return run(
        kernel,
        "project",
        (ranks * seqs,),
        [fixed(weight), fixed(bias), fixed(scale)]
        + [blocks[q].spec((1, length, width), source(q)) for q in range(ranks)],
        pl.BlockSpec((1, length, out_width), lambda i, p: (i % seqs, p[i // seqs], 0)),
        kind_of((seqs, length * ranks, out_width)),
        [weight, bias, scale, *arrays(blocks)],
        prefetch=(places,),
    )


def out_norm(places, contexts, weight, hidden, vectors, waits=()):
    seqs, length, width = hidden.shape
    ranks = len(contexts)
    part = contexts[0].shape[2]

    def kernel(place_ref, *refs):
        weight_ref, hidden_ref, vector_ref, sum_ref, first_ref = refs[ranks:]
        total = wide(hidden_ref[0]) + vector_ref[OUT_BIAS : OUT_BIAS + 1, :]
        for q in range(ranks):
            rows = pl.ds(pl.multiple_of(place_ref[q] * part, part), part)
            total = total + dot(refs[q][0], weight_ref[rows, :], 1, 0)
        sum_ref[0] = total
        normed, _ = standardize(total)
        first = normed * vector_ref[GAIN_ONE : GAIN_ONE + 1, :] + vector_ref[SHIFT_ONE : SHIFT_ONE + 1, :]
        first_ref[0] = first.astype(jnp.bfloat16)

    tokens = pl.BlockSpec((1, length, width), lambda b, p: (b, 0, 0))
    return run(
        kernel,
        "out_norm",
        (seqs,),
        [pl.BlockSpec((1, length, part), lambda b, p: (b, 0, 0))] * ranks + [fixed(weight), tokens, fixed(vectors)],
        [tokens, tokens],
        [kind_of(hidden.shape, jnp.float32), kind_of(hidden.shape)],
        [*contexts, weight, hidden, vectors],
        prefetch=(places,),
        waits=waits,
    )


def up_forward(own, other, weights, biases, waits=()):
    count, width = own.shape
    units = weights[0].shape[1]
    blocks = len(weights)
    tile = min(TILE, count)
    half = count // tile

    def kernel(own_ref, other_ref, *refs):
        def body(tokens):
            for q in range(blocks):
                upper = dot(tokens, refs[q][...], 1, 0) + refs[blocks + q][...]
                tail = 0.5 * (1.0 + lax.erf(upper * 0.7071067811865476))
                refs[2 * blocks + q][...] = (upper * tail).astype(jnp.bfloat16)
                bell = jnp.exp(-0.5 * upper * upper) * 0.3989422804014327
                refs[3 * blocks + q][...] = (tail + upper * bell).astype(jnp.bfloat16)

        @pl.when(pl.program_id(0) < half)
        def _():
            body(own_ref[...])

        @pl.when(pl.program_id(0) >= half)
        def _():
            body(other_ref[...])

    outs = run(
        kernel,
        "up_forward",
        (2 * half,),
        [
            pl.BlockSpec((tile, width), lambda i: (jnp.minimum(i, half - 1), 0)),
            pl.BlockSpec((tile, width), lambda i: (jnp.maximum(i - half, 0), 0)),
        ]
        + [w.whole() for w in weights]
        + [fixed(b) for b in biases],
        [pl.BlockSpec((tile, units), lambda i: (i, 0))] * (2 * blocks),
        [kind_of((2 * count, units))] * (2 * blocks),
        [own, other, *arrays(weights), *biases],
        waits=waits,
    )
    return list(outs[:blocks]), list(outs[blocks:])


def down_forward(actives, weights, first, count, dtype, waits=()):
    blocks = len(actives)
    units, width = weights[0].shape
    tile = min(TILE, count)

    def kernel(*refs):
        total = dot(refs[0][...], refs[blocks][...], 1, 0)
        for q in range(1, blocks):
            total = total + dot(refs[q][...], refs[blocks + q][...], 1, 0)
        refs[-1][...] = total.astype(dtype)

    return run(
        kernel,
        "down_forward",
        (count // tile,),
        [pl.BlockSpec((tile, units), lambda i: (i + first // tile, 0))] * blocks + [w.whole() for w in weights],
        pl.BlockSpec((tile, width), lambda i: (i, 0)),
        kind_of((count, width), dtype),
        [*actives, *arrays(weights)],
        waits=waits,
    )


def norm_two(mixed, mixed_other, sums_one, vectors, out_grad, keep):
    seqs, length, width = sums_one.shape

    def kernel(mixed_ref, other_ref, sum_ref, vector_ref, grad_ref, keep_ref, out_ref, dsum_ref, dmixed_ref, total_ref):
        @pl.when(pl.program_id(0) == 0)
        def _():
            total_ref[...] = jnp.zeros_like(total_ref)

        def vector(i):
            return vector_ref[i : i + 1, :]

        normed, _ = standardize(sum_ref[0])
        first = normed * vector(GAIN_ONE) + vector(SHIFT_ONE)
        mixed = mixed_ref[0] + wide(other_ref[0]) + vector(DOWN_BIAS)
        normed, inverse = standardize(first + mixed)
        out_ref[0] = (normed * vector(GAIN_TWO) + vector(SHIFT_TWO)).astype(jnp.bfloat16)
        cot = wide(grad_ref[0]) * keep_ref[0]
        dsum = standardize_back(cot, normed, inverse, vector(GAIN_TWO))
        dsum_ref[0] = dsum
        dmixed = dsum.astype(jnp.bfloat16)
        dmixed_ref[0] = dmixed
        total_ref[0:1, :] += column_sum(wide(dmixed))
        total_ref[1:2, :] += column_sum(cot * normed)
        total_ref[2:3, :] += column_sum(cot)

    tokens = pl.BlockSpec((1, length, width), lambda b: (b, 0, 0))
    shape = sums_one.shape
    return run(
        kernel,
        "norm_two",
        (seqs,),
        [tokens, tokens, tokens, fixed(vectors), tokens, pl.BlockSpec((1, length, 1), lambda b: (b, 0, 0))],
        [tokens, tokens, tokens, pl.BlockSpec((8, width), lambda b: (0, 0))],
        [kind_of(shape), kind_of(shape, jnp.float32), kind_of(shape), kind_of((8, width), jnp.float32)],
        [mixed.reshape(shape), mixed_other.reshape(shape), sums_one, vectors, out_grad, keep],
    )


def ffn_back(own, other, slopes, downs, ups, waits=()):
    blocks = len(slopes)
    count, width = own.shape
    units = slopes[0].shape[1]
    tile = min(TILE, count)
    half = count // tile

    def kernel(own_ref, other_ref, *refs):
        slope_refs, down_refs, up_refs = refs[:blocks], refs[blocks : 2 * blocks], refs[2 * blocks : 3 * blocks]
        upper_refs, total_ref, here_ref, there_ref = refs[3 * blocks : 4 * blocks], refs[-3], refs[-2], refs[-1]
        step = pl.program_id(0)

        @pl.when(step == 0)
        def _():
            total_ref[...] = jnp.zeros_like(total_ref)

        def body(grad):
            total = 0.0
            for q in range(blocks):
                upper = (dot(grad, down_refs[q][...], 1, 1) * wide(slope_refs[q][...])).astype(jnp.bfloat16)
                upper_refs[q][...] = upper
                total_ref[q : q + 1, :] += column_sum(wide(upper))
                total = total + dot(upper, up_refs[q][...], 1, 1)
            return total

        @pl.when(step < half)
        def _():
            there_ref[...] = body(other_ref[...]).astype(jnp.bfloat16)

        @pl.when(step >= half)
        def _():
            here_ref[...] = body(own_ref[...])

    def early(i):
        return (jnp.minimum(i, half - 1), 0)

    def late(i):
        return (jnp.maximum(i - half, 0), 0)

    def both(i):
        return ((i + half) % (2 * half), 0)

    outs = run(
        kernel,
        "feed_forward_back",
        (2 * half,),
        [pl.BlockSpec((tile, width), late), pl.BlockSpec((tile, width), early)]
        + [pl.BlockSpec((tile, units), both)] * blocks
        + [w.whole() for w in (*downs, *ups)],
        [pl.BlockSpec((tile, units), both)] * blocks
        + [
            pl.BlockSpec((max(8, blocks), units), lambda i: (0, 0)),
            pl.BlockSpec((tile, width), late),
            pl.BlockSpec((tile, width), early),
        ],
        [kind_of((2 * count, units))] * blocks
        + [
            kind_of((max(8, blocks), units), jnp.float32),
            kind_of((count, width), jnp.float32),
            kind_of((count, width)),
        ],
        [own, other, *slopes, *arrays(downs), *arrays(ups)],
        waits=waits,
    )
    return list(outs[:blocks]), outs[blocks], outs[blocks + 1], outs[blocks + 2]


def down_grad(actives, own, other, addends, waits=()):
    count, width = own.shape
    units = actives[0].shape[1]
    tile = min(TILE, units)
    blocks = len(actives)
    spread = [(q, a) for q in range(blocks) for a in addends[q]]

    def kernel(own_ref, other_ref, *refs):
        for q in range(blocks):
            total = dot(refs[q][:count, :], own_ref[...], 0, 0) + dot(refs[q][count:, :], other_ref[...], 0, 0)
            for j, (of, _) in enumerate(spread):
                if of == q:
                    total = total + wide(refs[blocks + j][...])
            refs[-1][q] = total.astype(jnp.bfloat16)

    return run(
        kernel,
        "down_grad",
        (units // tile,),
        [fixed(own), fixed(other)]
        + [pl.BlockSpec((2 * count, tile), lambda i: (0, i))] * blocks
        + [a.spec((tile, width), lambda i: (i, 0)) for _, a in spread],
        pl.BlockSpec((blocks, tile, width), lambda i: (0, i, 0)),
        kind_of((blocks, units, width)),
        [own, other, *actives, *(a.array for _, a in spread)],
        waits=waits,
    )


def up_grad(uppers, own, other, addends, waits=()):
    count, width = own.shape
    units = uppers[0].shape[1]
    tile = min(TILE, width)
    blocks = len(uppers)
    spread = [(q, a) for q in range(blocks) for a in addends[q]]

    def kernel(own_ref, other_ref, *refs):
        for q in range(blocks):
            total = dot(own_ref[...], refs[q][:count, :], 0, 0) + dot(other_ref[...], refs[q][count:, :], 0, 0)
            for j, (of, _) in enumerate(spread):
                if of == q:
                    total = total + wide(refs[blocks + j][...])
            refs[-1][q] = total.astype(jnp.bfloat16)

    columns = pl.BlockSpec((count, tile), lambda i: (0, i))
    return run(
        kernel,
        "up_grad",
        (width // tile,),
        [columns, columns]
        + [fixed(u) for u in uppers]
        + [a.spec((tile, units), lambda i: (i, 0)) for _, a in spread],
        pl.BlockSpec((blocks, tile, units), lambda i: (0, i, 0)),
        kind_of((blocks, width, units)),
        [own, other, *uppers, *(a.array for _, a in spread)],
        waits=waits,
    )


def norm_one_back(places, dfirst, dfirst_other, dsum_two, sums_one, vectors, weight, part, waits=()):
    seqs, length, width = sums_one.shape
    ranks = width // part

    def kernel(place_ref, own_ref, other_ref, dsum_ref, sum_ref, vector_ref, weight_ref, *outs):
        @pl.when(pl.program_id(0) == 0)
        def _():
            outs[-1][...] = jnp.zeros_like(outs[-1])

        upstream = dsum_ref[0] + own_ref[0] + wide(other_ref[0])
        normed, inverse = standardize(sum_ref[0])
        dsum = standardize_back(upstream, normed, inverse, vector_ref[GAIN_ONE : GAIN_ONE + 1, :])
        outs[0][0] = dsum
        dbranch = dsum.astype(jnp.bfloat16)
        outs[1][0] = dbranch
        for q in range(ranks):
            rows = pl.ds(pl.multiple_of(place_ref[q] * part, part), part)
            outs[2 + q][0] = dot(dbranch, weight_ref[rows, :], 1, 1).astype(jnp.bfloat16)
        outs[-1][0:1, :] += column_sum(wide(dbranch))
        outs[-1][1:2, :] += column_sum(upstream * normed)
        outs[-1][2:3, :] += column_sum(upstream)

    tokens = pl.BlockSpec((1, length, width), lambda b, p: (b, 0, 0))
    shape = sums_one.shape
    outs = run(
        kernel,
        "norm_one_back",
        (seqs,),
        [tokens, tokens, tokens, tokens, fixed(vectors), fixed(weight)],
        [tokens, tokens]
        + [pl.BlockSpec((1, length, part), lambda b, p: (b, 0, 0))] * ranks
        + [pl.BlockSpec((8, width), lambda b, p: (0, 0))],
        [kind_of(shape, jnp.float32), kind_of(shape)]
        + [kind_of((seqs, length, part))] * ranks
        + [kind_of((8, width), jnp.float32)],
        [dfirst.reshape(shape), dfirst_other.reshape(shape), dsum_two, sums_one, vectors, weight],
        prefetch=(places,),
        waits=waits,
    )
    return outs[0], outs[1], list(outs[2 : 2 + ranks]), outs[-1]


def out_grad_pack(places, contexts, dbranch, small, owners, waits=()):
    seqs, length, width = dbranch.shape
    ranks = len(contexts)
    part = contexts[0].shape[2]
    rows = width // owners
    extra = small.shape[0]
    each = part // rows

    def kernel(place_ref, *refs):
        dbranch_ref, small_ref, out_ref = refs[ranks:]
        grad = dbranch_ref[...].reshape(seqs * length, width)
        for q in range(ranks):
            product = dot(refs[q][...].reshape(seqs * length, part), grad, 0, 0).astype(jnp.bfloat16)
            for e in range(each):
                out_ref[place_ref[q] * each + e, :rows, :] = product[e * rows : (e + 1) * rows, :]
        for f in range(owners):
            out_ref[f, rows:, :] = jnp.zeros((extra, width), jnp.bfloat16)
            out_ref[f, rows:, :rows] = small_ref[:, f * rows : (f + 1) * rows]

    shape = (owners, rows + extra, width)
    return run(
        kernel,
        "out_grad_pack",
        (1,),
        [fixed(c) for c in contexts] + [fixed(dbranch), fixed(small)],
        pl.BlockSpec(shape, lambda i, p: (0, 0, 0)),
        kind_of(shape),
        [*contexts, dbranch, small],
        prefetch=(places,),
        waits=waits,
    )


def hidden_grad(places, dqkv, weight, length, picks, addends, dtype, waits=()):
    seqs, _, out_width = dqkv.shape
    width = weight.shape[0]
    blocks = len(picks)
    spread = [(k, a) for k in range(blocks) for a in addends[k]]

    def kernel(place_ref, weight_ref, *refs):
        for k in range(blocks):
            total = dot(refs[k][0], weight_ref[...], 1, 1)
            for j, (of, _) in enumerate(spread):
                if of == k:
                    total = total + wide(refs[blocks + j][0])
            refs[-1][k, 0] = total.astype(dtype)

    return run(
        kernel,
        "hidden_grad",
        (seqs,),
        [fixed(weight)]
        + [pl.BlockSpec((1, length, out_width), lambda b, p, q=q: (b, p[q], 0)) for q in picks]
        + [a.spec((1, length, width), lambda b, p: (b, 0, 0)) for _, a in spread],
        pl.BlockSpec((blocks, 1, length, width), lambda b, p: (0, b, 0, 0)),
        kind_of((blocks, seqs, length, width), dtype),
        [weight] + [dqkv] * blocks + [a.array for _, a in spread],
        prefetch=(places,),
        waits=waits,
        cost=10,
    )


def project_grad_pack(places, blocks, dqkv, owners, extra, waits=()):
    seqs, length, width = blocks[0].shape
    ranks = len(blocks)
    out_width = dqkv.shape[2]
    rows = width // owners
    group = max(1, TILE // rows)

    def kernel(place_ref, *refs):
        dqkv_ref, out_ref, total_ref = refs[ranks:]

        @pl.when(pl.program_id(0) == 0)
        def _():
            total_ref[...] = jnp.zeros_like(total_ref)
            total_ref[0:1, :] = column_sum(wide(dqkv_ref[...].reshape(-1, out_width)))

        total = 0.0
        for q in range(ranks):
            at = pl.ds(pl.multiple_of(place_ref[q] * length, length), length)
            for b in range(seqs):
                total = total + dot(refs[q][b], dqkv_ref[b, at, :], 0, 0)
        total = total.astype(jnp.bfloat16)
        sums = total_ref[...].astype(jnp.bfloat16)
        for e in range(group):
            out_ref[e, :rows, :] = total[e * rows : (e + 1) * rows, :]
            out_ref[e, rows:, :] = sums

    return run(
        kernel,
        "project_grad_pack",
        (owners // group,),
        [x.spec((seqs, length, group * rows), lambda i, p: (0, 0, i)) for x in blocks] + [fixed(dqkv)],
        pl.BlockSpec((group, rows + extra, out_width), lambda i, p: (i, 0, 0)),
        kind_of((owners, rows + extra, out_width)),
        [*arrays(blocks), dqkv],
        prefetch=(places,),
        scratch=(pltpu.VMEM((extra, out_width), jnp.float32),),
        waits=waits,
        cost=10,
    )


def lay_columns(places, blocks, rows):
    total, out_width = blocks[0].shape
    part = out_width // 3
    ranks = len(blocks)
    width = part * ranks

    def kernel(place_ref, *refs):
        for q in range(ranks):
            at = pl.ds(pl.multiple_of(place_ref[q] * part, part), part)
            for k in range(3):
                block = wide(refs[q][:, k * part : (k + 1) * part])
                refs[ranks + k][:, at] = block[:rows, :]
                refs[ranks + 3 + k][:, at] = block[rows : rows + 8, :]

    shape, below = (rows, width), (8, width)
    return run(
        kernel,
        "lay_columns",
        (1,),
        [b.whole() for b in blocks],
        [pl.BlockSpec(shape, lambda i, p: (0, 0))] * 3 + [pl.BlockSpec(below, lambda i, p: (0, 0))] * 3,
        [kind_of(shape, jnp.float32)] * 3 + [kind_of(below, jnp.float32)] * 3,
        arrays(blocks),
        prefetch=(places,),
        cost=10,
    )


def lay_up(places, blocks, chips, part):
    _, rows, _ = blocks[0].shape
    ranks = len(blocks)
    shape = (rows, 2 * chips * ranks * part)

    def kernel(place_ref, *refs):
        for q in range(ranks):
            for c in range(2):
                for z in range(chips):
                    at = pl.multiple_of(((z * 2 + c) * ranks + place_ref[q]) * part, part)
                    refs[ranks][:, pl.ds(at, part)] = wide(refs[q][c, :, z * part : (z + 1) * part])

    return run(
        kernel,
        "lay_up",
        (1,),
        [b.whole() for b in blocks],
        pl.BlockSpec(shape, lambda i, p: (0, 0)),
        kind_of(shape, jnp.float32),
        arrays(blocks),
        prefetch=(places,),
        cost=10,
    )


def lay_rows(places, blocks, waits=()):
    part, width = blocks[0].shape
    ranks = len(blocks)
    shape = (part * ranks, width)

    def kernel(place_ref, *refs):
        for q in range(ranks):
            refs[ranks][pl.ds(pl.multiple_of(place_ref[q] * part, part), part), :] = wide(refs[q][...])

    return run(
        kernel,
        "lay_rows",
        (1,),
        [b.whole() for b in blocks],
        pl.BlockSpec(shape, lambda i, p: (0, 0)),
        kind_of(shape, jnp.float32),
        arrays(blocks),
        prefetch=(places,),
        waits=waits,
        cost=10,
    )


def lay_chips(at, blocks, waits):
    rows, width = blocks[0].shape
    chips = len(blocks)

    def kernel(at_ref, *refs):
        for d in range(chips):
            refs[chips][at_ref[d]] = refs[d][...]

    shape = (chips, rows, width)
    return run(
        kernel,
        "lay_chips",
        (1,),
        [fixed(b) for b in blocks],
        pl.BlockSpec(shape, lambda i, p: (0, 0, 0)),
        kind_of(shape),
        blocks,
        prefetch=(at,),
        cost=100,
        waits=waits,
    )


def hold(array, waits):
    def kernel(from_ref, to_ref):
        to_ref[...] = from_ref[...]

    rank = array.ndim
    return run(
        kernel,
        "hold",
        (1,),
        [fixed(array)],
        pl.BlockSpec(array.shape, lambda i: (0,) * rank),
        kind_of(array.shape, array.dtype),
        [array],
        waits=waits,
    )


def split(at, own, size, waits=()):
    _, width = own.shape
    chips = at.shape[0]

    def kernel(at_ref, own_ref, *outs):
        for d in range(chips):
            outs[d][...] = own_ref[pl.ds(pl.multiple_of(at_ref[d] * size, size), size), :]

    return run(
        kernel,
        "split",
        (1,),
        [fixed(own)],
        [pl.BlockSpec((size, width), lambda i, p: (0, 0))] * chips,
        [kind_of((size, width))] * chips,
        [own],
        prefetch=(at,),
        waits=waits,
    )


def tick(*waits, cost=10):
    def kernel(out_ref):
        out_ref[...] = jnp.zeros_like(out_ref)

    return run(
        kernel, "tick", (1,), [], pl.BlockSpec((8, 128), lambda i: (0, 0)), kind_of((8, 128), jnp.float32), [], waits=waits, cost=cost
    )


def total_rows(pieces, waits=()):
    def kernel(*refs):
        total = wide(refs[0][...])
        for ref in refs[1:-1]:
            total = total + wide(ref[...])
        refs[-1][...] = total.astype(jnp.bfloat16)

    shape = pieces[0].shape
    return run(
        kernel,
        "total_rows",
        (1,),
        [fixed(p) for p in pieces],
        pl.BlockSpec(shape, lambda i: (0, 0)),
        kind_of(shape),
        pieces,
        waits=waits,
    )


def total_halves(core, pieces, waits=()):
    rows, width = pieces[0].shape
    half = rows // 2

    def kernel(core_ref, *refs):
        for out_ref, of in ((refs[-2], core_ref[0]), (refs[-1], 1 - core_ref[0])):
            at = pl.ds(pl.multiple_of(of * half, half), half)
            total = wide(refs[0][at, :])
            for ref in refs[1:-2]:
                total = total + wide(ref[at, :])
            out_ref[...] = total.astype(jnp.bfloat16)

    return run(
        kernel,
        "total_halves",
        (1,),
        [fixed(p) for p in pieces],
        [pl.BlockSpec((half, width), lambda i, p: (0, 0))] * 2,
        [kind_of((half, width))] * 2,
        pieces,
        prefetch=(core,),
        waits=waits,
    )


def pair(core, own, other, waits=()):
    rows, width = own.shape

    def kernel(core_ref, own_ref, other_ref, out_ref):
        out_ref[core_ref[0]] = own_ref[...]
        out_ref[1 - core_ref[0]] = other_ref[...]

    shape = (2, rows, width)
    return run(
        kernel,
        "pair",
        (1,),
        [fixed(own), fixed(other)],
        pl.BlockSpec(shape, lambda i, p: (0, 0, 0)),
        kind_of(shape),
        [own, other],
        prefetch=(core,),
        waits=waits,
    )


def plan_rows(segments):
    b, t = segments.shape
    n = t // SPAN
    win = min(3 * SPAN, t)
    spans = segments.reshape(b, n, SPAN)
    place = jnp.arange(t, dtype=jnp.int32)
    low = jnp.min(jnp.where(segments[:, None, :] == spans[:, :, :1], place, t), axis=2)
    high = jnp.max(jnp.where(segments[:, None, :] == spans[:, :, -1:], place, -1), axis=2)
    start = jnp.minimum(low // SPAN * SPAN, t - win)
    fits = jnp.all(high < start + win, axis=1)
    single = jnp.all(segments == segments[:, :1], axis=1)
    kind = jnp.where(single, 0, jnp.where(fits, 1, 2))
    return kind.astype(jnp.int32), start.astype(jnp.int32)

def fwd_kernel(heads, kind_ref, start_ref, place_ref, qkv_ref, row_ref, col_ref, ctx_ref, lse_ref, *part_refs):
    b = pl.program_id(0)
    t = qkv_ref.shape[1]
    hw = heads * HEAD_DIM
    win = min(3 * SPAN, t)
    kind = kind_ref[b]

    def piece(h, which, rows):
        lo = which * hw + h * HEAD_DIM
        return qkv_ref[0, rows, lo:lo + HEAD_DIM]

    def attend(h, rows, count, keys, masked):
        q = piece(h, 0, rows)
        s = dot(q, piece(h, 1, keys), 1, 1)
        if masked:
            s = jnp.where(col_ref[0, rows, :] == row_ref[0, :, keys], s, MASKED)
        m = jnp.max(s, axis=1, keepdims=True)
        e = jnp.exp(s - m)
        total = jnp.sum(e, axis=1, keepdims=True)
        c = dot(e.astype(jnp.bfloat16), piece(h, 2, keys), 1, 0) / total
        ctx_ref[0, rows, h * HEAD_DIM:(h + 1) * HEAD_DIM] = c.astype(jnp.bfloat16)
        lse = jnp.broadcast_to(m + jnp.log(total), (count, 128))
        lse_ref[0, h:h + 1, rows] = jnp.transpose(lse)[0:1, :]

    def dense(masked):
        tile = min(256, t)
        def body(i, _):
            rows = pl.ds(pl.multiple_of(i * tile, tile), tile)
            for h in range(heads):
                attend(h, rows, tile, pl.ds(0, t), masked)
            return 0
        lax.fori_loop(0, t // tile, body, 0)

    @pl.when(kind == 0)
    def _():
        dense(False)

    @pl.when(kind == 2)
    def _():
        dense(True)

    @pl.when(kind == 1)
    def _():
        def body(i, _):
            rows = pl.ds(pl.multiple_of(i * SPAN, SPAN), SPAN)
            keys = pl.ds(pl.multiple_of(start_ref[b, i], SPAN), win)
            for h in range(heads):
                attend(h, rows, SPAN, keys, True)
            return 0
        lax.fori_loop(0, t // SPAN, body, 0)

    length = part_refs[0].shape[1]
    for q, part_ref in enumerate(part_refs):
        part_ref[0] = ctx_ref[0, pl.ds(pl.multiple_of(place_ref[q] * length, length), length), :]


def attention(qkv, segments, kind, start, places, waits):
    ranks = places.shape[0]
    b, t, w = qkv.shape
    hw = w // 3
    heads = hw // HEAD_DIM

    def at(i, *_):
        return (i, 0, 0)

    return run(
        functools.partial(fwd_kernel, heads),
        "attention_forward",
        (b,),
        [pl.BlockSpec((1, t, w), at), pl.BlockSpec((1, 1, t), at), pl.BlockSpec((1, t, 1), at)],
        [pl.BlockSpec((1, t, hw), at), pl.BlockSpec((1, heads, t), at)]
        + [pl.BlockSpec((1, t // ranks, hw), at)] * ranks,
        [kind_of((b, t, hw)), kind_of((b, heads, t), jnp.float32)] + [kind_of((b, t // ranks, hw))] * ranks,
        [qkv, segments[:, None, :], segments[:, :, None]],
        prefetch=(kind, start, places),
        waits=waits,
        cost=100,
    )

def bwd_kernel(heads, b, kind_ref, start_ref, qkv_ref, do_ref, ctx_ref, lse_ref, row_ref, col_ref, out_ref, dq_acc, delta_ref):
    t = qkv_ref.shape[1]
    hw = heads * HEAD_DIM
    win = min(3 * SPAN, t)
    kind = kind_ref[b]

    def lanes(h, which=0):
        lo = which * hw + h * HEAD_DIM
        return slice(lo, lo + HEAD_DIM)

    for h in range(heads):
        prod = do_ref[0, :, lanes(h)].astype(jnp.float32) * ctx_ref[0, :, lanes(h)].astype(jnp.float32)
        d = jnp.sum(prod, axis=1, keepdims=True)
        delta_ref[h:h + 1, :] = jnp.transpose(jnp.broadcast_to(d, (t, 128)))[0:1, :]

    def back(h, keys, queries, masked):
        k = qkv_ref[0, keys, lanes(h, 1)]
        v = qkv_ref[0, keys, lanes(h, 2)]
        q = qkv_ref[0, queries, lanes(h, 0)]
        do = do_ref[0, queries, lanes(h)]
        s = dot(k, q, 1, 1)
        if masked:
            s = jnp.where(col_ref[0, keys, :] == row_ref[0, :, queries], s, MASKED)
        p = jnp.exp(s - lse_ref[0, h:h + 1, queries])
        dp = dot(v, do, 1, 1)
        ds = (p * (dp - delta_ref[h:h + 1, queries])).astype(jnp.bfloat16)
        dv = dot(p.astype(jnp.bfloat16), do, 1, 0)
        dk = dot(ds, q, 1, 0)
        out_ref[0, keys, lanes(h, 1)] = dk.astype(jnp.bfloat16)
        out_ref[0, keys, lanes(h, 2)] = dv.astype(jnp.bfloat16)
        return dot(k, ds, 0, 0)

    dq_acc[...] = jnp.zeros_like(dq_acc)

    def dense(masked):
        tile = min(256, t)
        def body(j, _):
            keys = pl.ds(pl.multiple_of(j * tile, tile), tile)
            for h in range(heads):
                dq_acc[h] += back(h, keys, pl.ds(0, t), masked)
            return 0
        lax.fori_loop(0, t // tile, body, 0)

    @pl.when(kind == 0)
    def _():
        dense(False)

    @pl.when(kind == 2)
    def _():
        dense(True)

    @pl.when(kind == 1)
    def _():
        def body(j, _):
            keys = pl.ds(pl.multiple_of(j * SPAN, SPAN), SPAN)
            queries = pl.ds(pl.multiple_of(start_ref[b, j], SPAN), win)
            for h in range(heads):
                dq_acc[h, :, queries] += back(h, keys, queries, True)
            return 0
        lax.fori_loop(0, t // SPAN, body, 0)

    for h in range(heads):
        dq = jnp.transpose(dq_acc[h]) * (HEAD_DIM ** -0.5)
        out_ref[0, :, lanes(h, 0)] = dq.astype(jnp.bfloat16)

def attention_back(qkv, dparts, ctx, lse, segments, kind, start, places, which, buffer, waits):
    b, t, w = qkv.shape
    hw = w // 3
    heads = hw // HEAD_DIM
    ranks = len(dparts)
    length = t // ranks

    def kernel(kind_ref, start_ref, place_ref, qkv_ref, *refs):
        grad_ref = refs[-1]
        for q in range(ranks):
            grad_ref[0, pl.ds(pl.multiple_of(place_ref[q] * length, length), length), :] = refs[q][0]
        bwd_kernel(heads, which, kind_ref, start_ref, qkv_ref, grad_ref, *refs[ranks : ranks + 4], *refs[-4:-1])

    def at(i, *_):
        return (which, 0, 0)

    ins = [pl.BlockSpec((1, t, w), at)] + [pl.BlockSpec((1, length, hw), at)] * ranks
    ins += [
        pl.BlockSpec((1, t, hw), at),
        pl.BlockSpec((1, heads, t), at),
        pl.BlockSpec((1, 1, t), at),
        pl.BlockSpec((1, t, 1), at),
    ]
    operands = [qkv, *dparts, ctx, lse, segments[:, None, :], segments[:, :, None]]
    alias = None
    if buffer is not None:
        ins.append(pl.BlockSpec(memory_space=pl.ANY))
        operands.append(buffer)
        alias = {3 + len(ins) - 1: 0}
    return run(
        kernel,
        "attention_backward",
        (1,),
        ins,
        pl.BlockSpec((1, t, w), at),
        kind_of((b, t, w)),
        operands,
        prefetch=(kind, start, places),
        scratch=(
            pltpu.VMEM((heads, HEAD_DIM, t), jnp.float32),
            pltpu.VMEM((heads, t), jnp.float32),
            pltpu.VMEM((1, t, hw), jnp.bfloat16),
        ),
        alias=alias,
        waits=waits,
    )


AXES = ("seq", "z", "core")
ROWS = ("z", "core")
EXTRA = 16


def low(tensor):
    return tensor.astype(jnp.bfloat16)


class Ring:
    def __init__(self):
        self.ranks = lax.axis_size("seq")
        self.chips = lax.axis_size("z")
        self.index = lax.axis_index("seq")
        self.core = lax.axis_index("core")
        self.count = self.ranks.bit_length() - 1

    def bit(self, k, core):
        if self.count == 2 and core == 1:
            k = 1 - k
        return 1 << k

    def offset(self, q, core):
        return sum(self.bit(k, core) for k in range(self.count) if q >> k & 1)

    def place(self, q):
        return jnp.bitwise_xor(self.index, jnp.where(self.core == 0, self.offset(q, 0), self.offset(q, 1)))

    def hop(self, block, k):
        pairs = []
        for s in range(self.ranks):
            for z in range(self.chips):
                for c in range(2):
                    to = s ^ self.bit(k, c)
                    pairs.append(((s * self.chips + z) * 2 + c, (to * self.chips + z) * 2 + c))
        return lax.ppermute(block, AXES, pairs)

    def gather(self, block):
        blocks = [block]
        for k in range(self.count):
            blocks = blocks + [self.hop(b, k) for b in blocks]
        return [View(b) for b in blocks]

    def total(self, block):
        for k in range(self.count):
            block = wide(block) + wide(self.hop(low(block), k))
        return block


    def exchange(self, blocks):
        out = [blocks[0]]
        for q in range(1, self.ranks):
            pairs = []
            for s in range(self.ranks):
                for z in range(self.chips):
                    for c in range(2):
                        to = s ^ self.offset(q, c)
                        pairs.append(((s * self.chips + z) * 2 + c, (to * self.chips + z) * 2 + c))
            out.append(lax.ppermute(blocks[q], AXES, pairs))
        return out

    def shift(self, block, d):
        return lax.ppermute(block, "z", [(z, (z + d) % self.chips) for z in range(self.chips)])


def swap(block):
    return lax.ppermute(block, "core", [(0, 1), (1, 0)])


def put(blocks, ring, axis):
    shape = list(blocks[0].shape)
    size = shape[axis]
    shape[axis] = size * len(blocks)
    whole = jnp.zeros(shape, blocks[0].dtype)
    for q, block in enumerate(blocks):
        whole = lax.dynamic_update_slice_in_dim(whole, block, ring.place(q) * size, axis)
    return whole


def local(
    hidden_in,
    segments,
    q_weight,
    k_weight,
    v_weight,
    out_weight,
    q_bias,
    v_bias,
    out_bias,
    up_weight,
    up_bias,
    down_weight,
    down_bias,
    norm1_gain,
    norm1_bias,
    norm2_gain,
    norm2_bias,
    out_grad,
):
    ring = Ring()
    here, core = ring.index, ring.core
    ranks, chips = ring.ranks, ring.chips
    owners = chips * 2
    z_index = lax.axis_index("z")
    owner = z_index * 2 + core
    seqs, length, width = hidden_in.shape
    full = length * ranks
    head_width = width // ranks
    out_width = 3 * head_width
    rows = width // owners
    units = down_weight.shape[0]
    part = units // ranks
    count = seqs * length
    score_scale = HEAD_DIM ** (-0.5)
    first_core = core == 0
    core_index = core.astype(jnp.int32).reshape(1)
    places = jnp.stack([ring.place(q) for q in range(ranks)]).astype(jnp.int32)
    blocks = range(ranks)

    heads_at = here * head_width
    mine = jnp.concatenate(
        [lax.dynamic_slice_in_dim(w, heads_at, head_width, 1) for w in (q_weight, k_weight, v_weight)], axis=1
    )
    vectors = (q_bias, v_bias, out_bias, down_bias, norm1_gain, norm1_bias, norm2_gain, norm2_bias)
    known = len(vectors)
    packed = jnp.pad(
        up_bias.reshape(-1, rows), ((known, EXTRA - known - units // rows), (0, out_width - rows))
    )
    for i, vector in enumerate(vectors):
        packed = packed + jnp.pad(vector[None], ((i, EXTRA - 1 - i), (0, out_width - rows)))
    mine = jnp.concatenate([mine, packed], axis=0)
    gathered = lax.all_gather(mine, ROWS, axis=0)

    def up_columns(of_core):
        return jnp.concatenate(
            [
                lax.dynamic_slice_in_dim(up_weight, ((z * 2 + of_core) * ranks + here) * part, part, 1)
                for z in range(chips)
            ],
            axis=1,
        )

    own_up, other_up = up_columns(core), swap(up_columns(1 - core))
    up_rows = jnp.concatenate(
        [jnp.where(first_core, own_up, other_up), jnp.where(first_core, other_up, own_up)], axis=0
    )
    hidden = ring.gather(hidden_in)
    shifts = jnp.stack([(z_index - d) % chips for d in range(chips)]).astype(jnp.int32)
    up_block = lay_chips(shifts, [up_rows] + [ring.shift(up_rows, d) for d in range(1, chips)], ())
    up_block = hold(up_block.reshape(width, chips * part), (hidden[-1].array,))
    down_rows = hold(lax.dynamic_slice_in_dim(down_weight, here * part, part, 0), (gathered,))
    down_block = lax.all_gather(down_rows, "z", axis=0, tiled=True)
    output_weight = lax.all_gather(hold(out_weight, (down_rows,)), ROWS, axis=0, tiled=True)
    up_weights = ring.gather(up_block)
    kind, start = plan_rows(segments)
    keep = wide(lax.dynamic_slice_in_dim(segments, here * length, length, 1) != 0)[:, :, None]

    qkv_weight = gathered[:, :rows].reshape(width, out_width)
    gathered = wide(gathered[:, rows:, :rows])
    vectors = gathered.transpose(1, 0, 2).reshape(EXTRA, width)
    biases = lax.dynamic_slice_in_dim(vectors, heads_at, head_width, 1)
    qkv_bias = jnp.concatenate([biases[0], jnp.zeros_like(biases[0]), biases[1]])[None]
    scales = jnp.where(jnp.arange(out_width) < head_width, score_scale, 1.0)[None]
    qkv = project(places, hidden, qkv_weight, qkv_bias, scales)
    contexts, log_totals, *context_parts = attention(
        qkv, segments, kind, start, places, (*arrays(up_weights[1:3]), down_block)
    )
    context_parts = ring.exchange(context_parts)
    down_weights = ring.gather(down_block)
    sums_one, first_low = out_norm(
        places,
        context_parts,
        output_weight,
        hidden_in,
        vectors,
        arrays(down_weights[1:2]),
    )

    first_low = first_low.reshape(count, width)
    first_other = swap(first_low)
    upper_bias = gathered[:, known : known + units // rows].reshape(chips, 2, ranks, part)
    upper_bias = lax.dynamic_index_in_dim(upper_bias, core, 1, False)
    upper_bias = [
        lax.dynamic_index_in_dim(upper_bias, ring.place(q), 1, False).reshape(1, -1) for q in blocks
    ]
    actives, slopes = up_forward(first_low, first_other, up_weights, upper_bias)
    mixed_other = down_forward(actives, down_weights, count, count, jnp.bfloat16)
    mixed = down_forward(actives, down_weights, 0, count, jnp.float32, (mixed_other,))
    layer_out, dsum_two, dmixed, totals_two = norm_two(mixed, swap(mixed_other), sums_one, vectors, out_grad, keep)

    dmixed = dmixed.reshape(count, width)
    dmixed_other = swap(dmixed)
    none = [()] * ranks
    odd, even = [q for q in blocks if q % 2], [q for q in blocks if q % 2 == 0]
    down_sent = down_grad([actives[q] for q in odd], dmixed, dmixed_other, none)
    duppers, up_sums, dfirst, dfirst_other = ffn_back(
        dmixed, dmixed_other, slopes, down_weights, up_weights, (tick(down_sent),)
    )
    dfirst_other = swap(dfirst_other)
    dsum_one, dbranch, dcontexts, totals_one = norm_one_back(
        places, dfirst, dfirst_other, dsum_two, sums_one, vectors, output_weight, head_width, (tick(duppers[0], cost=10),)
    )
    dcontexts = ring.exchange(dcontexts)

    def spread(made, sent):
        came = {q: [] for q in blocks}
        for k in range(ring.count):
            step = 1 << k
            got = ring.hop(sent, k)
            for i, q in enumerate(range(0, ranks, 2 * step)):
                came[q].append(View(got, i))
            if k + 1 < ring.count:
                turn = [q + 2 * step for q in range(0, ranks, 4 * step)]
                sent = made(turn, [came[q] for q in turn])
        return came[0], sent

    def down_made(turn, addends):
        return down_grad([actives[q] for q in turn], dmixed, dmixed_other, addends, (tick(dbranch),))

    down_came, down_hop = spread(down_made, down_sent)
    up_sent = up_grad([duppers[q] for q in odd], first_low, first_other, none, (down_hop,))

    extra = -(-(6 + ranks) // EXTRA) * EXTRA
    up_totals = put([up_sums[q : q + 1] for q in blocks], ring, 0).reshape(ranks, chips, 1, part)
    up_totals = jnp.where(jnp.arange(2)[None, None, :, None] == core, up_totals, 0.0)
    up_totals = jnp.pad(up_totals, ((0, 0), (0, 0), (0, 0), (0, rows - part))).reshape(ranks, width)
    small = jnp.concatenate(
        [totals_two[:3], totals_one[:3], up_totals, jnp.zeros((extra - 6 - ranks, width), jnp.float32)], axis=0
    )
    out_pack = out_grad_pack(places, context_parts, dbranch, low(small), owners, (up_sent,))
    out_shard = lax.psum_scatter(out_pack.reshape(-1, width), ROWS, scatter_dimension=0, tiled=True)

    common = (qkv, dcontexts, contexts, log_totals, segments, kind, start, places)
    dqkv = attention_back(*common, 0, None, (out_pack,))

    def up_made(turn, addends):
        return up_grad([duppers[q] for q in turn], first_low, first_other, addends, (dqkv,))

    up_came, up_hop = spread(up_made, up_sent)
    down_own = down_grad([actives[0]], dmixed, dmixed_other, [down_came], (up_hop,))[0]
    ahead = jnp.stack([(z_index + d) % chips for d in range(chips)]).astype(jnp.int32)
    down_pieces = split(ahead, down_own, part)
    for which in range(1, seqs):
        dqkv = attention_back(*common, which, dqkv, (down_pieces[0], up_hop))

    def shifted(pieces):
        return [pieces[0]] + [ring.shift(pieces[d], d) for d in range(1, chips)]

    down_shard = total_rows(shifted(down_pieces), (dqkv, out_shard))
    down_parts = ring.gather(down_shard)

    def hidden_made(turn, addends, waits=()):
        return hidden_grad(places, dqkv, qkv_weight, length, turn, addends, jnp.bfloat16, waits or (qkv_pack,))

    up_own = up_grad([duppers[0]], first_low, first_other, [up_came], (dqkv,))[0]
    up_pieces = split(ahead, up_own, 2 * rows)
    hidden_sent = hidden_made(odd, none, (up_pieces[0], down_shard))
    qkv_pack = project_grad_pack(places, hidden, dqkv, owners, EXTRA, (hidden_sent, *arrays(down_parts)))
    qkv_shard = lax.psum_scatter(qkv_pack.reshape(-1, out_width), ROWS, scatter_dimension=0, tiled=True)

    hidden_came, hidden_hop = spread(hidden_made, hidden_sent)
    keep_part, take_part = total_halves(core_index, shifted(up_pieces), (qkv_pack,))
    down_weight_grad = lay_rows(places, down_parts, (keep_part,))
    up_pair = pair(core_index, keep_part, swap(take_part), (down_weight_grad,))
    input_grad = hidden_grad(
        places, dqkv, qkv_weight, length, [0], [[View(dsum_one)] + hidden_came], jnp.float32
    )[0]

    up_parts = ring.gather(up_pair)
    qkv_parts = ring.gather(qkv_shard)
    out_pack = ring.total(out_shard)
    if part % 128 == 0:
        up_weight_grad = lay_up(places, up_parts, chips, part)
    else:
        up_weight_grad = wide(put([b.value()[None] for b in up_parts], ring, 0))
        up_weight_grad = (
            up_weight_grad.reshape(ranks, 2, rows, chips, part).transpose(2, 3, 1, 0, 4).reshape(rows, owners * units)
        )
    if head_width % 128 == 0:
        *qkv_grads, q_sums, _, v_sums = lay_columns(places, qkv_parts, rows)
    else:
        laid = wide(put([b.value()[None] for b in qkv_parts], ring, 0))
        laid = laid.reshape(ranks, rows + EXTRA, 3, head_width).transpose(2, 1, 0, 3).reshape(3, -1, width)
        qkv_grads, q_sums, v_sums = [g[:rows] for g in laid], laid[0, rows:], laid[2, rows:]

    def mine_of(sums):
        return lax.dynamic_slice_in_dim(sums[0], owner * rows, rows, 0)

    small = out_pack[rows:, :rows]
    up_bias_grad = small[6 : 6 + ranks, :part].reshape(-1)
    return (
        layer_out,
        input_grad,
        *qkv_grads,
        out_pack[:rows],
        mine_of(q_sums),
        mine_of(v_sums),
        small[3],
        up_weight_grad,
        up_bias_grad,
        down_weight_grad,
        small[0],
        small[4],
        small[5],
        small[1],
        small[2],
    )


def solution(mesh):
    ranks, owners = mesh.shape["seq"], mesh.shape["fsdp"]
    grid = Mesh(mesh.devices.reshape(ranks, owners // 2, 2), AXES)
    tokens, matrix, vector = P(ROWS, "seq", None), P(ROWS, None), P(ROWS)
    return jax.shard_map(
        local,
        mesh=grid,
        in_specs=(
            tokens,
            matrix,
            matrix,
            matrix,
            matrix,
            matrix,
            vector,
            vector,
            vector,
            matrix,
            vector,
            matrix,
            vector,
            vector,
            vector,
            vector,
            vector,
            tokens,
        ),
        out_specs=(
            tokens,
            tokens,
            matrix,
            matrix,
            matrix,
            matrix,
            vector,
            vector,
            vector,
            matrix,
            vector,
            matrix,
            vector,
            vector,
            vector,
            vector,
            vector,
        ),
        check_vma=False,
    )
```

profile of v0, /device:TPU:0, one launch (start us, length us, event | category | flops | bytes accessed | tf_op | source)
XLA Modules:
  0.0 416.6 jit_solution(18179249984558410751)
XLA Ops:
  18.1 3.7 collective-permute-start.6
  23.2 10.6 %collective-permute-done.refs_5_.refs_2_ = bf16[2,256,1024]{2,1,0:T(8,128)(2,1)} collective-permute-done((bf16[2,256,1024]{2,1,0:T(8,128)(2,1)}, bf16[2,256,1024]{2,1,0:T(8,128)(2,1)}, u32[]{:S(2)}, u32[]{:S(2)}) %collective-permute-start) | collective-permute-done | bytes 1048608 | tf_op jit(solution)/shard_map/ppermute | solution.py:993
  35.5 23.4 %collective-permute-done.5.refs_3_ = bf16[256,512]{1,0:T(8,128)(2,1)S(1)} collective-permute-done((bf16[256,512]{1,0:T(8,128)(2,1)S(1)}, bf16[256,512]{1,0:T(8,128)(2,1)S(1)}, u32[]{:S(2)}, u32[]{:S(2)}) %collective-permute-start.5) | collective-permute-done | bytes 262176 | tf_op jit(solution)/shard_map/ppermute | solution.py:1020
  70.8 7.6 %project.1.refs_3_ = bf16[2,1024,768]{2,1,0:T(8,128)(2,1)S(1)} custom-call(s32[4]{0:T(128)S(1)} %pad_add_fusion.1.refs_0_.refs_2_, bf16[1024,768]{1,0:T(8,128)(2,1)S(1)} %bitcast.87, f32[1,768]{1,0:T(1,128)S(1)} %broadcast_in_dim.133.refs_2_, f32[1,768]{1,0:T(1,128)S(1)} %compare_select_fusion.refs_3_, bf16[2,256,1024]{2,1,0:T(8,128)(2,1)S(1)} %copy-done.7, ...), custom_call_target="tpu_custom_call" | custom-call | flops 10000000000 | bytes 1000 | tf_op jit(solution)/shard_map/project/pallas_call | solution.py:31
  80.2 9.1 %all-gather.5.cloned.1.call-done.refs_8_.refs_4_.refs_6_ = bf16[512,1024]{1,0:T(8,128)(2,1)} async-done(((bf16[128,1024]{1,0:T(8,128)(2,1)}), bf16[512,1024]{1,0:T(8,128)(2,1)}) %all-gather.5.cloned.1.call-update) | async-done | bytes 1048592 | tf_op jit(solution)/shard_map/all_gather | solution.py:1109
  94.3 22.0 %attention_forward.1 = (bf16[2,1024,256]{2,1,0:T(8,128)(2,1)S(1)}, f32[2,4,1024]{2,1,0:T(4,128)S(1)}, bf16[2,256,256]{2,1,0:T(8,128)(2,1)S(1)}, bf16[2,256,256]{...) custom-call(s32[2]{0:T(128)S(1)} %select_select_fusion.refs_0_, ...), custom_call_target="tpu_custom_call" | custom-call | flops 99999997952 | bytes 1000 | tf_op jit(solution)/shard_map/attention_forward/pallas_call | solution.py:31
  123.1 4.6 %collective-permute-done.9.refs_2_ = bf16[2,256,256]{2,1,0:T(8,128)(2,1)S(1)} collective-permute-done((bf16[2,256,256]{2,1,0:T(8,128)(2,1)S(1)}, bf16[2,256,256]{2,1,0:T(8,128)(2,1)S(1)}, u32[]{:S(2)}, u32[]{:S(2)}) %collective-permute-start.9) | collective-permute-done | bytes 262176 | tf_op jit(solution)/shard_map/ppermute | solution.py:1016
  127.7 6.2 %collective-permute-done.11.refs_4_ = bf16[2,256,256]{2,1,0:T(8,128)(2,1)S(1)} collective-permute-done((bf16[2,256,256]{2,1,0:T(8,128)(2,1)S(1)}, bf16[2,256,256]{2,1,0:T(8,128)(2,1)S(1)}, u32[]{:S(2)}, u32[]{:S(2)}) %collective-permute-start.11) | collective-permute-done | bytes 262176 | tf_op jit(solution)/shard_map/ppermute | solution.py:1016
  139.9 3.4 out_norm.1
  148.3 10.0 %up_forward.1 = (bf16[1024,512]{1,0:T(8,128)(2,1)S(1)}, bf16[1024,512]{1,0:T(8,128)(2,1)S(1)}, bf16[1024,512]{1,0:T(8,128)(2,1)S(1)}, bf16[1024,512]{1,0:T(8,128...) custom-call(bf16[512,1024]{1,0:T(8,128)(2,1)} %bitcast.26.refs_0_, ...), custom_call_target="tpu_custom_call" | custom-call | flops 10000000000 | bytes 1000 | tf_op jit(solution)/shard_map/up_forward/pallas_call | solution.py:31
  161.1 11.2 %collective-permute-done.16.refs_7_.refs_9_ = bf16[512,1024]{1,0:T(8,128)(2,1)S(1)} collective-permute-done((bf16[512,1024]{1,0:T(8,128)(2,1)}, bf16[512,1024]{1,0:T(8,128)(2,1)S(1)}, u32[]{:S(2)}, u32[]{:S(2)}) %collective-permute-start.16) | collective-permute-done | bytes 1048608 | tf_op jit(solution)/shard_map/ppermute | solution.py:993
  172.3 3.8 down_forward.2.refs_8_
  189.5 4.8 %norm_two.1 = (bf16[2,256,1024]{2,1,0:T(8,128)(2,1)}, f32[2,256,1024]{2,1,0:T(8,128)S(1)}, bf16[2,256,1024]{2,1,0:T(8,128)(2,1)}, f32[8,1024]{1,0:T(8,128)S(1)}) custom-call(f32[2,256,1024]{2,1,0:T(8,128)S(1)} %bitcast.100, bf16[2,256,1024]{2,1,0:T(8,128)(2,1)} %bitcast.33.refs_1_, f32[2,256,1024]{2,1,0:T(8,128)S(1)} %copy-done.54, f32[16,1024]{1,0:T(8,128)S(1)} %bitcast.96, ...), custom_call_target="tpu_custom_call" | custom-call | flops 10000000000 | bytes 1000 | tf_op jit(solution)/shard_map/norm_two/pallas_call | solution.py:31
  201.2 5.2 %down_grad.3.refs_0_ = bf16[2,512,1024]{2,1,0:T(8,128)(2,1)} custom-call(bf16[512,1024]{1,0:T(8,128)(2,1)} %bitcast.35.refs_0_, bf16[512,1024]{1,0:T(8,128)(2,1)} %collective-permute-done.18.refs_1_, bf16[1024,512]{1,0:T(8,128)(2,1)S(1)} %copy-done.86, bf16[1024,512]{1,0:T(8,128)(2,1)S(1)} %copy-done.89), custom_call_target="tpu_custom_call" | custom-call | flops 10000000000 | bytes 1000 | tf_op jit(solution)/shard_map/down_grad/pallas_call | solution.py:31
  209.8 13.4 %feed_forward_back.1 = (bf16[1024,512]{1,0:T(8,128)(2,1)S(1)}, bf16[1024,512]{1,0:T(8,128)(2,1)S(1)}, bf16[1024,512]{1,0:T(8,128)(2,1)S(1)}, bf16[1024,512]{1,0:...) custom-call(bf16[512,1024]{1,0:T(8,128)(2,1)} %bitcast.35.refs_0_, ...), custom_call_target="tpu_custom_call" | custom-call | flops 10000000000 | bytes 1000 | tf_op jit(solution)/shard_map/feed_forward_back/pallas_call | solution.py:31
  234.8 4.5 %norm_one_back.1 = (f32[2,256,1024]{2,1,0:T(8,128)S(1)}, bf16[2,256,1024]{2,1,0:T(8,128)(2,1)S(1)}, bf16[2,256,256]{2,1,0:T(8,128)(2,1)S(1)}, bf16[2,256,256]{2,...) custom-call(s32[4]{0:T(128)S(1)} %pad_add_fusion.1.refs_0_.refs_2_, ...), custom_call_target="tpu_custom_call" | custom-call | flops 10000000000 | bytes 1000 | tf_op jit(solution)/shard_map/norm_one_back/pallas_call | solution.py:31
  244.1 4.0 down_grad.4.refs_4_
  248.1 5.4 %up_grad.3.refs_7_ = bf16[2,1024,512]{2,1,0:T(8,128)(2,1)} custom-call(bf16[512,1024]{1,0:T(8,128)(2,1)} %bitcast.26.refs_0_, bf16[512,1024]{1,0:T(8,128)(2,1)} %collective-permute-done.13.refs_1_, bf16[1024,512]{1,0:T(8,128)(2,1)S(1)} %copy-done.72, bf16[1024,512]{1,0:T(8,128)(2,1)S(1)} %copy-done.74, bf16[1,512,1024]{2,1,0:T(8,128)(2,1)} %down_grad.4.refs_4_), custom_call_target="tpu_custom_call" | custom-call | flops 10000000000 | bytes 1000 | tf_op jit(solution)/shard_map/up_grad/pallas_call | solution.py:31
  255.4 3.3 out_grad_pack.1.refs_12_
  262.8 16.0 %attention_backward.2.refs_4_.refs_12_ = bf16[2,1024,768]{2,1,0:T(8,128)(2,1)S(1)} custom-call(s32[2]{0:T(128)S(1)} %select_select_fusion.refs_0_, s32[2,8]{1,0:T(2,128)S(1)} %get-tuple-element.118.refs_1_, s32[4]{0:T(128)S(1)} %pad_add_fusion.1.refs_0_.refs_2_, bf16[2,1024,768]{2,1,0:T(8,128)(2,1)S(1)} %copy-done.44, bf16[2,256,256]{2,1,0:T(8,128)(2,1)S(1)} %copy-done.91, ...), custom_call_target="tpu_custom_call" | custom-call | flops 10000000000 | bytes 1000 | tf_op jit(solution)/shard_map/attention_backward/pallas_call | solution.py:31
  278.7 11.5 %collective-permute-done.25.refs_3_ = bf16[2,1024,512]{2,1,0:T(8,128)(2,1)} collective-permute-done((bf16[2,1024,512]{2,1,0:T(8,128)(2,1)}, bf16[2,1024,512]{2,1,0:T(8,128)(2,1)}, u32[]{:S(2)}, u32[]{:S(2)}) %collective-permute-start.25) | collective-permute-done | bytes 2097184 | tf_op jit(solution)/shard_map/ppermute | solution.py:993
  290.2 3.8 up_grad.4.refs_5_.refs_14_
  295.2 3.5 down_grad.5
  304.2 13.5 %attention_backward.3.refs_5_.refs_4_.refs_2_.refs_3_ = bf16[2,1024,768]{2,1,0:T(8,128)(2,1)S(1)} custom-call(s32[2]{0:T(128)S(1)} %select_select_fusion.refs_0_, s32[2,8]{1,0:T(2,128)S(1)} %get-tuple-element.118.refs_1_, s32[4]{0:T(128)S(1)} %pad_add_fusion.1.refs_0_.refs_2_, bf16[2,1024,768]{2,1,0:T(8,128)(2,1)S(1)} %copy-done.45, ...), custom_call_target="tpu_custom_call", output_to_operand_aliasing={{}: (12, {})} | custom-call | flops 10000000000 | bytes 1000 | tf_op jit(solution)/shard_map/attention_backward/pallas_call | solution.py:31
  317.8 4.7 %up_grad.5 = bf16[1,1024,512]{2,1,0:T(8,128)(2,1)S(1)} custom-call(bf16[512,1024]{1,0:T(8,128)(2,1)} %bitcast.26.refs_0_, bf16[512,1024]{1,0:T(8,128)(2,1)} %collective-permute-done.13.refs_1_, bf16[1024,512]{1,0:T(8,128)(2,1)S(1)} %copy-done.60, bf16[2,1024,512]{2,1,0:T(8,128)(2,1)} %collective-permute-done.25.refs_3_, ...), custom_call_target="tpu_custom_call" | custom-call | flops 10000000000 | bytes 1000 | tf_op jit(solution)/shard_map/up_grad/pallas_call | solution.py:31
  329.7 3.6 collective-permute-start.40
  337.3 3.6 hidden_grad.3.refs_6_
  350.4 7.4 %project_grad_pack.1.refs_4_.refs_5_ = bf16[8,144,768]{2,1,0:T(8,128)(2,1)} custom-call(s32[4]{0:T(128)S(1)} %pad_add_fusion.1.refs_0_.refs_2_, bf16[2,256,1024]{2,1,0:T(8,128)(2,1)S(1)} %copy-done.9, bf16[2,256,1024]{2,1,0:T(8,128)(2,1)} %collective-permute-done.refs_5_.refs_2_, bf16[2,256,1024]{2,1,0:T(8,128)(2,1)} %collective-permute-done.1.refs_6_.refs_3_, ...), custom_call_target="tpu_custom_call" | custom-call | flops 10000000000 | bytes 1000 | tf_op jit(solution)/shard_map/project_grad_pack/pallas_call | solution.py:31
  367.4 13.1 %collective-permute-done.44.refs_2_ = bf16[2,128,512]{2,1,0:T(8,128)(2,1)S(1)} collective-permute-done((bf16[2,128,512]{2,1,0:T(8,128)(2,1)S(1)}, bf16[2,128,512]{2,1,0:T(8,128)(2,1)S(1)}, u32[]{:S(2)}, u32[]{:S(2)}) %collective-permute-start.44) | collective-permute-done | bytes 262176 | tf_op jit(solution)/shard_map/ppermute | solution.py:993
  381.2 3.6 hidden_grad.4
  391.7 3.1 lay_up.1
  402.3 4.0 hidden_grad.5
  (386 shorter events, 154.2 us)
Async XLA Ops:
  7.2 53.3 %all-gather.9.cloned.1.call-start = ((), (), s32[]{:S(2)}) async-start(), calls=%async_computation.6 | async-start | bytes 1990656 | tf_op jit(solution)/shard_map/all_gather | solution.py:1089
  7.3 61.1 %collective-permute-start.1 = (bf16[2,256,1024]{2,1,0:T(8,128)(2,1)}, bf16[2,256,1024]{2,1,0:T(8,128)(2,1)}, u32[]{:S(2)}, u32[]{:S(2)}) collective-permute-start(bf16[2,256,1024]{2,1,0:T(8,128)(2,1)} %refs_1_.1), channel_id=1, source_target_pairs={{0,16},{1,9},{2,18},{3,11},{4,20},{5,13},{6,22},{7,15},{8,24},{9,1... | collective-permute-start | bytes 3145736 | tf_op jit(solution)/shard_map/ppermute | solution.py:993
  10.3 23.4 %collective-permute-start = (bf16[2,256,1024]{2,1,0:T(8,128)(2,1)}, bf16[2,256,1024]{2,1,0:T(8,128)(2,1)}, u32[]{:S(2)}, u32[]{:S(2)}) collective-permute-start(bf16[2,256,1024]{2,1,0:T(8,128)(2,1)} %refs_1_.1), channel_id=1, source_target_pairs={{0,8},{1,17},{2,10},{3,19},{4,12},{5,21},{6,14},{7,23},{8,0},{9,25... | collective-permute-start | bytes 3145736 | tf_op jit(solution)/shard_map/ppermute | solution.py:993
  15.1 74.2 %all-gather.5.cloned.1.call-start = ((), (), s32[]{:S(2)}) async-start(), calls=%async_computation.2 | async-start | bytes 1310720 | tf_op jit(solution)/shard_map/all_gather | solution.py:1109
  18.1 17.5 %collective-permute-start.6 = (bf16[256,512]{1,0:T(8,128)(2,1)S(1)}, bf16[256,512]{1,0:T(8,128)(2,1)S(1)}, u32[]{:S(2)}, u32[]{:S(2)}) collective-permute-start(bf16[256,512]{1,0:T(8,128)(2,1)S(1)} %pad_maximum_fusion.refs_1_), channel_id=1, source_target_pairs={{0,6},{2,0},{4,2},{6,4},{1,7},{3,1},{5,3},{7,5},{8,14},{10,8},{12,... | collective-permute-start | bytes 786440 | tf_op jit(solution)/shard_map/ppermute | solution.py:1020
  21.7 37.2 %collective-permute-start.5 = (bf16[256,512]{1,0:T(8,128)(2,1)S(1)}, bf16[256,512]{1,0:T(8,128)(2,1)S(1)}, u32[]{:S(2)}, u32[]{:S(2)}) collective-permute-start(bf16[256,512]{1,0:T(8,128)(2,1)S(1)} %pad_maximum_fusion.refs_1_), channel_id=1, source_target_pairs={{0,4},{2,6},{4,0},{6,2},{1,5},{3,7},{5,1},{7,3},{8,12},{10,14},{12... | collective-permute-start | bytes 786440 | tf_op jit(solution)/shard_map/ppermute | solution.py:1020
  21.7 37.2 %collective-permute-start.4 = (bf16[256,512]{1,0:T(8,128)(2,1)S(1)}, bf16[256,512]{1,0:T(8,128)(2,1)S(1)}, u32[]{:S(2)}, u32[]{:S(2)}) collective-permute-start(bf16[256,512]{1,0:T(8,128)(2,1)S(1)} %pad_maximum_fusion.refs_1_), channel_id=1, source_target_pairs={{0,2},{2,4},{4,6},{6,0},{1,3},{3,5},{5,7},{7,1},{8,10},{10,12},{12... | collective-permute-start | bytes 786440 | tf_op jit(solution)/shard_map/ppermute | solution.py:1020
  33.7 29.1 %collective-permute-start.2 = (bf16[2,256,1024]{2,1,0:T(8,128)(2,1)}, bf16[2,256,1024]{2,1,0:T(8,128)(2,1)S(1)}, u32[]{:S(2)}, u32[]{:S(2)}) collective-permute-start(bf16[2,256,1024]{2,1,0:T(8,128)(2,1)} %collective-permute-done.refs_5_.refs_2_), channel_id=1, source_target_pairs={{0,16},{1,9},{2,18},{3,11},{4,20},{5,13},{6,22},{7,15},{8,24},{9,1... | collective-permute-start | bytes 3145736 | tf_op jit(solution)/shard_map/ppermute | solution.py:993
  62.7 72.1 %all-gather.7.cloned.1.call-start = ((), (), s32[]{:S(2)}) async-start(), calls=%async_computation.3 | async-start | bytes 2359296 | tf_op jit(solution)/shard_map/all_gather | solution.py:1110
  65.5 25.7 %collective-permute-start.8 = (bf16[1024,512]{1,0:T(8,128)(2,1)}, bf16[1024,512]{1,0:T(8,128)(2,1)}, u32[]{:S(2)}, u32[]{:S(2)}) collective-permute-start(bf16[1024,512]{1,0:T(8,128)(2,1)} %hold.3.refs_2_.refs_10_), channel_id=1, source_target_pairs={{0,16},{1,9},{2,18},{3,11},{4,20},{5,13},{6,22},{7,15},{8,24},{9,1... | collective-permute-start | bytes 3145736 | tf_op jit(solution)/shard_map/ppermute | solution.py:993
  65.8 25.4 %collective-permute-start.7 = (bf16[1024,512]{1,0:T(8,128)(2,1)}, bf16[1024,512]{1,0:T(8,128)(2,1)}, u32[]{:S(2)}, u32[]{:S(2)}) collective-permute-start(bf16[1024,512]{1,0:T(8,128)(2,1)} %hold.3.refs_2_.refs_10_), channel_id=1, source_target_pairs={{0,8},{1,17},{2,10},{3,19},{4,12},{5,21},{6,14},{7,23},{8,0},{9,25... | collective-permute-start | bytes 3145736 | tf_op jit(solution)/shard_map/ppermute | solution.py:993
  68.0 255.2 %reduce-scatter.3.cloned.1.call-start = ((), (), s32[]{:S(2)}) async-start(), calls=%async_computation.4 | async-start | bytes 2654208 | tf_op jit(solution)/shard_map/reduce_scatter | solution.py:1188
  89.3 44.6 %collective-permute-start.12 = (bf16[512,1024]{1,0:T(8,128)(2,1)}, bf16[512,1024]{1,0:T(8,128)(2,1)S(1)}, u32[]{:S(2)}, u32[]{:S(2)}) collective-permute-start(bf16[512,1024]{1,0:T(8,128)(2,1)} %all-gather.5.cloned.1.call-done.refs_8_.refs_4_.refs_6_), channel_id=1, source_target_pairs={{0,8},{1,17},{2,10},{3,19},{4,12},{5,21},{6,14},{7,23},{8,0},{9,25... | collective-permute-start | bytes 3145736 | tf_op jit(solution)/shard_map/ppermute | solution.py:993
  122.1 26.0 %collective-permute-start.14 = (bf16[1024,512]{1,0:T(8,128)(2,1)}, bf16[1024,512]{1,0:T(8,128)(2,1)}, u32[]{:S(2)}, u32[]{:S(2)}) collective-permute-start(bf16[1024,512]{1,0:T(8,128)(2,1)} %collective-permute-done.7.refs_6_.refs_3_.refs_11_), channel_id=1, source_target_pairs={{0,16},{1,9},{2,18},{3,11},{4,20},{5,13},{6,22},{7,15},{8,24},{9,1... | collective-permute-start | bytes 3145736 | tf_op jit(solution)/shard_map/ppermute | solution.py:993
  147.0 25.3 %collective-permute-start.16 = (bf16[512,1024]{1,0:T(8,128)(2,1)}, bf16[512,1024]{1,0:T(8,128)(2,1)S(1)}, u32[]{:S(2)}, u32[]{:S(2)}) collective-permute-start(bf16[512,1024]{1,0:T(8,128)(2,1)} %copy-done.17), channel_id=1, source_target_pairs={{0,16},{1,9},{2,18},{3,11},{4,20},{5,13},{6,22},{7,15},{8,24},{9,1... | collective-permute-start | bytes 3145736 | tf_op jit(solution)/shard_map/ppermute | solution.py:993
  206.4 36.4 %collective-permute-start.23 = (bf16[2,512,1024]{2,1,0:T(8,128)(2,1)}, bf16[2,512,1024]{2,1,0:T(8,128)(2,1)}, u32[]{:S(2)}, u32[]{:S(2)}) collective-permute-start(bf16[2,512,1024]{2,1,0:T(8,128)(2,1)} %down_grad.3.refs_0_), channel_id=1, source_target_pairs={{0,8},{1,17},{2,10},{3,19},{4,12},{5,21},{6,14},{7,23},{8,0},{9,25... | collective-permute-start | bytes 6291464 | tf_op jit(solution)/shard_map/ppermute | solution.py:993
  239.3 19.5 %collective-permute-start.20 = (bf16[2,256,256]{2,1,0:T(8,128)(2,1)}, bf16[2,256,256]{2,1,0:T(8,128)(2,1)}, u32[]{:S(2)}, u32[]{:S(2)}) collective-permute-start(bf16[2,256,256]{2,1,0:T(8,128)(2,1)} %get-tuple-element.87), channel_id=1, source_target_pairs={{0,8},{1,17},{2,10},{3,19},{4,12},{5,21},{6,14},{7,23},{8,0},{9,25... | collective-permute-start | bytes 786440 | tf_op jit(solution)/shard_map/ppermute | solution.py:1016
  239.9 18.9 %collective-permute-start.21 = (bf16[2,256,256]{2,1,0:T(8,128)(2,1)}, bf16[2,256,256]{2,1,0:T(8,128)(2,1)}, u32[]{:S(2)}, u32[]{:S(2)}) collective-permute-start(bf16[2,256,256]{2,1,0:T(8,128)(2,1)} %get-tuple-element.88), channel_id=1, source_target_pairs={{0,16},{1,9},{2,18},{3,11},{4,20},{5,13},{6,22},{7,15},{8,24},{9,1... | collective-permute-start | bytes 786440 | tf_op jit(solution)/shard_map/ppermute | solution.py:1016
  241.1 17.7 %collective-permute-start.22 = (bf16[2,256,256]{2,1,0:T(8,128)(2,1)}, bf16[2,256,256]{2,1,0:T(8,128)(2,1)}, u32[]{:S(2)}, u32[]{:S(2)}) collective-permute-start(bf16[2,256,256]{2,1,0:T(8,128)(2,1)} %get-tuple-element.89), channel_id=1, source_target_pairs={{0,24},{1,25},{2,26},{3,27},{4,28},{5,29},{6,30},{7,31},{8,16},{9,... | collective-permute-start | bytes 786440 | tf_op jit(solution)/shard_map/ppermute | solution.py:1016
  253.5 36.7 %collective-permute-start.25 = (bf16[2,1024,512]{2,1,0:T(8,128)(2,1)}, bf16[2,1024,512]{2,1,0:T(8,128)(2,1)}, u32[]{:S(2)}, u32[]{:S(2)}) collective-permute-start(bf16[2,1024,512]{2,1,0:T(8,128)(2,1)} %up_grad.3.refs_7_), channel_id=1, source_target_pairs={{0,8},{1,17},{2,10},{3,19},{4,12},{5,21},{6,14},{7,23},{8,0},{9,25... | collective-permute-start | bytes 6291464 | tf_op jit(solution)/shard_map/ppermute | solution.py:993
  254.2 41.0 %collective-permute-start.24 = (bf16[1,512,1024]{2,1,0:T(8,128)(2,1)}, bf16[1,512,1024]{2,1,0:T(8,128)(2,1)}, u32[]{:S(2)}, u32[]{:S(2)}) collective-permute-start(bf16[1,512,1024]{2,1,0:T(8,128)(2,1)} %down_grad.4.refs_4_), channel_id=1, source_target_pairs={{0,16},{1,9},{2,18},{3,11},{4,20},{5,13},{6,22},{7,15},{8,24},{9,1... | collective-permute-start | bytes 3145736 | tf_op jit(solution)/shard_map/ppermute | solution.py:993
  258.7 131.8 %reduce-scatter.5.cloned.1.call-start = ((), (), s32[]{:S(2)}) async-start(), calls=%async_computation.5 | async-start | bytes 1990656 | tf_op jit(solution)/shard_map/reduce_scatter | solution.py:1216
  294.1 23.7 %collective-permute-start.26 = (bf16[1,1024,512]{2,1,0:T(8,128)(2,1)S(1)}, bf16[1,1024,512]{2,1,0:T(8,128)(2,1)S(1)}, u32[]{:S(2)}, u32[]{:S(2)}) collective-permute-start(bf16[1,1024,512]{2,1,0:T(8,128)(2,1)S(1)} %up_grad.4.refs_5_.refs_14_), channel_id=1, source_target_pairs={{0,16},{1,9},{2,18},{3,11},{4,20},{5,13},{6,22},{7,15},{8,24},{9,1... | collective-permute-start | bytes 3145736 | tf_op jit(solution)/shard_map/ppermute | solution.py:993
  299.3 23.1 %collective-permute-start.27 = (bf16[128,1024]{1,0:T(8,128)(2,1)S(1)}, bf16[128,1024]{1,0:T(8,128)(2,1)S(1)}, u32[]{:S(2)}, u32[]{:S(2)}) collective-permute-start(bf16[128,1024]{1,0:T(8,128)(2,1)S(1)} %get-tuple-element.102), channel_id=1, source_target_pairs={{0,2},{2,4},{4,6},{6,0},{1,3},{3,5},{5,7},{7,1},{8,10},{10,12},{12... | collective-permute-start | bytes 786440 | tf_op jit(solution)/shard_map/ppermute | solution.py:1020
  300.9 21.6 %collective-permute-start.28 = (bf16[128,1024]{1,0:T(8,128)(2,1)S(1)}, bf16[128,1024]{1,0:T(8,128)(2,1)S(1)}, u32[]{:S(2)}, u32[]{:S(2)}) collective-permute-start(bf16[128,1024]{1,0:T(8,128)(2,1)S(1)} %get-tuple-element.103), channel_id=1, source_target_pairs={{0,4},{2,6},{4,0},{6,2},{1,5},{3,7},{5,1},{7,3},{8,12},{10,14},{12... | collective-permute-start | bytes 786440 | tf_op jit(solution)/shard_map/ppermute | solution.py:1020
  301.8 20.6 %collective-permute-start.29 = (bf16[128,1024]{1,0:T(8,128)(2,1)S(1)}, bf16[128,1024]{1,0:T(8,128)(2,1)S(1)}, u32[]{:S(2)}, u32[]{:S(2)}) collective-permute-start(bf16[128,1024]{1,0:T(8,128)(2,1)S(1)} %get-tuple-element.104), channel_id=1, source_target_pairs={{0,6},{2,0},{4,2},{6,4},{1,7},{3,1},{5,3},{7,5},{8,14},{10,8},{12,... | collective-permute-start | bytes 786440 | tf_op jit(solution)/shard_map/ppermute | solution.py:1020
  329.7 28.1 %collective-permute-start.40 = (bf16[256,512]{1,0:T(8,128)(2,1)}, bf16[256,512]{1,0:T(8,128)(2,1)}, u32[]{:S(2)}, u32[]{:S(2)}) collective-permute-start(bf16[256,512]{1,0:T(8,128)(2,1)} %get-tuple-element.110), channel_id=1, source_target_pairs={{0,2},{2,4},{4,6},{6,0},{1,3},{3,5},{5,7},{7,1},{8,10},{10,12},{12... | collective-permute-start | bytes 786440 | tf_op jit(solution)/shard_map/ppermute | solution.py:1020
  333.3 24.6 %collective-permute-start.41 = (bf16[256,512]{1,0:T(8,128)(2,1)}, bf16[256,512]{1,0:T(8,128)(2,1)}, u32[]{:S(2)}, u32[]{:S(2)}) collective-permute-start(bf16[256,512]{1,0:T(8,128)(2,1)} %get-tuple-element.111), channel_id=1, source_target_pairs={{0,4},{2,6},{4,0},{6,2},{1,5},{3,7},{5,1},{7,3},{8,12},{10,14},{12... | collective-permute-start | bytes 786440 | tf_op jit(solution)/shard_map/ppermute | solution.py:1020
  347.9 33.4 %collective-permute-start.30 = (bf16[2,2,256,1024]{3,2,1,0:T(8,128)(2,1)}, bf16[2,2,256,1024]{3,2,1,0:T(8,128)(2,1)}, u32[]{:S(2)}, u32[]{:S(2)}) collective-permute-start(bf16[2,2,256,1024]{3,2,1,0:T(8,128)(2,1)} %hidden_grad.3.refs_6_), channel_id=1, source_target_pairs={{0,8},{1,17},{2,10},{3,19},{4,12},{5,21},{6,14},{7,23},{8,0},{9,25... | collective-permute-start | bytes 6291464 | tf_op jit(solution)/shard_map/ppermute | solution.py:993
  363.8 16.7 %collective-permute-start.44 = (bf16[2,128,512]{2,1,0:T(8,128)(2,1)S(1)}, bf16[2,128,512]{2,1,0:T(8,128)(2,1)S(1)}, u32[]{:S(2)}, u32[]{:S(2)}) collective-permute-start(bf16[2,128,512]{2,1,0:T(8,128)(2,1)S(1)} %pair.1.refs_1_), channel_id=1, source_target_pairs={{0,8},{1,17},{2,10},{3,19},{4,12},{5,21},{6,14},{7,23},{8,0},{9,25... | collective-permute-start | bytes 786440 | tf_op jit(solution)/shard_map/ppermute | solution.py:993
  366.7 24.9 %collective-permute-start.45 = (bf16[2,128,512]{2,1,0:T(8,128)(2,1)S(1)}, bf16[2,128,512]{2,1,0:T(8,128)(2,1)S(1)}, u32[]{:S(2)}, u32[]{:S(2)}) collective-permute-start(bf16[2,128,512]{2,1,0:T(8,128)(2,1)S(1)} %pair.1.refs_1_), channel_id=1, source_target_pairs={{0,16},{1,9},{2,18},{3,11},{4,20},{5,13},{6,22},{7,15},{8,24},{9,1... | collective-permute-start | bytes 786440 | tf_op jit(solution)/shard_map/ppermute | solution.py:993
  384.9 17.4 %collective-permute-start.34 = (bf16[1,2,256,1024]{3,2,1,0:T(8,128)(2,1)}, bf16[1,2,256,1024]{3,2,1,0:T(8,128)(2,1)S(1)}, u32[]{:S(2)}, u32[]{:S(2)}) collective-permute-start(bf16[1,2,256,1024]{3,2,1,0:T(8,128)(2,1)} %hidden_grad.4), channel_id=1, source_target_pairs={{0,16},{1,9},{2,18},{3,11},{4,20},{5,13},{6,22},{7,15},{8,24},{9,1... | collective-permute-start | bytes 3145736 | tf_op jit(solution)/shard_map/ppermute | solution.py:993
  (125 other events, 740.9 us)
Sparse Core Ops, SparseCore 0:
  15.2 44.7 all-gather.8
  62.9 26.3 all-gather.4
  91.5 28.5 all-gather.6
  258.8 35.1 reduce-scatter.2
  358.0 32.5 reduce-scatter.4
where the time goes:
time: 421 us; the launch traced here: 417 us
  Pallas kernels  163 us (39%)
  waiting for transfers between devices  108 us (26%)
  local copies, waits for them, and re-layouts  68.5 us (16%)
  starting transfers between devices  55.1 us (13%)
  between operations  15 us (4%)
  other arithmetic  6.78 us (2%)
    pallas_call x37, Pallas kernels, run(): pl.pallas_call(waiting, grid_spec=pltpu.PrefetchScalarGridSpec(num_scalar...  163 us
    unnamed x213, local copies, waits for them, and re-layouts  60.8 us
    ppermute x26, waiting for transfers between devices, hop(): return lax.ppermute(block, AXES, pairs)  57.7 us
    ppermute x26, starting transfers between devices, hop(): return lax.ppermute(block, AXES, pairs)  30.1 us
    ppermute x9, waiting for transfers between devices, shift(): lax.ppermute(block, 'z', [(z, (z + d) % self.chips) for z in range(self.c...  23.4 us
    ppermute x9, starting transfers between devices, shift(): lax.ppermute(block, 'z', [(z, (z + d) % self.chips) for z in range(self.c...  16.3 us
    ppermute x6, waiting for transfers between devices, exchange(): out.append(lax.ppermute(blocks[q], AXES, pairs))  10.8 us
    all_gather x1, waiting for transfers between devices, local(): down_block = lax.all_gather(down_rows, 'z', axis=0, tiled=True)  9.13 us
  transfers between devices with their start and end apart: 52, of which 18 were waited for; matrix products, arithmetic and copies ran while one was open for 3% of the time, Pallas kernels for 35%

commit v1 on v0

--- a/solution.py
+++ b/solution.py
@@ -9,7 +9,12 @@
 from jax.sharding import PartitionSpec as P
 
 HEAD_DIM = 64
-SPAN = 128
+SPAN = 256
+ALIGN = 128
+WINDOW = 512
+FORWARD_SPAN = 1024
+BACKWARD_SPAN = 512
+UNROLL = True
 MASKED = -1e30
 
 
@@ -35,8 +40,8 @@
         ),
         out_shape=shapes,
         input_output_aliases=alias or {},
-        compiler_params=pltpu.CompilerParams(vmem_limit_bytes=28 << 20),
-        cost_estimate=pl.CostEstimate(flops=cost * 1000000000, bytes_accessed=1000, transcendentals=0),
+        compiler_params=pltpu.CompilerParams(vmem_limit_bytes=50 << 20),
+        cost_estimate=pl.CostEstimate(flops=cost * 3000000000, bytes_accessed=1000, transcendentals=0),
         name=name,
     )(*prefetch, *operands)
 
@@ -565,7 +570,7 @@
     )
 
 
-def lay_up(places, blocks, chips, part):
+def lay_up(places, blocks, chips, part, waits=()):
     _, rows, _ = blocks[0].shape
     ranks = len(blocks)
     shape = (rows, 2 * chips * ranks * part)
@@ -586,6 +591,7 @@
         kind_of(shape, jnp.float32),
         arrays(blocks),
         prefetch=(places,),
+        waits=waits,
         cost=10,
     )
 
@@ -670,6 +676,7 @@
         [kind_of((size, width))] * chips,
         [own],
         prefetch=(at,),
+        cost=100,
         waits=waits,
     )
 
@@ -751,68 +758,82 @@
 
 def plan_rows(segments):
     b, t = segments.shape
-    n = t // SPAN
-    win = min(3 * SPAN, t)
-    spans = segments.reshape(b, n, SPAN)
+    span, win = min(SPAN, t), min(WINDOW, t)
+    spans = segments.reshape(b, t // span, span)
     place = jnp.arange(t, dtype=jnp.int32)
     low = jnp.min(jnp.where(segments[:, None, :] == spans[:, :, :1], place, t), axis=2)
     high = jnp.max(jnp.where(segments[:, None, :] == spans[:, :, -1:], place, -1), axis=2)
-    start = jnp.minimum(low // SPAN * SPAN, t - win)
+    start = jnp.minimum(low // ALIGN * ALIGN, t - win)
     fits = jnp.all(high < start + win, axis=1)
     single = jnp.all(segments == segments[:, :1], axis=1)
     kind = jnp.where(single, 0, jnp.where(fits, 1, 2))
     return kind.astype(jnp.int32), start.astype(jnp.int32)
 
+def aligned(start, size):
+    return start if isinstance(start, int) else pl.multiple_of(start, size)
+
+
+def bias_of(col_ref, keys, row_ref, queries):
+    return jnp.where(col_ref[0, keys, :] == row_ref[0, :, queries], 0.0, MASKED)
+
+
+def over(count, body):
+    if count == 1:
+        body(0)
+    else:
+        lax.fori_loop(0, count, lambda g, c: (body(g), c)[1], 0, unroll=UNROLL)
+
+
 def fwd_kernel(heads, kind_ref, start_ref, place_ref, qkv_ref, row_ref, col_ref, ctx_ref, lse_ref, *part_refs):
     b = pl.program_id(0)
     t = qkv_ref.shape[1]
     hw = heads * HEAD_DIM
-    win = min(3 * SPAN, t)
+    span, win = min(SPAN, t), min(WINDOW, t)
     kind = kind_ref[b]
 
-    def piece(h, which, rows):
-        lo = which * hw + h * HEAD_DIM
-        return qkv_ref[0, rows, lo:lo + HEAD_DIM]
-
-    def attend(h, rows, count, keys, masked):
-        q = piece(h, 0, rows)
-        s = dot(q, piece(h, 1, keys), 1, 1)
-        if masked:
-            s = jnp.where(col_ref[0, rows, :] == row_ref[0, :, keys], s, MASKED)
-        m = jnp.max(s, axis=1, keepdims=True)
-        e = jnp.exp(s - m)
-        total = jnp.sum(e, axis=1, keepdims=True)
-        c = dot(e.astype(jnp.bfloat16), piece(h, 2, keys), 1, 0) / total
-        ctx_ref[0, rows, h * HEAD_DIM:(h + 1) * HEAD_DIM] = c.astype(jnp.bfloat16)
-        lse = jnp.broadcast_to(m + jnp.log(total), (count, 128))
-        lse_ref[0, h:h + 1, rows] = jnp.transpose(lse)[0:1, :]
-
-    def dense(masked):
-        tile = min(256, t)
+    group = min(2, heads)
+    lanes = group * HEAD_DIM
+
+    def attend(g, rows, keys, bias):
+        def piece(which):
+            return pl.ds(aligned(which * hw + g * lanes, lanes), lanes)
+
+        query, key, value = (qkv_ref[0, r, piece(w)] for w, r in enumerate((rows, keys, keys)))
+        parts = []
+        for e in range(group):
+            at = slice(e * HEAD_DIM, (e + 1) * HEAD_DIM)
+            s = dot(key[:, at], query[:, at], 1, 1)
+            if bias is not None:
+                s = s + bias
+            m = jnp.max(s, axis=0, keepdims=True)
+            p = jnp.exp(s - m)
+            total = jnp.sum(p, axis=0, keepdims=True)
+            parts.append(dot(value[:, at], p.astype(jnp.bfloat16), 0, 0) / total)
+            lse_ref[0, pl.ds(g * group + e, 1), rows] = m + jnp.log(total)
+        ctx_ref[0, rows, piece(0)] = jnp.transpose(jnp.concatenate(parts, axis=0)).astype(jnp.bfloat16)
+
+    def each(size, masked, keys_of):
+        size = min(size, t)
+
         def body(i, _):
-            rows = pl.ds(pl.multiple_of(i * tile, tile), tile)
-            for h in range(heads):
-                attend(h, rows, tile, pl.ds(0, t), masked)
+            rows = pl.ds(pl.multiple_of(i * size, size), size)
+            bias = bias_of(col_ref, keys_of(i), row_ref, rows) if masked else None
+            over(heads // group, lambda g: attend(g, rows, keys_of(i), bias))
             return 0
-        lax.fori_loop(0, t // tile, body, 0)
+
+        lax.fori_loop(0, t // size, body, 0)
 
     @pl.when(kind == 0)
     def _():
-        dense(False)
+        each(FORWARD_SPAN, False, lambda i: pl.ds(0, t))
 
     @pl.when(kind == 2)
     def _():
-        dense(True)
+        each(span, True, lambda i: pl.ds(0, t))
 
     @pl.when(kind == 1)
     def _():
-        def body(i, _):
-            rows = pl.ds(pl.multiple_of(i * SPAN, SPAN), SPAN)
-            keys = pl.ds(pl.multiple_of(start_ref[b, i], SPAN), win)
-            for h in range(heads):
-                attend(h, rows, SPAN, keys, True)
-            return 0
-        lax.fori_loop(0, t // SPAN, body, 0)
+        each(span, True, lambda i: pl.ds(pl.multiple_of(start_ref[b, i], ALIGN), win))
 
     length = part_refs[0].shape[1]
     for q, part_ref in enumerate(part_refs):
@@ -845,67 +866,74 @@
 def bwd_kernel(heads, b, kind_ref, start_ref, qkv_ref, do_ref, ctx_ref, lse_ref, row_ref, col_ref, out_ref, dq_acc, delta_ref):
     t = qkv_ref.shape[1]
     hw = heads * HEAD_DIM
-    win = min(3 * SPAN, t)
+    span, win = min(SPAN, t), min(WINDOW, t)
     kind = kind_ref[b]
 
     def lanes(h, which=0):
         lo = which * hw + h * HEAD_DIM
         return slice(lo, lo + HEAD_DIM)
 
-    for h in range(heads):
-        prod = do_ref[0, :, lanes(h)].astype(jnp.float32) * ctx_ref[0, :, lanes(h)].astype(jnp.float32)
-        d = jnp.sum(prod, axis=1, keepdims=True)
-        delta_ref[h:h + 1, :] = jnp.transpose(jnp.broadcast_to(d, (t, 128)))[0:1, :]
-
-    def back(h, keys, queries, masked):
-        k = qkv_ref[0, keys, lanes(h, 1)]
-        v = qkv_ref[0, keys, lanes(h, 2)]
-        q = qkv_ref[0, queries, lanes(h, 0)]
-        do = do_ref[0, queries, lanes(h)]
-        s = dot(k, q, 1, 1)
-        if masked:
-            s = jnp.where(col_ref[0, keys, :] == row_ref[0, :, queries], s, MASKED)
-        p = jnp.exp(s - lse_ref[0, h:h + 1, queries])
-        dp = dot(v, do, 1, 1)
-        ds = (p * (dp - delta_ref[h:h + 1, queries])).astype(jnp.bfloat16)
-        dv = dot(p.astype(jnp.bfloat16), do, 1, 0)
-        dk = dot(ds, q, 1, 0)
-        out_ref[0, keys, lanes(h, 1)] = dk.astype(jnp.bfloat16)
-        out_ref[0, keys, lanes(h, 2)] = dv.astype(jnp.bfloat16)
-        return dot(k, ds, 0, 0)
+    prod = do_ref[0].astype(jnp.float32) * ctx_ref[0].astype(jnp.float32)
+    high = prod.astype(jnp.bfloat16)
+    rest = (prod - high.astype(jnp.float32)).astype(jnp.bfloat16)
+    head = lax.broadcasted_iota(jnp.int32, (delta_ref.shape[0], hw), 0)
+    of = lax.broadcasted_iota(jnp.int32, (delta_ref.shape[0], hw), 1) // HEAD_DIM
+    ones = (head == of).astype(jnp.bfloat16)
+    delta_ref[...] = dot(ones, high, 1, 1) + dot(ones, rest, 1, 1)
+
+    group = min(2, heads)
+    lanes = group * HEAD_DIM
+
+    def back(g, keys, queries, bias):
+        def piece(which):
+            return pl.ds(aligned(which * hw + g * lanes, lanes), lanes)
+
+        query, key, value = (qkv_ref[0, r, piece(w)] for w, r in enumerate((queries, keys, keys)))
+        grad = do_ref[0, queries, piece(0)]
+        key_grads, value_grads = [], []
+        for e in range(group):
+            at = slice(e * HEAD_DIM, (e + 1) * HEAD_DIM)
+            row = pl.ds(g * group + e, 1)
+            s = dot(key[:, at], query[:, at], 1, 1)
+            if bias is not None:
+                s = s + bias
+            p = jnp.exp(s - lse_ref[0, row, queries])
+            dp = dot(value[:, at], grad[:, at], 1, 1)
+            ds = (p * (dp - delta_ref[row, queries])).astype(jnp.bfloat16)
+            value_grads.append(dot(p.astype(jnp.bfloat16), grad[:, at], 1, 0))
+            key_grads.append(dot(ds, query[:, at], 1, 0))
+            into = pl.ds(aligned(g * lanes + e * HEAD_DIM, HEAD_DIM), HEAD_DIM)
+            dq_acc[into, queries] += dot(key[:, at], ds, 0, 0)
+        out_ref[0, keys, piece(1)] = jnp.concatenate(key_grads, axis=1).astype(jnp.bfloat16)
+        out_ref[0, keys, piece(2)] = jnp.concatenate(value_grads, axis=1).astype(jnp.bfloat16)
 
     dq_acc[...] = jnp.zeros_like(dq_acc)
 
-    def dense(masked):
-        tile = min(256, t)
+    def each(size, masked, queries_of):
+        size = min(size, t)
+
         def body(j, _):
-            keys = pl.ds(pl.multiple_of(j * tile, tile), tile)
-            for h in range(heads):
-                dq_acc[h] += back(h, keys, pl.ds(0, t), masked)
+            keys = pl.ds(pl.multiple_of(j * size, size), size)
+            bias = bias_of(col_ref, keys, row_ref, queries_of(j)) if masked else None
+            over(heads // group, lambda g: back(g, keys, queries_of(j), bias))
             return 0
-        lax.fori_loop(0, t // tile, body, 0)
+
+        lax.fori_loop(0, t // size, body, 0)
 
     @pl.when(kind == 0)
     def _():
-        dense(False)
+        each(BACKWARD_SPAN, False, lambda j: pl.ds(0, t))
 
     @pl.when(kind == 2)
     def _():
-        dense(True)
+        each(span, True, lambda j: pl.ds(0, t))
 
     @pl.when(kind == 1)
     def _():
-        def body(j, _):
-            keys = pl.ds(pl.multiple_of(j * SPAN, SPAN), SPAN)
-            queries = pl.ds(pl.multiple_of(start_ref[b, j], SPAN), win)
-            for h in range(heads):
-                dq_acc[h, :, queries] += back(h, keys, queries, True)
-            return 0
-        lax.fori_loop(0, t // SPAN, body, 0)
-
-    for h in range(heads):
-        dq = jnp.transpose(dq_acc[h]) * (HEAD_DIM ** -0.5)
-        out_ref[0, :, lanes(h, 0)] = dq.astype(jnp.bfloat16)
+        each(span, True, lambda j: pl.ds(pl.multiple_of(start_ref[b, j], ALIGN), win))
+
+    out_ref[0, :, :hw] = (jnp.transpose(dq_acc[...]) * (HEAD_DIM**-0.5)).astype(jnp.bfloat16)
+
 
 def attention_back(qkv, dparts, ctx, lse, segments, kind, start, places, which, buffer, waits):
     b, t, w = qkv.shape
@@ -946,8 +974,8 @@
         operands,
         prefetch=(kind, start, places),
         scratch=(
-            pltpu.VMEM((heads, HEAD_DIM, t), jnp.float32),
-            pltpu.VMEM((heads, t), jnp.float32),
+            pltpu.VMEM((hw, t), jnp.float32),
+            pltpu.VMEM((-(-heads // 8) * 8, t), jnp.float32),
             pltpu.VMEM((1, t, hw), jnp.bfloat16),
         ),
         alias=alias,
@@ -997,12 +1025,6 @@
         for k in range(self.count):
             blocks = blocks + [self.hop(b, k) for b in blocks]
         return [View(b) for b in blocks]
-
-    def total(self, block):
-        for k in range(self.count):
-            block = wide(block) + wide(self.hop(low(block), k))
-        return block
-
 
     def exchange(self, blocks):
         out = [blocks[0]]
@@ -1086,7 +1108,6 @@
     for i, vector in enumerate(vectors):
         packed = packed + jnp.pad(vector[None], ((i, EXTRA - 1 - i), (0, out_width - rows)))
     mine = jnp.concatenate([mine, packed], axis=0)
-    gathered = lax.all_gather(mine, ROWS, axis=0)
 
     def up_columns(of_core):
         return jnp.concatenate(
@@ -1105,6 +1126,7 @@
     shifts = jnp.stack([(z_index - d) % chips for d in range(chips)]).astype(jnp.int32)
     up_block = lay_chips(shifts, [up_rows] + [ring.shift(up_rows, d) for d in range(1, chips)], ())
     up_block = hold(up_block.reshape(width, chips * part), (hidden[-1].array,))
+    gathered = lax.all_gather(mine, ROWS, axis=0)
     down_rows = hold(lax.dynamic_slice_in_dim(down_weight, here * part, part, 0), (gathered,))
     down_block = lax.all_gather(down_rows, "z", axis=0, tiled=True)
     output_weight = lax.all_gather(hold(out_weight, (down_rows,)), ROWS, axis=0, tiled=True)
@@ -1120,17 +1142,16 @@
     scales = jnp.where(jnp.arange(out_width) < head_width, score_scale, 1.0)[None]
     qkv = project(places, hidden, qkv_weight, qkv_bias, scales)
     contexts, log_totals, *context_parts = attention(
-        qkv, segments, kind, start, places, (*arrays(up_weights[1:3]), down_block)
+        qkv, segments, kind, start, places, (up_block,)
     )
     context_parts = ring.exchange(context_parts)
-    down_weights = ring.gather(down_block)
+    down_weights = ring.gather(hold(down_block, (*context_parts[1:], *arrays(up_weights[1:3]))))
     sums_one, first_low = out_norm(
         places,
         context_parts,
         output_weight,
         hidden_in,
         vectors,
-        arrays(down_weights[1:2]),
     )
 
     first_low = first_low.reshape(count, width)
@@ -1140,7 +1161,9 @@
     upper_bias = [
         lax.dynamic_index_in_dim(upper_bias, ring.place(q), 1, False).reshape(1, -1) for q in blocks
     ]
-    actives, slopes = up_forward(first_low, first_other, up_weights, upper_bias)
+    actives, slopes = up_forward(
+        first_low, first_other, up_weights, upper_bias, arrays(down_weights[1:2])
+    )
     mixed_other = down_forward(actives, down_weights, count, count, jnp.bfloat16)
     mixed = down_forward(actives, down_weights, 0, count, jnp.float32, (mixed_other,))
     layer_out, dsum_two, dmixed, totals_two = norm_two(mixed, swap(mixed_other), sums_one, vectors, out_grad, keep)
@@ -1191,43 +1214,46 @@
     dqkv = attention_back(*common, 0, None, (out_pack,))
 
     def up_made(turn, addends):
-        return up_grad([duppers[q] for q in turn], first_low, first_other, addends, (dqkv,))
-
-    up_came, up_hop = spread(up_made, up_sent)
-    down_own = down_grad([actives[0]], dmixed, dmixed_other, [down_came], (up_hop,))[0]
+        return up_grad([duppers[q] for q in turn], first_low, first_other, addends, (down_pieces[0],))
+
+    down_own = down_grad([actives[0]], dmixed, dmixed_other, [down_came], (dqkv,))[0]
     ahead = jnp.stack([(z_index + d) % chips for d in range(chips)]).astype(jnp.int32)
     down_pieces = split(ahead, down_own, part)
+    up_came, up_hop = spread(up_made, up_sent)
     for which in range(1, seqs):
-        dqkv = attention_back(*common, which, dqkv, (down_pieces[0], up_hop))
+        dqkv = attention_back(*common, which, dqkv, (up_hop,))
 
     def shifted(pieces):
         return [pieces[0]] + [ring.shift(pieces[d], d) for d in range(1, chips)]
 
-    down_shard = total_rows(shifted(down_pieces), (dqkv, out_shard))
+    def hidden_made(turn, addends, waits=()):
+        return hidden_grad(places, dqkv, qkv_weight, length, turn, addends, jnp.bfloat16, waits or (up_pieces[0],))
+
+    qkv_pack = project_grad_pack(places, hidden, dqkv, owners, EXTRA, (out_shard,))
+    qkv_shard = lax.psum_scatter(qkv_pack.reshape(-1, out_width), ROWS, scatter_dimension=0, tiled=True)
+    out_sum = [wide(out_shard)]
+    for k in range(ring.count):
+        out_sent = low(out_sum[-1])
+        out_sum.append(out_sum[-1] + wide(ring.hop(out_sent, k)))
+    hidden_sent = hidden_made(odd, none, (qkv_pack, out_sent))
+    down_shard = total_rows(shifted(down_pieces), (hidden_sent,))
+    up_own = up_grad([duppers[0]], first_low, first_other, [up_came], (down_shard,))[0]
+    up_pieces = split(ahead, up_own, 2 * rows)
+    hidden_came, hidden_hop = spread(hidden_made, hidden_sent)
+    keep_part, take_part = total_halves(core_index, shifted(up_pieces), (hidden_hop,))
+    down_shard = hold(down_shard, (keep_part,))
     down_parts = ring.gather(down_shard)
-
-    def hidden_made(turn, addends, waits=()):
-        return hidden_grad(places, dqkv, qkv_weight, length, turn, addends, jnp.bfloat16, waits or (qkv_pack,))
-
-    up_own = up_grad([duppers[0]], first_low, first_other, [up_came], (dqkv,))[0]
-    up_pieces = split(ahead, up_own, 2 * rows)
-    hidden_sent = hidden_made(odd, none, (up_pieces[0], down_shard))
-    qkv_pack = project_grad_pack(places, hidden, dqkv, owners, EXTRA, (hidden_sent, *arrays(down_parts)))
-    qkv_shard = lax.psum_scatter(qkv_pack.reshape(-1, out_width), ROWS, scatter_dimension=0, tiled=True)
-
-    hidden_came, hidden_hop = spread(hidden_made, hidden_sent)
-    keep_part, take_part = total_halves(core_index, shifted(up_pieces), (qkv_pack,))
-    down_weight_grad = lay_rows(places, down_parts, (keep_part,))
-    up_pair = pair(core_index, keep_part, swap(take_part), (down_weight_grad,))
+    up_pair = pair(core_index, keep_part, swap(take_part), (down_shard,))
     input_grad = hidden_grad(
         places, dqkv, qkv_weight, length, [0], [[View(dsum_one)] + hidden_came], jnp.float32
     )[0]
 
     up_parts = ring.gather(up_pair)
     qkv_parts = ring.gather(qkv_shard)
-    out_pack = ring.total(out_shard)
+    out_pack = out_sum[-1]
+    down_weight_grad = lay_rows(places, down_parts, (input_grad,))
     if part % 128 == 0:
-        up_weight_grad = lay_up(places, up_parts, chips, part)
+        up_weight_grad = lay_up(places, up_parts, chips, part, (input_grad,))
     else:
         up_weight_grad = wide(put([b.value()[None] for b in up_parts], ring, 0))
         up_weight_grad = (

time: 421 us -> 391 us (0.929)
  local copies, waits for them, and re-layouts: 68.5 us -> 34.4 us
  Pallas kernels: 163 us -> 175 us
  waiting for transfers between devices: 108 us -> 97.2 us
    unnamed x213 -> x126, local copies, waits for them, and re-layouts: 60.8 us -> 23.6 us
    ppermute x26, waiting for transfers between devices: 57.7 us -> 43.4 us  [hop(): return lax.ppermute(block, AXES, pairs)]
    pallas_call x37 -> x39, Pallas kernels: 163 us -> 175 us  [run(): pl.pallas_call(waiting, grid_spec=pltpu.PrefetchScalarGridSpec(num_scalar...]
    ppermute x9, waiting for transfers between devices: 23.4 us -> 33.2 us  [shift(): lax.ppermute(block, 'z', [(z, (z + d) % self.chips) for z in range(self.c...]
    all_gather x1, waiting for transfers between devices: 9.13 us -> 0.01 us  [local(): down_block = lax.all_gather(down_rows, 'z', axis=0, tiled=True)]
    all_gather x1, waiting for transfers between devices: 0.01 us -> 6.65 us  [local(): lax.all_gather(hold(out_weight, (down_rows,)), ROWS, axis=0, tiled=True)]
  transfers between devices with their start and end apart: 52 -> 52, of which waited for: 18 -> 17; matrix products, arithmetic and copies ran while one was open for 3% -> 4% of each run, Pallas kernels for 35% -> 41%
where the time goes in v1:
time: 391 us; the launch traced here: 384 us
  Pallas kernels  175 us (45%)
  waiting for transfers between devices  97.2 us (25%)
  starting transfers between devices  56.3 us (14%)
  local copies, waits for them, and re-layouts  34.4 us (9%)
  between operations  14.8 us (4%)
  other arithmetic  6.99 us (2%)
    pallas_call x39, Pallas kernels, run(): pl.pallas_call(waiting, grid_spec=pltpu.PrefetchScalarGridSpec(num_scalar...  175 us
    ppermute x26, waiting for transfers between devices, hop(): return lax.ppermute(block, AXES, pairs)  43.4 us
    ppermute x9, waiting for transfers between devices, shift(): lax.ppermute(block, 'z', [(z, (z + d) % self.chips) for z in range(self.c...  33.2 us
    ppermute x26, starting transfers between devices, hop(): return lax.ppermute(block, AXES, pairs)  29.7 us
    unnamed x126, local copies, waits for them, and re-layouts  23.6 us
    ppermute x9, starting transfers between devices, shift(): lax.ppermute(block, 'z', [(z, (z + d) % self.chips) for z in range(self.c...  18.5 us
    ppermute x6, waiting for transfers between devices, exchange(): out.append(lax.ppermute(blocks[q], AXES, pairs))  10.8 us
  transfers between devices with their start and end apart: 52, of which 17 were waited for; matrix products, arithmetic and copies ran while one was open for 4% of the time, Pallas kernels for 41%

profile of v1, /device:TPU:0, one launch (start us, length us, event | category | flops | bytes accessed | tf_op | source)
XLA Modules:
  0.0 384.1 jit_solution(11814443580309061090)
XLA Ops:
  18.1 3.7 collective-permute-start.6
  23.3 10.5 %collective-permute-done.refs_5_.refs_2_ = bf16[2,256,1024]{2,1,0:T(8,128)(2,1)} collective-permute-done((bf16[2,256,1024]{2,1,0:T(8,128)(2,1)}, bf16[2,256,1024]{2,1,0:T(8,128)(2,1)}, u32[]{:S(2)}, u32[]{:S(2)}) %collective-permute-start) | collective-permute-done | bytes 1048608 | tf_op jit(solution)/shard_map/ppermute | solution.py:1021
  35.5 23.5 %collective-permute-done.5.refs_3_ = bf16[256,512]{1,0:T(8,128)(2,1)S(1)} collective-permute-done((bf16[256,512]{1,0:T(8,128)(2,1)S(1)}, bf16[256,512]{1,0:T(8,128)(2,1)S(1)}, u32[]{:S(2)}, u32[]{:S(2)}) %collective-permute-start.5) | collective-permute-done | bytes 262176 | tf_op jit(solution)/shard_map/ppermute | solution.py:1042
  69.1 10.0 %project.1.refs_3_ = bf16[2,1024,768]{2,1,0:T(8,128)(2,1)} custom-call(s32[4]{0:T(128)S(1)} %pad_add_fusion.1.refs_0_.refs_2_, bf16[1024,768]{1,0:T(8,128)(2,1)} %bitcast.84, f32[1,768]{1,0:T(1,128)S(1)} %broadcast_in_dim.133.refs_2_, f32[1,768]{1,0:T(1,128)S(1)} %compare_select_fusion.refs_3_, bf16[2,256,1024]{2,1,0:T(8,128)(2,1)S(1)} %copy-done.17, ...), custom_call_target="tpu_custom_call" | custom-call | flops 30000001024 | bytes 1000 | tf_op jit(solution)/shard_map/project/pallas_call | solution.py:36
  79.1 16.2 %attention_forward.1 = (bf16[2,1024,256]{2,1,0:T(8,128)(2,1)S(1)}, f32[2,4,1024]{2,1,0:T(4,128)S(1)}, bf16[2,256,256]{2,1,0:T(8,128)(2,1)S(1)}, bf16[2,256,256]{...) custom-call(s32[2]{0:T(128)S(1)} %select_select_fusion.refs_0_, ...), custom_call_target="tpu_custom_call" | custom-call | flops 299999985664 | bytes 1000 | tf_op jit(solution)/shard_map/attention_forward/pallas_call | solution.py:36
  101.8 3.7 collective-permute-done.7.refs_2_.refs_1_
  106.1 6.5 %collective-permute-done.9.refs_4_.refs_3_ = bf16[2,256,256]{2,1,0:T(8,128)(2,1)S(1)} collective-permute-done((bf16[2,256,256]{2,1,0:T(8,128)(2,1)S(1)}, bf16[2,256,256]{2,1,0:T(8,128)(2,1)S(1)}, u32[]{:S(2)}, u32[]{:S(2)}) %collective-permute-start.9) | collective-permute-done | bytes 262176 | tf_op jit(solution)/shard_map/ppermute | solution.py:1038
  116.6 6.6 %all-gather.5.cloned.1.call-done.refs_5_.refs_6_ = bf16[1024,1024]{1,0:T(8,128)(2,1)} async-done(((bf16[128,1024]{1,0:T(8,128)(2,1)}), bf16[1024,1024]{1,0:T(8,128)(2,1)}) %all-gather.5.cloned.1.call-update) | async-done | bytes 2097168 | tf_op jit(solution)/shard_map/all_gather | solution.py:1132
  123.3 5.2 %out_norm.1 = (f32[2,256,1024]{2,1,0:T(8,128)}, bf16[2,256,1024]{2,1,0:T(8,128)(2,1)}) custom-call(s32[4]{0:T(128)S(1)} %pad_add_fusion.1.refs_0_.refs_2_, bf16[2,256,256]{2,1,0:T(8,128)(2,1)S(1)} %get-tuple-element.66.refs_1_, bf16[2,256,256]{2,1,0:T(8,128)(2,1)S(1)} %collective-permute-done.7.refs_2_.refs_1_, ...), custom_call_target="tpu_custom_call" | custom-call | flops 30000001024 | bytes 1000 | tf_op jit(solution)/shard_map/out_norm/pallas_call | solution.py:36
  134.9 11.0 %up_forward.1 = (bf16[1024,512]{1,0:T(8,128)(2,1)S(1)}, bf16[1024,512]{1,0:T(8,128)(2,1)S(1)}, bf16[1024,512]{1,0:T(8,128)(2,1)S(1)}, bf16[1024,512]{1,0:T(8,128...) custom-call(bf16[512,1024]{1,0:T(8,128)(2,1)} %bitcast.26.refs_0_, ...), custom_call_target="tpu_custom_call" | custom-call | flops 30000001024 | bytes 1000 | tf_op jit(solution)/shard_map/up_forward/pallas_call | solution.py:36
  146.9 9.8 %collective-permute-done.16.refs_7_.refs_9_ = bf16[512,1024]{1,0:T(8,128)(2,1)S(1)} collective-permute-done((bf16[512,1024]{1,0:T(8,128)(2,1)}, bf16[512,1024]{1,0:T(8,128)(2,1)S(1)}, u32[]{:S(2)}, u32[]{:S(2)}) %collective-permute-start.16) | collective-permute-done | bytes 1048608 | tf_op jit(solution)/shard_map/ppermute | solution.py:1021
  157.7 5.0 %down_forward.2.refs_8_ = bf16[512,1024]{1,0:T(8,128)(2,1)S(1)} custom-call(bf16[1024,512]{1,0:T(8,128)(2,1)S(1)} %get-tuple-element.71.refs_0_.refs_2_, bf16[1024,512]{1,0:T(8,128)(2,1)S(1)} %get-tuple-element.72.refs_1_.refs_2_, bf16[1024,512]{1,0:T(8,128)(2,1)} %copy-done.45, bf16[1024,512]{1,0:T(8,128)(2,1)} %get-tuple-element.74.refs_3_, ...), custom_call_target="tpu_custom_call" | custom-call | flops 30000001024 | bytes 1000 | tf_op jit(solution)/shard_map/down_forward/pallas_call | solution.py:36
  163.6 5.8 %down_forward.3 = f32[512,1024]{1,0:T(8,128)} custom-call(bf16[1024,512]{1,0:T(8,128)(2,1)S(1)} %get-tuple-element.71.refs_0_.refs_2_, bf16[1024,512]{1,0:T(8,128)(2,1)S(1)} %get-tuple-element.72.refs_1_.refs_2_, bf16[1024,512]{1,0:T(8,128)(2,1)S(1)} %copy-done.46, bf16[1024,512]{1,0:T(8,128)(2,1)} %get-tuple-element.74.refs_3_, ...), custom_call_target="tpu_custom_call" | custom-call | flops 30000001024 | bytes 1000 | tf_op jit(solution)/shard_map/down_forward/pallas_call | solution.py:36
  169.4 5.6 %norm_two.1 = (bf16[2,256,1024]{2,1,0:T(8,128)(2,1)}, f32[2,256,1024]{2,1,0:T(8,128)}, bf16[2,256,1024]{2,1,0:T(8,128)(2,1)}, f32[8,1024]{1,0:T(8,128)S(1)}) custom-call(f32[2,256,1024]{2,1,0:T(8,128)} %bitcast.120, bf16[2,256,1024]{2,1,0:T(8,128)(2,1)S(1)} %bitcast.96, f32[2,256,1024]{2,1,0:T(8,128)} %get-tuple-element.75.refs_2_.refs_4_, ...), custom_call_target="tpu_custom_call" | custom-call | flops 30000001024 | bytes 1000 | tf_op jit(solution)/shard_map/norm_two/pallas_call | solution.py:36
  179.1 5.3 %down_grad.3.refs_0_ = bf16[2,512,1024]{2,1,0:T(8,128)(2,1)} custom-call(bf16[512,1024]{1,0:T(8,128)(2,1)} %bitcast.35.refs_0_, bf16[512,1024]{1,0:T(8,128)(2,1)S(1)} %collective-permute-done.18.refs_1_, bf16[1024,512]{1,0:T(8,128)(2,1)S(1)} %copy-done.48, bf16[1024,512]{1,0:T(8,128)(2,1)} %get-tuple-element.74.refs_3_), custom_call_target="tpu_custom_call" | custom-call | flops 30000001024 | bytes 1000 | tf_op jit(solution)/shard_map/down_grad/pallas_call | solution.py:36
  185.9 17.1 %feed_forward_back.1 = (bf16[1024,512]{1,0:T(8,128)(2,1)S(1)}, bf16[1024,512]{1,0:T(8,128)(2,1)S(1)}, bf16[1024,512]{1,0:T(8,128)(2,1)S(1)}, bf16[1024,512]{1,0:...) custom-call(bf16[512,1024]{1,0:T(8,128)(2,1)} %bitcast.35.refs_0_, ...), custom_call_target="tpu_custom_call" | custom-call | flops 30000001024 | bytes 1000 | tf_op jit(solution)/shard_map/feed_forward_back/pallas_call | solution.py:36
  207.8 7.1 %norm_one_back.1 = (f32[2,256,1024]{2,1,0:T(8,128)}, bf16[2,256,1024]{2,1,0:T(8,128)(2,1)S(1)}, bf16[2,256,256]{2,1,0:T(8,128)(2,1)S(1)}, bf16[2,256,256]{2,1,0:...) custom-call(s32[4]{0:T(128)S(1)} %pad_add_fusion.1.refs_0_.refs_2_, ...), custom_call_target="tpu_custom_call" | custom-call | flops 30000001024 | bytes 1000 | tf_op jit(solution)/shard_map/norm_one_back/pallas_call | solution.py:36
  219.7 3.8 down_grad.4.refs_4_
  225.1 5.6 %up_grad.3.refs_7_ = bf16[2,1024,512]{2,1,0:T(8,128)(2,1)} custom-call(bf16[512,1024]{1,0:T(8,128)(2,1)} %bitcast.26.refs_0_, bf16[512,1024]{1,0:T(8,128)(2,1)S(1)} %copy-done.21, bf16[1024,512]{1,0:T(8,128)(2,1)S(1)} %copy-done.40, bf16[1024,512]{1,0:T(8,128)(2,1)} %get-tuple-element.97.refs_3_, bf16[1,512,1024]{2,1,0:T(8,128)(2,1)} %down_grad.4.refs_4_), custom_call_target="tpu_custom_call" | custom-call | flops 30000001024 | bytes 1000 | tf_op jit(solution)/shard_map/up_grad/pallas_call | solution.py:36
  231.3 3.3 out_grad_pack.1.refs_12_
  236.8 14.8 %attention_backward.2.refs_5_.refs_12_ = bf16[2,1024,768]{2,1,0:T(8,128)(2,1)} custom-call(s32[2]{0:T(128)S(1)} %copy-done.36, s32[2,4]{1,0:T(2,128)S(1)} %get-tuple-element.118.refs_1_, s32[4]{0:T(128)S(1)} %pad_add_fusion.1.refs_0_.refs_2_, bf16[2,1024,768]{2,1,0:T(8,128)(2,1)} %project.1.refs_3_, bf16[2,256,256]{2,1,0:T(8,128)(2,1)S(1)} %copy-done.50, ...), custom_call_target="tpu_custom_call" | custom-call | flops 30000001024 | bytes 1000 | tf_op jit(solution)/shard_map/attention_backward/pallas_call | solution.py:36
  251.6 3.4 down_grad.5
  263.8 4.9 %up_grad.4.refs_13_ = bf16[1,1024,512]{2,1,0:T(8,128)(2,1)} custom-call(bf16[512,1024]{1,0:T(8,128)(2,1)} %bitcast.26.refs_0_, bf16[512,1024]{1,0:T(8,128)(2,1)S(1)} %copy-done.22, bf16[1024,512]{1,0:T(8,128)(2,1)} %copy-done.38, bf16[2,1024,512]{2,1,0:T(8,128)(2,1)} %collective-permute-done.24.refs_3_, bf16[128,1024]{1,0:T(8,128)(2,1)S(1)} %get-tuple-element.99.refs_4_.refs_0_), custom_call_target="tpu_custom_call" | custom-call | flops 30000001024 | bytes 1000 | tf_op jit(solution)/shard_map/up_grad/pallas_call | solution.py:36
  269.7 10.8 %attention_backward.3.refs_5_.refs_2_.refs_3_ = bf16[2,1024,768]{2,1,0:T(8,128)(2,1)} custom-call(s32[2]{0:T(128)S(1)} %copy-done.36, s32[2,4]{1,0:T(2,128)S(1)} %get-tuple-element.118.refs_1_, s32[4]{0:T(128)S(1)} %pad_add_fusion.1.refs_0_.refs_2_, bf16[2,1024,768]{2,1,0:T(8,128)(2,1)} %project.1.refs_3_, ...), custom_call_target="tpu_custom_call", output_to_operand_aliasing={{}: (12, {})} | custom-call | flops 30000001024 | bytes 1000 | tf_op jit(solution)/shard_map/attention_backward/pallas_call | solution.py:36
  283.3 8.5 %project_grad_pack.1.refs_4_ = bf16[8,144,768]{2,1,0:T(8,128)(2,1)} custom-call(s32[4]{0:T(128)S(1)} %copy-done.11, bf16[2,256,1024]{2,1,0:T(8,128)(2,1)S(1)} %copy-done.19, bf16[2,256,1024]{2,1,0:T(8,128)(2,1)} %collective-permute-done.refs_5_.refs_2_, bf16[2,256,1024]{2,1,0:T(8,128)(2,1)} %collective-permute-done.1.refs_6_.refs_3_, ...), custom_call_target="tpu_custom_call" | custom-call | flops 30000001024 | bytes 1000 | tf_op jit(solution)/shard_map/project_grad_pack/pallas_call | solution.py:36
  294.8 4.7 %hidden_grad.3.refs_4_ = bf16[2,2,256,1024]{3,2,1,0:T(8,128)(2,1)} custom-call(s32[4]{0:T(128)S(1)} %copy-done.12, bf16[1024,768]{1,0:T(8,128)(2,1)S(1)} %bitcast.85, bf16[2,1024,768]{2,1,0:T(8,128)(2,1)} %attention_backward.3.refs_5_.refs_2_.refs_3_, bf16[2,1024,768]{2,1,0:T(8,128)(2,1)} %attention_backward.3.refs_5_.refs_2_.refs_3_, ...), custom_call_target="tpu_custom_call" | custom-call | flops 30000001024 | bytes 1000 | tf_op jit(solution)/shard_map/hidden_grad/pallas_call | solution.py:36
  303.5 4.3 %up_grad.5 = bf16[1,1024,512]{2,1,0:T(8,128)(2,1)S(1)} custom-call(bf16[512,1024]{1,0:T(8,128)(2,1)} %bitcast.26.refs_0_, bf16[512,1024]{1,0:T(8,128)(2,1)S(1)} %copy-done.23, bf16[1024,512]{1,0:T(8,128)(2,1)} %copy-done.37, bf16[2,1024,512]{2,1,0:T(8,128)(2,1)} %collective-permute-done.24.refs_3_, bf16[1,1024,512]{2,1,0:T(8,128)(2,1)} %collective-permute-done.28.refs_4_, ...), custom_call_target="tpu_custom_call" | custom-call | flops 30000001024 | bytes 1000 | tf_op jit(solution)/shard_map/up_grad/pallas_call | solution.py:36
  308.5 5.8 %collective-permute-start.37 = (bf16[256,512]{1,0:T(8,128)(2,1)S(1)}, bf16[256,512]{1,0:T(8,128)(2,1)S(1)}, u32[]{:S(2)}, u32[]{:S(2)}) collective-permute-start(bf16[256,512]{1,0:T(8,128)(2,1)S(1)} %get-tuple-element.110), channel_id=1, source_target_pairs={{0,2},{2,4},{4,6},{6,0},{1,3},{3,5},{5,7},{7,1},{8,10},{10,12},{12... | collective-permute-start | bytes 786440 | tf_op jit(solution)/shard_map/ppermute | solution.py:1042
  318.7 7.8 %collective-permute-done.27.refs_3_.refs_4_ = bf16[2,2,256,1024]{3,2,1,0:T(8,128)(2,1)} collective-permute-done((bf16[2,2,256,1024]{3,2,1,0:T(8,128)(2,1)}, bf16[2,2,256,1024]{3,2,1,0:T(8,128)(2,1)}, u32[]{:S(2)}, u32[]{:S(2)}) %collective-permute-start.27) | collective-permute-done | bytes 2097184 | tf_op jit(solution)/shard_map/ppermute | solution.py:1021
  330.6 9.7 %collective-permute-done.38.refs_3_ = bf16[256,512]{1,0:T(8,128)(2,1)S(1)} collective-permute-done((bf16[256,512]{1,0:T(8,128)(2,1)S(1)}, bf16[256,512]{1,0:T(8,128)(2,1)S(1)}, u32[]{:S(2)}, u32[]{:S(2)}) %collective-permute-start.38) | collective-permute-done | bytes 262176 | tf_op jit(solution)/shard_map/ppermute | solution.py:1042
  350.7 4.7 %collective-permute-done.41.refs_2_ = bf16[2,128,512]{2,1,0:T(8,128)(2,1)S(1)} collective-permute-done((bf16[2,128,512]{2,1,0:T(8,128)(2,1)S(1)}, bf16[2,128,512]{2,1,0:T(8,128)(2,1)S(1)}, u32[]{:S(2)}, u32[]{:S(2)}) %collective-permute-start.41) | collective-permute-done | bytes 262176 | tf_op jit(solution)/shard_map/ppermute | solution.py:1021
  356.3 4.4 %hidden_grad.5 = f32[1,2,256,1024]{3,2,1,0:T(8,128)} custom-call(s32[4]{0:T(128)S(1)} %copy-done.12, bf16[1024,768]{1,0:T(8,128)(2,1)S(1)} %bitcast.87, bf16[2,1024,768]{2,1,0:T(8,128)(2,1)} %attention_backward.3.refs_5_.refs_2_.refs_3_, f32[2,256,1024]{2,1,0:T(8,128)} %get-tuple-element.100.refs_3_, ...), custom_call_target="tpu_custom_call" | custom-call | flops 30000001024 | bytes 1000 | tf_op jit(solution)/shard_map/hidden_grad/pallas_call | solution.py:36
  (302 shorter events, 120.3 us)
Async XLA Ops:
  7.2 53.9 %all-gather.9.cloned.1.call-start = ((), (), s32[]{:S(2)}) async-start(), calls=%async_computation.6 | async-start | bytes 1990656 | tf_op jit(solution)/shard_map/all_gather | solution.py:1129
  7.3 60.6 %collective-permute-start.1 = (bf16[2,256,1024]{2,1,0:T(8,128)(2,1)}, bf16[2,256,1024]{2,1,0:T(8,128)(2,1)}, u32[]{:S(2)}, u32[]{:S(2)}) collective-permute-start(bf16[2,256,1024]{2,1,0:T(8,128)(2,1)} %refs_1_.1), channel_id=1, source_target_pairs={{0,16},{1,9},{2,18},{3,11},{4,20},{5,13},{6,22},{7,15},{8,24},{9,1... | collective-permute-start | bytes 3145736 | tf_op jit(solution)/shard_map/ppermute | solution.py:1021
  10.3 23.4 %collective-permute-start = (bf16[2,256,1024]{2,1,0:T(8,128)(2,1)}, bf16[2,256,1024]{2,1,0:T(8,128)(2,1)}, u32[]{:S(2)}, u32[]{:S(2)}) collective-permute-start(bf16[2,256,1024]{2,1,0:T(8,128)(2,1)} %refs_1_.1), channel_id=1, source_target_pairs={{0,8},{1,17},{2,10},{3,19},{4,12},{5,21},{6,14},{7,23},{8,0},{9,25... | collective-permute-start | bytes 3145736 | tf_op jit(solution)/shard_map/ppermute | solution.py:1021
  15.1 97.6 %all-gather.7.cloned.1.call-start = ((), (), s32[]{:S(2)}) async-start(), calls=%async_computation.3 | async-start | bytes 1310720 | tf_op jit(solution)/shard_map/all_gather | solution.py:1131
  21.8 37.2 %collective-permute-start.5 = (bf16[256,512]{1,0:T(8,128)(2,1)S(1)}, bf16[256,512]{1,0:T(8,128)(2,1)S(1)}, u32[]{:S(2)}, u32[]{:S(2)}) collective-permute-start(bf16[256,512]{1,0:T(8,128)(2,1)S(1)} %pad_maximum_fusion.refs_1_), channel_id=1, source_target_pairs={{0,4},{2,6},{4,0},{6,2},{1,5},{3,7},{5,1},{7,3},{8,12},{10,14},{12... | collective-permute-start | bytes 786440 | tf_op jit(solution)/shard_map/ppermute | solution.py:1042
  21.8 37.2 %collective-permute-start.4 = (bf16[256,512]{1,0:T(8,128)(2,1)S(1)}, bf16[256,512]{1,0:T(8,128)(2,1)S(1)}, u32[]{:S(2)}, u32[]{:S(2)}) collective-permute-start(bf16[256,512]{1,0:T(8,128)(2,1)S(1)} %pad_maximum_fusion.refs_1_), channel_id=1, source_target_pairs={{0,2},{2,4},{4,6},{6,0},{1,3},{3,5},{5,7},{7,1},{8,10},{10,12},{12... | collective-permute-start | bytes 786440 | tf_op jit(solution)/shard_map/ppermute | solution.py:1042
  33.7 25.9 %collective-permute-start.2 = (bf16[2,256,1024]{2,1,0:T(8,128)(2,1)}, bf16[2,256,1024]{2,1,0:T(8,128)(2,1)}, u32[]{:S(2)}, u32[]{:S(2)}) collective-permute-start(bf16[2,256,1024]{2,1,0:T(8,128)(2,1)} %collective-permute-done.refs_5_.refs_2_), channel_id=1, source_target_pairs={{0,16},{1,9},{2,18},{3,11},{4,20},{5,13},{6,22},{7,15},{8,24},{9,1... | collective-permute-start | bytes 3145736 | tf_op jit(solution)/shard_map/ppermute | solution.py:1021
  60.7 41.1 %collective-permute-start.12 = (bf16[1024,512]{1,0:T(8,128)(2,1)}, bf16[1024,512]{1,0:T(8,128)(2,1)}, u32[]{:S(2)}, u32[]{:S(2)}) collective-permute-start(bf16[1024,512]{1,0:T(8,128)(2,1)} %hold.5.refs_6_.refs_2_.refs_10_), channel_id=1, source_target_pairs={{0,16},{1,9},{2,18},{3,11},{4,20},{5,13},{6,22},{7,15},{8,24},{9,1... | collective-permute-start | bytes 3145736 | tf_op jit(solution)/shard_map/ppermute | solution.py:1021
  61.1 38.9 %collective-permute-start.11 = (bf16[1024,512]{1,0:T(8,128)(2,1)}, bf16[1024,512]{1,0:T(8,128)(2,1)}, u32[]{:S(2)}, u32[]{:S(2)}) collective-permute-start(bf16[1024,512]{1,0:T(8,128)(2,1)} %hold.5.refs_6_.refs_2_.refs_10_), channel_id=1, source_target_pairs={{0,8},{1,17},{2,10},{3,19},{4,12},{5,21},{6,14},{7,23},{8,0},{9,25... | collective-permute-start | bytes 3145736 | tf_op jit(solution)/shard_map/ppermute | solution.py:1021
  63.4 59.9 %all-gather.5.cloned.1.call-start = ((), (), s32[]{:S(2)}) async-start(), calls=%async_computation.2 | async-start | bytes 2359296 | tf_op jit(solution)/shard_map/all_gather | solution.py:1132
  67.6 212.9 %reduce-scatter.3.cloned.1.call-start = ((), (), s32[]{:S(2)}) async-start(), calls=%async_computation.4 | async-start | bytes 2654208 | tf_op jit(solution)/shard_map/reduce_scatter | solution.py:1211
  100.0 33.9 %collective-permute-start.13 = (bf16[1024,512]{1,0:T(8,128)(2,1)}, bf16[1024,512]{1,0:T(8,128)(2,1)}, u32[]{:S(2)}, u32[]{:S(2)}) collective-permute-start(bf16[1024,512]{1,0:T(8,128)(2,1)} %collective-permute-done.11.refs_4_.refs_3_.refs_11_), channel_id=1, source_target_pairs={{0,16},{1,9},{2,18},{3,11},{4,20},{5,13},{6,22},{7,15},{8,24},{9,1... | collective-permute-start | bytes 3145736 | tf_op jit(solution)/shard_map/ppermute | solution.py:1021
  114.9 18.6 %collective-permute-start.14 = (bf16[512,1024]{1,0:T(8,128)(2,1)}, bf16[512,1024]{1,0:T(8,128)(2,1)}, u32[]{:S(2)}, u32[]{:S(2)}) collective-permute-start(bf16[512,1024]{1,0:T(8,128)(2,1)} %hold.8.refs_4_.refs_6_), channel_id=1, source_target_pairs={{0,8},{1,17},{2,10},{3,19},{4,12},{5,21},{6,14},{7,23},{8,0},{9,25... | collective-permute-start | bytes 3145736 | tf_op jit(solution)/shard_map/ppermute | solution.py:1021
  133.5 23.1 %collective-permute-start.16 = (bf16[512,1024]{1,0:T(8,128)(2,1)}, bf16[512,1024]{1,0:T(8,128)(2,1)S(1)}, u32[]{:S(2)}, u32[]{:S(2)}) collective-permute-start(bf16[512,1024]{1,0:T(8,128)(2,1)} %collective-permute-done.14.refs_10_.refs_5_.refs_7_), channel_id=1, source_target_pairs={{0,16},{1,9},{2,18},{3,11},{4,20},{5,13},{6,22},{7,15},{8,24},{9,1... | collective-permute-start | bytes 3145736 | tf_op jit(solution)/shard_map/ppermute | solution.py:1021
  184.4 34.1 %collective-permute-start.23 = (bf16[2,512,1024]{2,1,0:T(8,128)(2,1)}, bf16[2,512,1024]{2,1,0:T(8,128)(2,1)}, u32[]{:S(2)}, u32[]{:S(2)}) collective-permute-start(bf16[2,512,1024]{2,1,0:T(8,128)(2,1)} %down_grad.3.refs_0_), channel_id=1, source_target_pairs={{0,8},{1,17},{2,10},{3,19},{4,12},{5,21},{6,14},{7,23},{8,0},{9,25... | collective-permute-start | bytes 6291464 | tf_op jit(solution)/shard_map/ppermute | solution.py:1021
  214.9 19.8 %collective-permute-start.20 = (bf16[2,256,256]{2,1,0:T(8,128)(2,1)}, bf16[2,256,256]{2,1,0:T(8,128)(2,1)S(1)}, u32[]{:S(2)}, u32[]{:S(2)}) collective-permute-start(bf16[2,256,256]{2,1,0:T(8,128)(2,1)} %get-tuple-element.87), channel_id=1, source_target_pairs={{0,8},{1,17},{2,10},{3,19},{4,12},{5,21},{6,14},{7,23},{8,0},{9,25... | collective-permute-start | bytes 786440 | tf_op jit(solution)/shard_map/ppermute | solution.py:1038
  215.9 18.8 %collective-permute-start.21 = (bf16[2,256,256]{2,1,0:T(8,128)(2,1)}, bf16[2,256,256]{2,1,0:T(8,128)(2,1)}, u32[]{:S(2)}, u32[]{:S(2)}) collective-permute-start(bf16[2,256,256]{2,1,0:T(8,128)(2,1)} %get-tuple-element.88), channel_id=1, source_target_pairs={{0,16},{1,9},{2,18},{3,11},{4,20},{5,13},{6,22},{7,15},{8,24},{9,1... | collective-permute-start | bytes 786440 | tf_op jit(solution)/shard_map/ppermute | solution.py:1038
  217.0 17.7 %collective-permute-start.22 = (bf16[2,256,256]{2,1,0:T(8,128)(2,1)}, bf16[2,256,256]{2,1,0:T(8,128)(2,1)}, u32[]{:S(2)}, u32[]{:S(2)}) collective-permute-start(bf16[2,256,256]{2,1,0:T(8,128)(2,1)} %get-tuple-element.89), channel_id=1, source_target_pairs={{0,24},{1,25},{2,26},{3,27},{4,28},{5,29},{6,30},{7,31},{8,16},{9,... | collective-permute-start | bytes 786440 | tf_op jit(solution)/shard_map/ppermute | solution.py:1038
  223.6 28.0 %collective-permute-start.25 = (bf16[1,512,1024]{2,1,0:T(8,128)(2,1)}, bf16[1,512,1024]{2,1,0:T(8,128)(2,1)}, u32[]{:S(2)}, u32[]{:S(2)}) collective-permute-start(bf16[1,512,1024]{2,1,0:T(8,128)(2,1)} %down_grad.4.refs_4_), channel_id=1, source_target_pairs={{0,16},{1,9},{2,18},{3,11},{4,20},{5,13},{6,22},{7,15},{8,24},{9,1... | collective-permute-start | bytes 3145736 | tf_op jit(solution)/shard_map/ppermute | solution.py:1021
  230.7 33.1 %collective-permute-start.24 = (bf16[2,1024,512]{2,1,0:T(8,128)(2,1)}, bf16[2,1024,512]{2,1,0:T(8,128)(2,1)}, u32[]{:S(2)}, u32[]{:S(2)}) collective-permute-start(bf16[2,1024,512]{2,1,0:T(8,128)(2,1)} %up_grad.3.refs_7_), channel_id=1, source_target_pairs={{0,8},{1,17},{2,10},{3,19},{4,12},{5,21},{6,14},{7,23},{8,0},{9,25... | collective-permute-start | bytes 6291464 | tf_op jit(solution)/shard_map/ppermute | solution.py:1021
  234.6 126.1 %reduce-scatter.5.cloned.1.call-start = ((), (), s32[]{:S(2)}) async-start(), calls=%async_computation.5 | async-start | bytes 1990656 | tf_op jit(solution)/shard_map/reduce_scatter | solution.py:1233
  256.5 43.0 %collective-permute-start.29 = (bf16[128,1024]{1,0:T(8,128)(2,1)}, bf16[128,1024]{1,0:T(8,128)(2,1)}, u32[]{:S(2)}, u32[]{:S(2)}) collective-permute-start(bf16[128,1024]{1,0:T(8,128)(2,1)} %get-tuple-element.101), channel_id=1, source_target_pairs={{0,2},{2,4},{4,6},{6,0},{1,3},{3,5},{5,7},{7,1},{8,10},{10,12},{12... | collective-permute-start | bytes 786440 | tf_op jit(solution)/shard_map/ppermute | solution.py:1042
  257.4 43.3 %collective-permute-start.30 = (bf16[128,1024]{1,0:T(8,128)(2,1)}, bf16[128,1024]{1,0:T(8,128)(2,1)}, u32[]{:S(2)}, u32[]{:S(2)}) collective-permute-start(bf16[128,1024]{1,0:T(8,128)(2,1)} %get-tuple-element.102), channel_id=1, source_target_pairs={{0,4},{2,6},{4,0},{6,2},{1,5},{3,7},{5,1},{7,3},{8,12},{10,14},{12... | collective-permute-start | bytes 786440 | tf_op jit(solution)/shard_map/ppermute | solution.py:1042
  258.5 42.1 %collective-permute-start.31 = (bf16[128,1024]{1,0:T(8,128)(2,1)}, bf16[128,1024]{1,0:T(8,128)(2,1)}, u32[]{:S(2)}, u32[]{:S(2)}) collective-permute-start(bf16[128,1024]{1,0:T(8,128)(2,1)} %get-tuple-element.103), channel_id=1, source_target_pairs={{0,6},{2,0},{4,2},{6,4},{1,7},{3,1},{5,3},{7,5},{8,14},{10,8},{12,... | collective-permute-start | bytes 786440 | tf_op jit(solution)/shard_map/ppermute | solution.py:1042
  268.7 34.8 %collective-permute-start.28 = (bf16[1,1024,512]{2,1,0:T(8,128)(2,1)}, bf16[1,1024,512]{2,1,0:T(8,128)(2,1)}, u32[]{:S(2)}, u32[]{:S(2)}) collective-permute-start(bf16[1,1024,512]{2,1,0:T(8,128)(2,1)} %up_grad.4.refs_13_), channel_id=1, source_target_pairs={{0,16},{1,9},{2,18},{3,11},{4,20},{5,13},{6,22},{7,15},{8,24},{9,1... | collective-permute-start | bytes 3145736 | tf_op jit(solution)/shard_map/ppermute | solution.py:1021
  293.9 23.6 %collective-permute-start.36 = (bf16[144,1024]{1,0:T(8,128)(2,1)}, bf16[144,1024]{1,0:T(8,128)(2,1)}, u32[]{:S(2)}, u32[]{:S(2)}) collective-permute-start(bf16[144,1024]{1,0:T(8,128)(2,1)} %fusion.refs_5_), channel_id=1, source_target_pairs={{0,16},{1,9},{2,18},{3,11},{4,20},{5,13},{6,22},{7,15},{8,24},{9,1... | collective-permute-start | bytes 884744 | tf_op jit(solution)/shard_map/ppermute | solution.py:1021
  299.5 26.9 %collective-permute-start.27 = (bf16[2,2,256,1024]{3,2,1,0:T(8,128)(2,1)}, bf16[2,2,256,1024]{3,2,1,0:T(8,128)(2,1)}, u32[]{:S(2)}, u32[]{:S(2)}) collective-permute-start(bf16[2,2,256,1024]{3,2,1,0:T(8,128)(2,1)} %hidden_grad.3.refs_4_), channel_id=1, source_target_pairs={{0,8},{1,17},{2,10},{3,19},{4,12},{5,21},{6,14},{7,23},{8,0},{9,25... | collective-permute-start | bytes 6291464 | tf_op jit(solution)/shard_map/ppermute | solution.py:1021
  308.5 22.2 %collective-permute-start.37 = (bf16[256,512]{1,0:T(8,128)(2,1)S(1)}, bf16[256,512]{1,0:T(8,128)(2,1)S(1)}, u32[]{:S(2)}, u32[]{:S(2)}) collective-permute-start(bf16[256,512]{1,0:T(8,128)(2,1)S(1)} %get-tuple-element.110), channel_id=1, source_target_pairs={{0,2},{2,4},{4,6},{6,0},{1,3},{3,5},{5,7},{7,1},{8,10},{10,12},{12... | collective-permute-start | bytes 786440 | tf_op jit(solution)/shard_map/ppermute | solution.py:1042
  314.2 26.1 %collective-permute-start.38 = (bf16[256,512]{1,0:T(8,128)(2,1)S(1)}, bf16[256,512]{1,0:T(8,128)(2,1)S(1)}, u32[]{:S(2)}, u32[]{:S(2)}) collective-permute-start(bf16[256,512]{1,0:T(8,128)(2,1)S(1)} %get-tuple-element.111), channel_id=1, source_target_pairs={{0,4},{2,6},{4,0},{6,2},{1,5},{3,7},{5,1},{7,3},{8,12},{10,14},{12... | collective-permute-start | bytes 786440 | tf_op jit(solution)/shard_map/ppermute | solution.py:1042
  315.2 25.1 %collective-permute-start.39 = (bf16[256,512]{1,0:T(8,128)(2,1)S(1)}, bf16[256,512]{1,0:T(8,128)(2,1)S(1)}, u32[]{:S(2)}, u32[]{:S(2)}) collective-permute-start(bf16[256,512]{1,0:T(8,128)(2,1)S(1)} %get-tuple-element.112), channel_id=1, source_target_pairs={{0,6},{2,0},{4,2},{6,4},{1,7},{3,1},{5,3},{7,5},{8,14},{10,8},{12,... | collective-permute-start | bytes 786440 | tf_op jit(solution)/shard_map/ppermute | solution.py:1042
  329.4 26.9 %collective-permute-start.32 = (bf16[1,2,256,1024]{3,2,1,0:T(8,128)(2,1)S(1)}, bf16[1,2,256,1024]{3,2,1,0:T(8,128)(2,1)S(1)}, u32[]{:S(2)}, u32[]{:S(2)}) collective-permute-start(bf16[1,2,256,1024]{3,2,1,0:T(8,128)(2,1)S(1)} %hidden_grad.4.refs_5_), channel_id=1, source_target_pairs={{0,16},{1,9},{2,18},{3,11},{4,20},{5,13},{6,22},{7,15},{8,24},{9,1... | collective-permute-start | bytes 3145736 | tf_op jit(solution)/shard_map/ppermute | solution.py:1021
  346.5 21.7 %collective-permute-start.42 = (bf16[2,128,512]{2,1,0:T(8,128)(2,1)S(1)}, bf16[2,128,512]{2,1,0:T(8,128)(2,1)S(1)}, u32[]{:S(2)}, u32[]{:S(2)}) collective-permute-start(bf16[2,128,512]{2,1,0:T(8,128)(2,1)S(1)} %pair.1.refs_1_), channel_id=1, source_target_pairs={{0,16},{1,9},{2,18},{3,11},{4,20},{5,13},{6,22},{7,15},{8,24},{9,1... | collective-permute-start | bytes 786440 | tf_op jit(solution)/shard_map/ppermute | solution.py:1021
  (82 other events, 933.9 us)
Sparse Core Ops, SparseCore 0:
  15.2 44.7 all-gather.8
  63.5 28.9 all-gather.6
  94.7 28.5 all-gather.4
  234.7 40.5 reduce-scatter.2
  292.0 43.8 reduce-scatter.4

commit v2 on v1

--- a/solution.py
+++ b/solution.py
@@ -148,8 +148,9 @@
         for q in range(ranks):
             rows = pl.ds(pl.multiple_of(place_ref[q] * part, part), part)
             total = total + dot(refs[q][0], weight_ref[rows, :], 1, 0)
+        total = total.astype(jnp.bfloat16)
         sum_ref[0] = total
-        normed, _ = standardize(total)
+        normed, _ = standardize(wide(total))
         first = normed * vector_ref[GAIN_ONE : GAIN_ONE + 1, :] + vector_ref[SHIFT_ONE : SHIFT_ONE + 1, :]
         first_ref[0] = first.astype(jnp.bfloat16)
 
@@ -160,7 +161,7 @@
         (seqs,),
         [pl.BlockSpec((1, length, part), lambda b, p: (b, 0, 0))] * ranks + [fixed(weight), tokens, fixed(vectors)],
         [tokens, tokens],
-        [kind_of(hidden.shape, jnp.float32), kind_of(hidden.shape)],
+        [kind_of(hidden.shape), kind_of(hidden.shape)],
         [*contexts, weight, hidden, vectors],
         prefetch=(places,),
         waits=waits,
@@ -176,8 +177,9 @@
 
     def kernel(own_ref, other_ref, *refs):
         def body(tokens):
+            uppers = [dot(tokens, refs[q][...], 1, 0) for q in range(blocks)]
             for q in range(blocks):
-                upper = dot(tokens, refs[q][...], 1, 0) + refs[blocks + q][...]
+                upper = uppers[q] + refs[blocks + q][...]
                 tail = 0.5 * (1.0 + lax.erf(upper * 0.7071067811865476))
                 refs[2 * blocks + q][...] = (upper * tail).astype(jnp.bfloat16)
                 bell = jnp.exp(-0.5 * upper * upper) * 0.3989422804014327
@@ -235,7 +237,7 @@
 def norm_two(mixed, mixed_other, sums_one, vectors, out_grad, keep):
     seqs, length, width = sums_one.shape
 
-    def kernel(mixed_ref, other_ref, sum_ref, vector_ref, grad_ref, keep_ref, out_ref, dsum_ref, dmixed_ref, total_ref):
+    def kernel(mixed_ref, other_ref, sum_ref, vector_ref, grad_ref, keep_ref, out_ref, dmixed_ref, total_ref):
         @pl.when(pl.program_id(0) == 0)
         def _():
             total_ref[...] = jnp.zeros_like(total_ref)
@@ -243,15 +245,13 @@
         def vector(i):
             return vector_ref[i : i + 1, :]
 
-        normed, _ = standardize(sum_ref[0])
+        normed, _ = standardize(wide(sum_ref[0]))
         first = normed * vector(GAIN_ONE) + vector(SHIFT_ONE)
-        mixed = mixed_ref[0] + wide(other_ref[0]) + vector(DOWN_BIAS)
+        mixed = wide(mixed_ref[0]) + wide(other_ref[0]) + vector(DOWN_BIAS)
         normed, inverse = standardize(first + mixed)
         out_ref[0] = (normed * vector(GAIN_TWO) + vector(SHIFT_TWO)).astype(jnp.bfloat16)
         cot = wide(grad_ref[0]) * keep_ref[0]
-        dsum = standardize_back(cot, normed, inverse, vector(GAIN_TWO))
-        dsum_ref[0] = dsum
-        dmixed = dsum.astype(jnp.bfloat16)
+        dmixed = standardize_back(cot, normed, inverse, vector(GAIN_TWO)).astype(jnp.bfloat16)
         dmixed_ref[0] = dmixed
         total_ref[0:1, :] += column_sum(wide(dmixed))
         total_ref[1:2, :] += column_sum(cot * normed)
@@ -264,8 +264,8 @@
         "norm_two",
         (seqs,),
         [tokens, tokens, tokens, fixed(vectors), tokens, pl.BlockSpec((1, length, 1), lambda b: (b, 0, 0))],
-        [tokens, tokens, tokens, pl.BlockSpec((8, width), lambda b: (0, 0))],
-        [kind_of(shape), kind_of(shape, jnp.float32), kind_of(shape), kind_of((8, width), jnp.float32)],
+        [tokens, tokens, pl.BlockSpec((8, width), lambda b: (0, 0))],
+        [kind_of(shape), kind_of(shape), kind_of((8, width), jnp.float32)],
         [mixed.reshape(shape), mixed_other.reshape(shape), sums_one, vectors, out_grad, keep],
     )
 
@@ -287,12 +287,14 @@
             total_ref[...] = jnp.zeros_like(total_ref)
 
         def body(grad):
+            back = [dot(grad, down_refs[q][...], 1, 1) for q in range(blocks)]
             total = 0.0
             for q in range(blocks):
-                upper = (dot(grad, down_refs[q][...], 1, 1) * wide(slope_refs[q][...])).astype(jnp.bfloat16)
-                upper_refs[q][...] = upper
-                total_ref[q : q + 1, :] += column_sum(wide(upper))
-                total = total + dot(upper, up_refs[q][...], 1, 1)
+                upper = back[q] * wide(slope_refs[q][...])
+                total_ref[q : q + 1, :] += column_sum(upper)
+                upper_refs[q][...] = upper.astype(jnp.bfloat16)
+            for q in range(blocks):
+                total = total + dot(upper_refs[q][...], up_refs[q][...], 1, 1)
             return total
 
         @pl.when(step < half)
@@ -301,7 +303,7 @@
 
         @pl.when(step >= half)
         def _():
-            here_ref[...] = body(own_ref[...])
+            here_ref[...] = body(own_ref[...]).astype(jnp.bfloat16)
 
     def early(i):
         return (jnp.minimum(i, half - 1), 0)
@@ -328,7 +330,7 @@
         [kind_of((2 * count, units))] * blocks
         + [
             kind_of((max(8, blocks), units), jnp.float32),
-            kind_of((count, width), jnp.float32),
+            kind_of((count, width)),
             kind_of((count, width)),
         ],
         [own, other, *slopes, *arrays(downs), *arrays(ups)],
@@ -396,24 +398,23 @@
     )
 
 
-def norm_one_back(places, dfirst, dfirst_other, dsum_two, sums_one, vectors, weight, part, waits=()):
+def norm_one_back(places, dfirst, dfirst_other, dmixed, sums_one, vectors, weight, part, waits=()):
     seqs, length, width = sums_one.shape
     ranks = width // part
 
-    def kernel(place_ref, own_ref, other_ref, dsum_ref, sum_ref, vector_ref, weight_ref, *outs):
+    def kernel(place_ref, own_ref, other_ref, dmixed_ref, sum_ref, vector_ref, weight_ref, *outs):
         @pl.when(pl.program_id(0) == 0)
         def _():
             outs[-1][...] = jnp.zeros_like(outs[-1])
 
-        upstream = dsum_ref[0] + own_ref[0] + wide(other_ref[0])
-        normed, inverse = standardize(sum_ref[0])
+        upstream = wide(dmixed_ref[0]) + wide(own_ref[0]) + wide(other_ref[0])
+        normed, inverse = standardize(wide(sum_ref[0]))
         dsum = standardize_back(upstream, normed, inverse, vector_ref[GAIN_ONE : GAIN_ONE + 1, :])
-        outs[0][0] = dsum
         dbranch = dsum.astype(jnp.bfloat16)
-        outs[1][0] = dbranch
+        outs[0][0] = dbranch
         for q in range(ranks):
             rows = pl.ds(pl.multiple_of(place_ref[q] * part, part), part)
-            outs[2 + q][0] = dot(dbranch, weight_ref[rows, :], 1, 1).astype(jnp.bfloat16)
+            outs[1 + q][0] = dot(dbranch, weight_ref[rows, :], 1, 1).astype(jnp.bfloat16)
         outs[-1][0:1, :] += column_sum(wide(dbranch))
         outs[-1][1:2, :] += column_sum(upstream * normed)
         outs[-1][2:3, :] += column_sum(upstream)
@@ -425,17 +426,17 @@
         "norm_one_back",
         (seqs,),
         [tokens, tokens, tokens, tokens, fixed(vectors), fixed(weight)],
-        [tokens, tokens]
+        [tokens]
         + [pl.BlockSpec((1, length, part), lambda b, p: (b, 0, 0))] * ranks
         + [pl.BlockSpec((8, width), lambda b, p: (0, 0))],
-        [kind_of(shape, jnp.float32), kind_of(shape)]
+        [kind_of(shape)]
         + [kind_of((seqs, length, part))] * ranks
         + [kind_of((8, width), jnp.float32)],
-        [dfirst.reshape(shape), dfirst_other.reshape(shape), dsum_two, sums_one, vectors, weight],
+        [dfirst.reshape(shape), dfirst_other.reshape(shape), dmixed.reshape(shape), sums_one, vectors, weight],
         prefetch=(places,),
         waits=waits,
     )
-    return outs[0], outs[1], list(outs[2 : 2 + ranks]), outs[-1]
+    return outs[0], list(outs[1 : 1 + ranks]), outs[-1]
 
 
 def out_grad_pack(places, contexts, dbranch, small, owners, waits=()):
@@ -497,7 +498,7 @@
         [weight] + [dqkv] * blocks + [a.array for _, a in spread],
         prefetch=(places,),
         waits=waits,
-        cost=10,
+        cost=2,
     )
 
 
@@ -538,7 +539,7 @@
         prefetch=(places,),
         scratch=(pltpu.VMEM((extra, out_width), jnp.float32),),
         waits=waits,
-        cost=10,
+        cost=2,
     )
 
 
@@ -566,7 +567,7 @@
         [kind_of(shape, jnp.float32)] * 3 + [kind_of(below, jnp.float32)] * 3,
         arrays(blocks),
         prefetch=(places,),
-        cost=10,
+        cost=2,
     )
 
 
@@ -592,7 +593,7 @@
         arrays(blocks),
         prefetch=(places,),
         waits=waits,
-        cost=10,
+        cost=2,
     )
 
 
@@ -615,7 +616,7 @@
         arrays(blocks),
         prefetch=(places,),
         waits=waits,
-        cost=10,
+        cost=2,
     )
 
 
@@ -1165,8 +1166,8 @@
         first_low, first_other, up_weights, upper_bias, arrays(down_weights[1:2])
     )
     mixed_other = down_forward(actives, down_weights, count, count, jnp.bfloat16)
-    mixed = down_forward(actives, down_weights, 0, count, jnp.float32, (mixed_other,))
-    layer_out, dsum_two, dmixed, totals_two = norm_two(mixed, swap(mixed_other), sums_one, vectors, out_grad, keep)
+    mixed = down_forward(actives, down_weights, 0, count, jnp.bfloat16, (mixed_other,))
+    layer_out, dmixed, totals_two = norm_two(mixed, swap(mixed_other), sums_one, vectors, out_grad, keep)
 
     dmixed = dmixed.reshape(count, width)
     dmixed_other = swap(dmixed)
@@ -1177,8 +1178,8 @@
         dmixed, dmixed_other, slopes, down_weights, up_weights, (tick(down_sent),)
     )
     dfirst_other = swap(dfirst_other)
-    dsum_one, dbranch, dcontexts, totals_one = norm_one_back(
-        places, dfirst, dfirst_other, dsum_two, sums_one, vectors, output_weight, head_width, (tick(duppers[0], cost=10),)
+    dbranch, dcontexts, totals_one = norm_one_back(
+        places, dfirst, dfirst_other, dmixed, sums_one, vectors, output_weight, head_width, (tick(duppers[0], cost=10),)
     )
     dcontexts = ring.exchange(dcontexts)
 
@@ -1227,33 +1228,34 @@
         return [pieces[0]] + [ring.shift(pieces[d], d) for d in range(1, chips)]
 
     def hidden_made(turn, addends, waits=()):
-        return hidden_grad(places, dqkv, qkv_weight, length, turn, addends, jnp.bfloat16, waits or (up_pieces[0],))
-
-    qkv_pack = project_grad_pack(places, hidden, dqkv, owners, EXTRA, (out_shard,))
+        return hidden_grad(places, dqkv, qkv_weight, length, turn, addends, jnp.bfloat16, waits or (up_pair,))
+
+    down_shard = total_rows(shifted(down_pieces), (dqkv, up_came[-1].array))
+    down_parts = ring.gather(down_shard)
+    up_own = up_grad([duppers[0]], first_low, first_other, [up_came], (down_shard,))[0]
+    up_pieces = split(ahead, up_own, 2 * rows)
+    hidden_sent = hidden_made(odd, none, (up_pieces[0], *arrays(down_parts[1:2])))
+    qkv_pack = project_grad_pack(
+        places, hidden, dqkv, owners, EXTRA, (hidden_sent, out_shard, *arrays(down_parts[2:]))
+    )
     qkv_shard = lax.psum_scatter(qkv_pack.reshape(-1, out_width), ROWS, scatter_dimension=0, tiled=True)
     out_sum = [wide(out_shard)]
     for k in range(ring.count):
         out_sent = low(out_sum[-1])
         out_sum.append(out_sum[-1] + wide(ring.hop(out_sent, k)))
-    hidden_sent = hidden_made(odd, none, (qkv_pack, out_sent))
-    down_shard = total_rows(shifted(down_pieces), (hidden_sent,))
-    up_own = up_grad([duppers[0]], first_low, first_other, [up_came], (down_shard,))[0]
-    up_pieces = split(ahead, up_own, 2 * rows)
+    keep_part, take_part = total_halves(core_index, shifted(up_pieces), (qkv_pack,))
+    down_weight_grad = lay_rows(places, down_parts, (keep_part,))
+    up_pair = pair(core_index, keep_part, swap(take_part), (down_weight_grad,))
     hidden_came, hidden_hop = spread(hidden_made, hidden_sent)
-    keep_part, take_part = total_halves(core_index, shifted(up_pieces), (hidden_hop,))
-    down_shard = hold(down_shard, (keep_part,))
-    down_parts = ring.gather(down_shard)
-    up_pair = pair(core_index, keep_part, swap(take_part), (down_shard,))
     input_grad = hidden_grad(
-        places, dqkv, qkv_weight, length, [0], [[View(dsum_one)] + hidden_came], jnp.float32
+        places, dqkv, qkv_weight, length, [0], [[View(dbranch)] + hidden_came], jnp.float32
     )[0]
 
     up_parts = ring.gather(up_pair)
     qkv_parts = ring.gather(qkv_shard)
     out_pack = out_sum[-1]
-    down_weight_grad = lay_rows(places, down_parts, (input_grad,))
     if part % 128 == 0:
-        up_weight_grad = lay_up(places, up_parts, chips, part, (input_grad,))
+        up_weight_grad = lay_up(places, up_parts, chips, part, (hidden_hop,))
     else:
         up_weight_grad = wide(put([b.value()[None] for b in up_parts], ring, 0))
         up_weight_grad = (

time: 391 us -> 381 us (0.974)
  Pallas kernels: 175 us -> 170 us
    ppermute x9, waiting for transfers between devices: 33.2 us -> 27.2 us  [shift(): lax.ppermute(block, 'z', [(z, (z + d) % self.chips) for z in range(self.c...]
    ppermute x26, waiting for transfers between devices: 43.4 us -> 48.9 us  [hop(): return lax.ppermute(block, AXES, pairs)]
    pallas_call x39 -> x38, Pallas kernels: 175 us -> 170 us  [run(): pl.pallas_call(waiting, grid_spec=pltpu.PrefetchScalarGridSpec(num_scalar...]
    unnamed x126 -> x116, local copies, waits for them, and re-layouts: 23.6 us -> 23.8 us
  transfers between devices with their start and end apart: 52 -> 52, of which waited for: 17 -> 18; matrix products, arithmetic and copies ran while one was open for 4% -> 4% of each run, Pallas kernels for 41% -> 41%
where the time goes in v2:
time: 381 us; the launch traced here: 377 us
  Pallas kernels  170 us (45%)
  waiting for transfers between devices  96.7 us (25%)
  starting transfers between devices  56.9 us (15%)
  local copies, waits for them, and re-layouts  34.7 us (9%)
  between operations  14.8 us (4%)
  other arithmetic  4.08 us (1%)
    pallas_call x38, Pallas kernels, run(): pl.pallas_call(waiting, grid_spec=pltpu.PrefetchScalarGridSpec(num_scalar...  170 us
    ppermute x26, waiting for transfers between devices, hop(): return lax.ppermute(block, AXES, pairs)  48.9 us
    ppermute x26, starting transfers between devices, hop(): return lax.ppermute(block, AXES, pairs)  30.9 us
    ppermute x9, waiting for transfers between devices, shift(): lax.ppermute(block, 'z', [(z, (z + d) % self.chips) for z in range(self.c...  27.2 us
    unnamed x116, local copies, waits for them, and re-layouts  23.8 us
    ppermute x9, starting transfers between devices, shift(): lax.ppermute(block, 'z', [(z, (z + d) % self.chips) for z in range(self.c...  18 us
    ppermute x6, waiting for transfers between devices, exchange(): out.append(lax.ppermute(blocks[q], AXES, pairs))  10.8 us
  transfers between devices with their start and end apart: 52, of which 18 were waited for; matrix products, arithmetic and copies ran while one was open for 4% of the time, Pallas kernels for 41%

profile of v2, /device:TPU:0, one launch (start us, length us, event | category | flops | bytes accessed | tf_op | source)
XLA Modules:
  0.0 377.2 jit_solution(1403184395243808379)
XLA Ops:
  18.1 3.7 collective-permute-start.6
  23.2 10.5 %collective-permute-done.refs_5_.refs_2_ = bf16[2,256,1024]{2,1,0:T(8,128)(2,1)} collective-permute-done((bf16[2,256,1024]{2,1,0:T(8,128)(2,1)}, bf16[2,256,1024]{2,1,0:T(8,128)(2,1)}, u32[]{:S(2)}, u32[]{:S(2)}) %collective-permute-start) | collective-permute-done | bytes 1048608 | tf_op jit(solution)/shard_map/ppermute | solution.py:1022
  35.5 23.5 %collective-permute-done.5.refs_3_ = bf16[256,512]{1,0:T(8,128)(2,1)S(1)} collective-permute-done((bf16[256,512]{1,0:T(8,128)(2,1)S(1)}, bf16[256,512]{1,0:T(8,128)(2,1)S(1)}, u32[]{:S(2)}, u32[]{:S(2)}) %collective-permute-start.5) | collective-permute-done | bytes 262176 | tf_op jit(solution)/shard_map/ppermute | solution.py:1043
  69.0 10.0 %project.1.refs_3_ = bf16[2,1024,768]{2,1,0:T(8,128)(2,1)} custom-call(s32[4]{0:T(128)S(1)} %pad_add_fusion.1.refs_0_.refs_2_, bf16[1024,768]{1,0:T(8,128)(2,1)} %bitcast.84, f32[1,768]{1,0:T(1,128)S(1)} %broadcast_in_dim.133.refs_2_, f32[1,768]{1,0:T(1,128)S(1)} %compare_select_fusion.refs_3_, bf16[2,256,1024]{2,1,0:T(8,128)(2,1)S(1)} %copy-done.10, ...), custom_call_target="tpu_custom_call" | custom-call | flops 30000001024 | bytes 1000 | tf_op jit(solution)/shard_map/project/pallas_call | solution.py:36
  78.9 16.2 %attention_forward.1 = (bf16[2,1024,256]{2,1,0:T(8,128)(2,1)S(1)}, f32[2,4,1024]{2,1,0:T(4,128)S(1)}, bf16[2,256,256]{2,1,0:T(8,128)(2,1)S(1)}, bf16[2,256,256]{...) custom-call(s32[2]{0:T(128)S(1)} %select_select_fusion.refs_0_, ...), custom_call_target="tpu_custom_call" | custom-call | flops 299999985664 | bytes 1000 | tf_op jit(solution)/shard_map/attention_forward/pallas_call | solution.py:36
  101.7 3.7 collective-permute-done.7.refs_2_.refs_1_
  105.9 6.6 %collective-permute-done.9.refs_4_.refs_3_ = bf16[2,256,256]{2,1,0:T(8,128)(2,1)S(1)} collective-permute-done((bf16[2,256,256]{2,1,0:T(8,128)(2,1)S(1)}, bf16[2,256,256]{2,1,0:T(8,128)(2,1)S(1)}, u32[]{:S(2)}, u32[]{:S(2)}) %collective-permute-start.9) | collective-permute-done | bytes 262176 | tf_op jit(solution)/shard_map/ppermute | solution.py:1039
  116.5 6.6 %all-gather.5.cloned.1.call-done.refs_5_.refs_6_ = bf16[1024,1024]{1,0:T(8,128)(2,1)} async-done(((bf16[128,1024]{1,0:T(8,128)(2,1)}), bf16[1024,1024]{1,0:T(8,128)(2,1)}) %all-gather.5.cloned.1.call-update) | async-done | bytes 2097168 | tf_op jit(solution)/shard_map/all_gather | solution.py:1133
  123.2 4.5 %out_norm.1 = (bf16[2,256,1024]{2,1,0:T(8,128)(2,1)S(1)}, bf16[2,256,1024]{2,1,0:T(8,128)(2,1)S(1)}) custom-call(s32[4]{0:T(128)S(1)} %pad_add_fusion.1.refs_0_.refs_2_, bf16[2,256,256]{2,1,0:T(8,128)(2,1)S(1)} %get-tuple-element.64.refs_1_, bf16[2,256,256]{2,1,0:T(8,128)(2,1)S(1)} %collective-permute-done.7.refs_2_.refs_1_, ...), custom_call_target="tpu_custom_call" | custom-call | flops 30000001024 | bytes 1000 | tf_op jit(solution)/shard_map/out_norm/pallas_call | solution.py:36
  133.8 11.0 %up_forward.1 = (bf16[1024,512]{1,0:T(8,128)(2,1)S(1)}, bf16[1024,512]{1,0:T(8,128)(2,1)S(1)}, bf16[1024,512]{1,0:T(8,128)(2,1)S(1)}, bf16[1024,512]{1,0:T(8,128...) custom-call(bf16[512,1024]{1,0:T(8,128)(2,1)} %bitcast.96, ...), custom_call_target="tpu_custom_call" | custom-call | flops 30000001024 | bytes 1000 | tf_op jit(solution)/shard_map/up_forward/pallas_call | solution.py:36
  145.9 10.9 %collective-permute-done.16.refs_7_.refs_9_ = bf16[512,1024]{1,0:T(8,128)(2,1)S(1)} collective-permute-done((bf16[512,1024]{1,0:T(8,128)(2,1)}, bf16[512,1024]{1,0:T(8,128)(2,1)S(1)}, u32[]{:S(2)}, u32[]{:S(2)}) %collective-permute-start.16) | collective-permute-done | bytes 1048608 | tf_op jit(solution)/shard_map/ppermute | solution.py:1022
  157.8 4.9 %down_forward.2.refs_8_ = bf16[512,1024]{1,0:T(8,128)(2,1)S(1)} custom-call(bf16[1024,512]{1,0:T(8,128)(2,1)S(1)} %get-tuple-element.69.refs_0_.refs_2_, bf16[1024,512]{1,0:T(8,128)(2,1)S(1)} %get-tuple-element.70.refs_1_.refs_2_, bf16[1024,512]{1,0:T(8,128)(2,1)} %copy-done.43, bf16[1024,512]{1,0:T(8,128)(2,1)} %get-tuple-element.72.refs_3_, ...), custom_call_target="tpu_custom_call" | custom-call | flops 30000001024 | bytes 1000 | tf_op jit(solution)/shard_map/down_forward/pallas_call | solution.py:36
  163.7 4.9 %down_forward.3 = bf16[512,1024]{1,0:T(8,128)(2,1)S(1)} custom-call(bf16[1024,512]{1,0:T(8,128)(2,1)S(1)} %get-tuple-element.69.refs_0_.refs_2_, bf16[1024,512]{1,0:T(8,128)(2,1)S(1)} %get-tuple-element.70.refs_1_.refs_2_, bf16[1024,512]{1,0:T(8,128)(2,1)} %copy-done.43, bf16[1024,512]{1,0:T(8,128)(2,1)} %get-tuple-element.72.refs_3_, ...), custom_call_target="tpu_custom_call" | custom-call | flops 30000001024 | bytes 1000 | tf_op jit(solution)/shard_map/down_forward/pallas_call | solution.py:36
  168.6 4.8 %norm_two.1 = (bf16[2,256,1024]{2,1,0:T(8,128)(2,1)}, bf16[2,256,1024]{2,1,0:T(8,128)(2,1)S(1)}, f32[8,1024]{1,0:T(8,128)S(1)}) custom-call(bf16[2,256,1024]{2,1,0:T(8,128)(2,1)S(1)} %bitcast.107, bf16[2,256,1024]{2,1,0:T(8,128)(2,1)S(1)} %bitcast.105, bf16[2,256,1024]{2,1,0:T(8,128)(2,1)} %copy-done.46, f32[16,1024]{1,0:T(8,128)S(1)} %bitcast.93, ...), custom_call_target="tpu_custom_call" | custom-call | flops 30000001024 | bytes 1000 | tf_op jit(solution)/shard_map/norm_two/pallas_call | solution.py:36
  177.4 5.0 %down_grad.3.refs_0_ = bf16[2,512,1024]{2,1,0:T(8,128)(2,1)} custom-call(bf16[512,1024]{1,0:T(8,128)(2,1)S(1)} %bitcast.101, bf16[512,1024]{1,0:T(8,128)(2,1)} %collective-permute-done.18.refs_1_, bf16[1024,512]{1,0:T(8,128)(2,1)S(1)} %copy-done.45, bf16[1024,512]{1,0:T(8,128)(2,1)} %get-tuple-element.72.refs_3_), custom_call_target="tpu_custom_call" | custom-call | flops 30000001024 | bytes 1000 | tf_op jit(solution)/shard_map/down_grad/pallas_call | solution.py:36
  183.8 15.6 %feed_forward_back.1 = (bf16[1024,512]{1,0:T(8,128)(2,1)S(1)}, bf16[1024,512]{1,0:T(8,128)(2,1)S(1)}, bf16[1024,512]{1,0:T(8,128)(2,1)S(1)}, bf16[1024,512]{1,0:...) custom-call(bf16[512,1024]{1,0:T(8,128)(2,1)} %bitcast.102, ...), custom_call_target="tpu_custom_call" | custom-call | flops 30000001024 | bytes 1000 | tf_op jit(solution)/shard_map/feed_forward_back/pallas_call | solution.py:36
  204.5 6.6 %norm_one_back.1 = (bf16[2,256,1024]{2,1,0:T(8,128)(2,1)S(1)}, bf16[2,256,256]{2,1,0:T(8,128)(2,1)S(1)}, bf16[2,256,256]{2,1,0:T(8,128)(2,1)}, bf16[2,256,256]{2...) custom-call(s32[4]{0:T(128)S(1)} %pad_add_fusion.1.refs_0_.refs_2_, ...), custom_call_target="tpu_custom_call" | custom-call | flops 30000001024 | bytes 1000 | tf_op jit(solution)/shard_map/norm_one_back/pallas_call | solution.py:36
  216.6 3.9 %down_grad.4.refs_4_ = bf16[1,512,1024]{2,1,0:T(8,128)(2,1)} custom-call(bf16[512,1024]{1,0:T(8,128)(2,1)S(1)} %bitcast.103, bf16[512,1024]{1,0:T(8,128)(2,1)} %collective-permute-done.18.refs_1_, bf16[1024,512]{1,0:T(8,128)(2,1)} %copy-done.43, bf16[2,512,1024]{2,1,0:T(8,128)(2,1)} %collective-permute-done.23.refs_3_, f32[8,128]{1,0:T(8,128)S(1)} %tick.5.refs_4_), custom_call_target="tpu_custom_call" | custom-call | flops 30000001024 | bytes 1000 | tf_op jit(solution)/shard_map/down_grad/pallas_call | solution.py:36
  221.9 5.7 %up_grad.3.refs_7_ = bf16[2,1024,512]{2,1,0:T(8,128)(2,1)} custom-call(bf16[512,1024]{1,0:T(8,128)(2,1)S(1)} %bitcast.97, bf16[512,1024]{1,0:T(8,128)(2,1)} %collective-permute-done.10.refs_1_, bf16[1024,512]{1,0:T(8,128)(2,1)S(1)} %copy-done.38, bf16[1024,512]{1,0:T(8,128)(2,1)} %get-tuple-element.94.refs_3_, bf16[1,512,1024]{2,1,0:T(8,128)(2,1)} %down_grad.4.refs_4_), custom_call_target="tpu_custom_call" | custom-call | flops 30000001024 | bytes 1000 | tf_op jit(solution)/shard_map/up_grad/pallas_call | solution.py:36
  233.7 14.7 %attention_backward.2.refs_5_.refs_12_ = bf16[2,1024,768]{2,1,0:T(8,128)(2,1)} custom-call(s32[2]{0:T(128)S(1)} %copy-done.30, s32[2,4]{1,0:T(2,128)S(1)} %get-tuple-element.114.refs_1_, s32[4]{0:T(128)S(1)} %pad_add_fusion.1.refs_0_.refs_2_, bf16[2,1024,768]{2,1,0:T(8,128)(2,1)} %project.1.refs_3_, bf16[2,256,256]{2,1,0:T(8,128)(2,1)S(1)} %copy-done.48, ...), custom_call_target="tpu_custom_call" | custom-call | flops 30000001024 | bytes 1000 | tf_op jit(solution)/shard_map/attention_backward/pallas_call | solution.py:36
  260.7 4.1 %up_grad.4.refs_13_ = bf16[1,1024,512]{2,1,0:T(8,128)(2,1)S(1)} custom-call(bf16[512,1024]{1,0:T(8,128)(2,1)S(1)} %bitcast.98, bf16[512,1024]{1,0:T(8,128)(2,1)} %collective-permute-done.10.refs_1_, bf16[1024,512]{1,0:T(8,128)(2,1)} %copy-done.36, bf16[2,1024,512]{2,1,0:T(8,128)(2,1)} %collective-permute-done.24.refs_3_, ...), custom_call_target="tpu_custom_call" | custom-call | flops 30000001024 | bytes 1000 | tf_op jit(solution)/shard_map/up_grad/pallas_call | solution.py:36
  265.8 10.5 %attention_backward.3.refs_4_.refs_2_.refs_3_.refs_5_ = bf16[2,1024,768]{2,1,0:T(8,128)(2,1)} custom-call(s32[2]{0:T(128)S(1)} %copy-done.30, s32[2,4]{1,0:T(2,128)S(1)} %get-tuple-element.114.refs_1_, s32[4]{0:T(128)S(1)} %pad_add_fusion.1.refs_0_.refs_2_, bf16[2,1024,768]{2,1,0:T(8,128)(2,1)} %project.1.refs_3_, ...), custom_call_target="tpu_custom_call", output_to_operand_aliasing={{}: (12, {})} | custom-call | flops 30000001024 | bytes 1000 | tf_op jit(solution)/shard_map/attention_backward/pallas_call | solution.py:36
  276.3 3.8 collective-permute-done.28.refs_2_
  283.8 4.3 %up_grad.5 = bf16[1,1024,512]{2,1,0:T(8,128)(2,1)S(1)} custom-call(bf16[512,1024]{1,0:T(8,128)(2,1)S(1)} %bitcast.99, bf16[512,1024]{1,0:T(8,128)(2,1)} %collective-permute-done.10.refs_1_, bf16[1024,512]{1,0:T(8,128)(2,1)} %copy-done.35, bf16[2,1024,512]{2,1,0:T(8,128)(2,1)} %collective-permute-done.24.refs_3_, bf16[1,1024,512]{2,1,0:T(8,128)(2,1)} %copy-done.18, ...), custom_call_target="tpu_custom_call" | custom-call | flops 30000001024 | bytes 1000 | tf_op jit(solution)/shard_map/up_grad/pallas_call | solution.py:36
  289.6 5.8 %collective-permute-start.32 = (bf16[256,512]{1,0:T(8,128)(2,1)}, bf16[256,512]{1,0:T(8,128)(2,1)S(1)}, u32[]{:S(2)}, u32[]{:S(2)}) collective-permute-start(bf16[256,512]{1,0:T(8,128)(2,1)} %get-tuple-element.101), channel_id=1, source_target_pairs={{0,2},{2,4},{4,6},{6,0},{1,3},{3,5},{5,7},{7,1},{8,10},{10,12},{12... | collective-permute-start | bytes 786440 | tf_op jit(solution)/shard_map/ppermute | solution.py:1043
  298.7 4.7 %hidden_grad.3.refs_6_ = bf16[2,2,256,1024]{3,2,1,0:T(8,128)(2,1)} custom-call(s32[4]{0:T(128)S(1)} %pad_add_fusion.1.refs_0_.refs_2_, bf16[1024,768]{1,0:T(8,128)(2,1)S(1)} %bitcast.85, bf16[2,1024,768]{2,1,0:T(8,128)(2,1)} %attention_backward.3.refs_4_.refs_2_.refs_3_.refs_5_, bf16[2,1024,768]{2,1,0:T(8,128)(2,1)} %attention_backward.3.refs_4_.refs_2_.refs_3_.refs_5_, ...), custom_call_target="tpu_custom_call" | custom-call | flops 6000000000 | bytes 1000 | tf_op jit(solution)/shard_map/hidden_grad/pallas_call | solution.py:36
  305.8 8.5 %project_grad_pack.1.refs_5_ = bf16[8,144,768]{2,1,0:T(8,128)(2,1)} custom-call(s32[4]{0:T(128)S(1)} %pad_add_fusion.1.refs_0_.refs_2_, bf16[2,256,1024]{2,1,0:T(8,128)(2,1)S(1)} %copy-done.11, bf16[2,256,1024]{2,1,0:T(8,128)(2,1)} %collective-permute-done.refs_5_.refs_2_, bf16[2,256,1024]{2,1,0:T(8,128)(2,1)} %collective-permute-done.1.refs_6_.refs_3_, ...), custom_call_target="tpu_custom_call" | custom-call | flops 6000000000 | bytes 1000 | tf_op jit(solution)/shard_map/project_grad_pack/pallas_call | solution.py:36
  325.6 11.0 %collective-permute-done.42 = bf16[144,1024]{1,0:T(8,128)(2,1)S(1)} collective-permute-done((bf16[144,1024]{1,0:T(8,128)(2,1)S(1)}, bf16[144,1024]{1,0:T(8,128)(2,1)S(1)}, u32[]{:S(2)}, u32[]{:S(2)}) %collective-permute-start.42) | collective-permute-done | bytes 294944 | tf_op jit(solution)/shard_map/ppermute | solution.py:1022
  338.6 3.6 collective-permute-done.44.refs_2_
  344.0 3.8 %hidden_grad.4.refs_5_ = bf16[1,2,256,1024]{3,2,1,0:T(8,128)(2,1)} custom-call(s32[4]{0:T(128)S(1)} %pad_add_fusion.1.refs_0_.refs_2_, bf16[1024,768]{1,0:T(8,128)(2,1)S(1)} %bitcast.86, bf16[2,1024,768]{2,1,0:T(8,128)(2,1)} %attention_backward.3.refs_4_.refs_2_.refs_3_.refs_5_, bf16[2,2,256,1024]{3,2,1,0:T(8,128)(2,1)} %collective-permute-done.31.refs_3_.refs_4_, ...), custom_call_target="tpu_custom_call" | custom-call | flops 6000000000 | bytes 1000 | tf_op jit(solution)/shard_map/hidden_grad/pallas_call | solution.py:36
  354.2 4.5 %collective-permute-done.39.refs_2_ = bf16[144,768]{1,0:T(8,128)(2,1)S(1)} collective-permute-done((bf16[144,768]{1,0:T(8,128)(2,1)}, bf16[144,768]{1,0:T(8,128)(2,1)S(1)}, u32[]{:S(2)}, u32[]{:S(2)}) %collective-permute-start.39) | collective-permute-done | bytes 221216 | tf_op jit(solution)/shard_map/ppermute | solution.py:1022
  363.0 4.3 %hidden_grad.5 = f32[1,2,256,1024]{3,2,1,0:T(8,128)} custom-call(s32[4]{0:T(128)S(1)} %pad_add_fusion.1.refs_0_.refs_2_, bf16[1024,768]{1,0:T(8,128)(2,1)S(1)} %bitcast.87, bf16[2,1024,768]{2,1,0:T(8,128)(2,1)} %attention_backward.3.refs_4_.refs_2_.refs_3_.refs_5_, bf16[2,256,1024]{2,1,0:T(8,128)(2,1)S(1)} %copy-done.32, ...), custom_call_target="tpu_custom_call" | custom-call | flops 6000000000 | bytes 1000 | tf_op jit(solution)/shard_map/hidden_grad/pallas_call | solution.py:36
  (291 shorter events, 120.4 us)
Async XLA Ops:
  7.2 53.8 %all-gather.9.cloned.1.call-start = ((), (), s32[]{:S(2)}) async-start(), calls=%async_computation.6 | async-start | bytes 1990656 | tf_op jit(solution)/shard_map/all_gather | solution.py:1130
  7.3 60.5 %collective-permute-start.1 = (bf16[2,256,1024]{2,1,0:T(8,128)(2,1)}, bf16[2,256,1024]{2,1,0:T(8,128)(2,1)}, u32[]{:S(2)}, u32[]{:S(2)}) collective-permute-start(bf16[2,256,1024]{2,1,0:T(8,128)(2,1)} %refs_1_.1), channel_id=1, source_target_pairs={{0,16},{1,9},{2,18},{3,11},{4,20},{5,13},{6,22},{7,15},{8,24},{9,1... | collective-permute-start | bytes 3145736 | tf_op jit(solution)/shard_map/ppermute | solution.py:1022
  10.3 23.4 %collective-permute-start = (bf16[2,256,1024]{2,1,0:T(8,128)(2,1)}, bf16[2,256,1024]{2,1,0:T(8,128)(2,1)}, u32[]{:S(2)}, u32[]{:S(2)}) collective-permute-start(bf16[2,256,1024]{2,1,0:T(8,128)(2,1)} %refs_1_.1), channel_id=1, source_target_pairs={{0,8},{1,17},{2,10},{3,19},{4,12},{5,21},{6,14},{7,23},{8,0},{9,25... | collective-permute-start | bytes 3145736 | tf_op jit(solution)/shard_map/ppermute | solution.py:1022
  15.1 97.5 %all-gather.7.cloned.1.call-start = ((), (), s32[]{:S(2)}) async-start(), calls=%async_computation.3 | async-start | bytes 1310720 | tf_op jit(solution)/shard_map/all_gather | solution.py:1132
  18.1 17.4 %collective-permute-start.6 = (bf16[256,512]{1,0:T(8,128)(2,1)S(1)}, bf16[256,512]{1,0:T(8,128)(2,1)S(1)}, u32[]{:S(2)}, u32[]{:S(2)}) collective-permute-start(bf16[256,512]{1,0:T(8,128)(2,1)S(1)} %pad_maximum_fusion.refs_1_), channel_id=1, source_target_pairs={{0,6},{2,0},{4,2},{6,4},{1,7},{3,1},{5,3},{7,5},{8,14},{10,8},{12,... | collective-permute-start | bytes 786440 | tf_op jit(solution)/shard_map/ppermute | solution.py:1043
  21.7 37.2 %collective-permute-start.5 = (bf16[256,512]{1,0:T(8,128)(2,1)S(1)}, bf16[256,512]{1,0:T(8,128)(2,1)S(1)}, u32[]{:S(2)}, u32[]{:S(2)}) collective-permute-start(bf16[256,512]{1,0:T(8,128)(2,1)S(1)} %pad_maximum_fusion.refs_1_), channel_id=1, source_target_pairs={{0,4},{2,6},{4,0},{6,2},{1,5},{3,7},{5,1},{7,3},{8,12},{10,14},{12... | collective-permute-start | bytes 786440 | tf_op jit(solution)/shard_map/ppermute | solution.py:1043
  21.7 37.2 %collective-permute-start.4 = (bf16[256,512]{1,0:T(8,128)(2,1)S(1)}, bf16[256,512]{1,0:T(8,128)(2,1)S(1)}, u32[]{:S(2)}, u32[]{:S(2)}) collective-permute-start(bf16[256,512]{1,0:T(8,128)(2,1)S(1)} %pad_maximum_fusion.refs_1_), channel_id=1, source_target_pairs={{0,2},{2,4},{4,6},{6,0},{1,3},{3,5},{5,7},{7,1},{8,10},{10,12},{12... | collective-permute-start | bytes 786440 | tf_op jit(solution)/shard_map/ppermute | solution.py:1043
  33.7 25.8 %collective-permute-start.2 = (bf16[2,256,1024]{2,1,0:T(8,128)(2,1)}, bf16[2,256,1024]{2,1,0:T(8,128)(2,1)}, u32[]{:S(2)}, u32[]{:S(2)}) collective-permute-start(bf16[2,256,1024]{2,1,0:T(8,128)(2,1)} %collective-permute-done.refs_5_.refs_2_), channel_id=1, source_target_pairs={{0,16},{1,9},{2,18},{3,11},{4,20},{5,13},{6,22},{7,15},{8,24},{9,1... | collective-permute-start | bytes 3145736 | tf_op jit(solution)/shard_map/ppermute | solution.py:1022
  60.6 41.1 %collective-permute-start.12 = (bf16[1024,512]{1,0:T(8,128)(2,1)}, bf16[1024,512]{1,0:T(8,128)(2,1)}, u32[]{:S(2)}, u32[]{:S(2)}) collective-permute-start(bf16[1024,512]{1,0:T(8,128)(2,1)} %hold.4.refs_6_.refs_2_.refs_10_), channel_id=1, source_target_pairs={{0,16},{1,9},{2,18},{3,11},{4,20},{5,13},{6,22},{7,15},{8,24},{9,1... | collective-permute-start | bytes 3145736 | tf_op jit(solution)/shard_map/ppermute | solution.py:1022
  61.0 38.9 %collective-permute-start.11 = (bf16[1024,512]{1,0:T(8,128)(2,1)}, bf16[1024,512]{1,0:T(8,128)(2,1)}, u32[]{:S(2)}, u32[]{:S(2)}) collective-permute-start(bf16[1024,512]{1,0:T(8,128)(2,1)} %hold.4.refs_6_.refs_2_.refs_10_), channel_id=1, source_target_pairs={{0,8},{1,17},{2,10},{3,19},{4,12},{5,21},{6,14},{7,23},{8,0},{9,25... | collective-permute-start | bytes 3145736 | tf_op jit(solution)/shard_map/ppermute | solution.py:1022
  63.3 59.9 %all-gather.5.cloned.1.call-start = ((), (), s32[]{:S(2)}) async-start(), calls=%async_computation.2 | async-start | bytes 2359296 | tf_op jit(solution)/shard_map/all_gather | solution.py:1133
  67.5 237.4 %reduce-scatter.3.cloned.1.call-start = ((), (), s32[]{:S(2)}) async-start(), calls=%async_computation.4 | async-start | bytes 2654208 | tf_op jit(solution)/shard_map/reduce_scatter | solution.py:1212
  99.9 33.9 %collective-permute-start.13 = (bf16[1024,512]{1,0:T(8,128)(2,1)}, bf16[1024,512]{1,0:T(8,128)(2,1)}, u32[]{:S(2)}, u32[]{:S(2)}) collective-permute-start(bf16[1024,512]{1,0:T(8,128)(2,1)} %collective-permute-done.11.refs_4_.refs_3_.refs_11_), channel_id=1, source_target_pairs={{0,16},{1,9},{2,18},{3,11},{4,20},{5,13},{6,22},{7,15},{8,24},{9,1... | collective-permute-start | bytes 3145736 | tf_op jit(solution)/shard_map/ppermute | solution.py:1022
  114.8 18.7 %collective-permute-start.14 = (bf16[512,1024]{1,0:T(8,128)(2,1)}, bf16[512,1024]{1,0:T(8,128)(2,1)}, u32[]{:S(2)}, u32[]{:S(2)}) collective-permute-start(bf16[512,1024]{1,0:T(8,128)(2,1)} %hold.7.refs_4_.refs_6_), channel_id=1, source_target_pairs={{0,8},{1,17},{2,10},{3,19},{4,12},{5,21},{6,14},{7,23},{8,0},{9,25... | collective-permute-start | bytes 3145736 | tf_op jit(solution)/shard_map/ppermute | solution.py:1022
  133.5 23.3 %collective-permute-start.16 = (bf16[512,1024]{1,0:T(8,128)(2,1)}, bf16[512,1024]{1,0:T(8,128)(2,1)S(1)}, u32[]{:S(2)}, u32[]{:S(2)}) collective-permute-start(bf16[512,1024]{1,0:T(8,128)(2,1)} %collective-permute-done.14.refs_10_.refs_5_.refs_7_), channel_id=1, source_target_pairs={{0,16},{1,9},{2,18},{3,11},{4,20},{5,13},{6,22},{7,15},{8,24},{9,1... | collective-permute-start | bytes 3145736 | tf_op jit(solution)/shard_map/ppermute | solution.py:1022
  182.3 33.0 %collective-permute-start.23 = (bf16[2,512,1024]{2,1,0:T(8,128)(2,1)}, bf16[2,512,1024]{2,1,0:T(8,128)(2,1)}, u32[]{:S(2)}, u32[]{:S(2)}) collective-permute-start(bf16[2,512,1024]{2,1,0:T(8,128)(2,1)} %down_grad.3.refs_0_), channel_id=1, source_target_pairs={{0,8},{1,17},{2,10},{3,19},{4,12},{5,21},{6,14},{7,23},{8,0},{9,25... | collective-permute-start | bytes 6291464 | tf_op jit(solution)/shard_map/ppermute | solution.py:1022
  211.8 19.8 %collective-permute-start.20 = (bf16[2,256,256]{2,1,0:T(8,128)(2,1)}, bf16[2,256,256]{2,1,0:T(8,128)(2,1)S(1)}, u32[]{:S(2)}, u32[]{:S(2)}) collective-permute-start(bf16[2,256,256]{2,1,0:T(8,128)(2,1)} %get-tuple-element.84), channel_id=1, source_target_pairs={{0,8},{1,17},{2,10},{3,19},{4,12},{5,21},{6,14},{7,23},{8,0},{9,25... | collective-permute-start | bytes 786440 | tf_op jit(solution)/shard_map/ppermute | solution.py:1039
  212.7 18.8 %collective-permute-start.21 = (bf16[2,256,256]{2,1,0:T(8,128)(2,1)}, bf16[2,256,256]{2,1,0:T(8,128)(2,1)S(1)}, u32[]{:S(2)}, u32[]{:S(2)}) collective-permute-start(bf16[2,256,256]{2,1,0:T(8,128)(2,1)} %get-tuple-element.85), channel_id=1, source_target_pairs={{0,16},{1,9},{2,18},{3,11},{4,20},{5,13},{6,22},{7,15},{8,24},{9,1... | collective-permute-start | bytes 786440 | tf_op jit(solution)/shard_map/ppermute | solution.py:1039
  213.8 17.8 %collective-permute-start.22 = (bf16[2,256,256]{2,1,0:T(8,128)(2,1)}, bf16[2,256,256]{2,1,0:T(8,128)(2,1)S(1)}, u32[]{:S(2)}, u32[]{:S(2)}) collective-permute-start(bf16[2,256,256]{2,1,0:T(8,128)(2,1)} %get-tuple-element.86), channel_id=1, source_target_pairs={{0,24},{1,25},{2,26},{3,27},{4,28},{5,29},{6,30},{7,31},{8,16},{9,... | collective-permute-start | bytes 786440 | tf_op jit(solution)/shard_map/ppermute | solution.py:1039
  220.4 27.9 %collective-permute-start.25 = (bf16[1,512,1024]{2,1,0:T(8,128)(2,1)}, bf16[1,512,1024]{2,1,0:T(8,128)(2,1)}, u32[]{:S(2)}, u32[]{:S(2)}) collective-permute-start(bf16[1,512,1024]{2,1,0:T(8,128)(2,1)} %down_grad.4.refs_4_), channel_id=1, source_target_pairs={{0,16},{1,9},{2,18},{3,11},{4,20},{5,13},{6,22},{7,15},{8,24},{9,1... | collective-permute-start | bytes 3145736 | tf_op jit(solution)/shard_map/ppermute | solution.py:1022
  227.6 33.1 %collective-permute-start.24 = (bf16[2,1024,512]{2,1,0:T(8,128)(2,1)}, bf16[2,1024,512]{2,1,0:T(8,128)(2,1)}, u32[]{:S(2)}, u32[]{:S(2)}) collective-permute-start(bf16[2,1024,512]{2,1,0:T(8,128)(2,1)} %up_grad.3.refs_7_), channel_id=1, source_target_pairs={{0,8},{1,17},{2,10},{3,19},{4,12},{5,21},{6,14},{7,23},{8,0},{9,25... | collective-permute-start | bytes 6291464 | tf_op jit(solution)/shard_map/ppermute | solution.py:1022
  231.5 118.6 %reduce-scatter.5.cloned.1.call-start = ((), (), s32[]{:S(2)}) async-start(), calls=%async_computation.5 | async-start | bytes 1990656 | tf_op jit(solution)/shard_map/reduce_scatter | solution.py:1241
  252.5 23.8 %collective-permute-start.27 = (bf16[128,1024]{1,0:T(8,128)(2,1)S(1)}, bf16[128,1024]{1,0:T(8,128)(2,1)S(1)}, u32[]{:S(2)}, u32[]{:S(2)}) collective-permute-start(bf16[128,1024]{1,0:T(8,128)(2,1)S(1)} %get-tuple-element.97), channel_id=1, source_target_pairs={{0,2},{2,4},{4,6},{6,0},{1,3},{3,5},{5,7},{7,1},{8,10},{10,12},{12... | collective-permute-start | bytes 786440 | tf_op jit(solution)/shard_map/ppermute | solution.py:1043
  253.3 26.7 %collective-permute-start.28 = (bf16[128,1024]{1,0:T(8,128)(2,1)S(1)}, bf16[128,1024]{1,0:T(8,128)(2,1)S(1)}, u32[]{:S(2)}, u32[]{:S(2)}) collective-permute-start(bf16[128,1024]{1,0:T(8,128)(2,1)S(1)} %get-tuple-element.98), channel_id=1, source_target_pairs={{0,4},{2,6},{4,0},{6,2},{1,5},{3,7},{5,1},{7,3},{8,12},{10,14},{12... | collective-permute-start | bytes 786440 | tf_op jit(solution)/shard_map/ppermute | solution.py:1043
  254.5 25.6 %collective-permute-start.29 = (bf16[128,1024]{1,0:T(8,128)(2,1)S(1)}, bf16[128,1024]{1,0:T(8,128)(2,1)S(1)}, u32[]{:S(2)}, u32[]{:S(2)}) collective-permute-start(bf16[128,1024]{1,0:T(8,128)(2,1)S(1)} %get-tuple-element.99), channel_id=1, source_target_pairs={{0,6},{2,0},{4,2},{6,4},{1,7},{3,1},{5,3},{7,5},{8,14},{10,8},{12,... | collective-permute-start | bytes 786440 | tf_op jit(solution)/shard_map/ppermute | solution.py:1043
  281.1 22.3 %collective-permute-start.35 = (bf16[128,1024]{1,0:T(8,128)(2,1)}, bf16[128,1024]{1,0:T(8,128)(2,1)}, u32[]{:S(2)}, u32[]{:S(2)}) collective-permute-start(bf16[128,1024]{1,0:T(8,128)(2,1)} %total_rows.1.refs_5_.refs_1_), channel_id=1, source_target_pairs={{0,16},{1,9},{2,18},{3,11},{4,20},{5,13},{6,22},{7,15},{8,24},{9,1... | collective-permute-start | bytes 786440 | tf_op jit(solution)/shard_map/ppermute | solution.py:1022
  289.6 24.8 %collective-permute-start.32 = (bf16[256,512]{1,0:T(8,128)(2,1)}, bf16[256,512]{1,0:T(8,128)(2,1)S(1)}, u32[]{:S(2)}, u32[]{:S(2)}) collective-permute-start(bf16[256,512]{1,0:T(8,128)(2,1)} %get-tuple-element.101), channel_id=1, source_target_pairs={{0,2},{2,4},{4,6},{6,0},{1,3},{3,5},{5,7},{7,1},{8,10},{10,12},{12... | collective-permute-start | bytes 786440 | tf_op jit(solution)/shard_map/ppermute | solution.py:1043
  295.4 19.0 %collective-permute-start.33 = (bf16[256,512]{1,0:T(8,128)(2,1)}, bf16[256,512]{1,0:T(8,128)(2,1)}, u32[]{:S(2)}, u32[]{:S(2)}) collective-permute-start(bf16[256,512]{1,0:T(8,128)(2,1)} %get-tuple-element.102), channel_id=1, source_target_pairs={{0,4},{2,6},{4,0},{6,2},{1,5},{3,7},{5,1},{7,3},{8,12},{10,14},{12... | collective-permute-start | bytes 786440 | tf_op jit(solution)/shard_map/ppermute | solution.py:1043
  303.4 40.7 %collective-permute-start.31 = (bf16[2,2,256,1024]{3,2,1,0:T(8,128)(2,1)}, bf16[2,2,256,1024]{3,2,1,0:T(8,128)(2,1)}, u32[]{:S(2)}, u32[]{:S(2)}) collective-permute-start(bf16[2,2,256,1024]{3,2,1,0:T(8,128)(2,1)} %hidden_grad.3.refs_6_), channel_id=1, source_target_pairs={{0,8},{1,17},{2,10},{3,19},{4,12},{5,21},{6,14},{7,23},{8,0},{9,25... | collective-permute-start | bytes 6291464 | tf_op jit(solution)/shard_map/ppermute | solution.py:1022
  318.1 18.5 %collective-permute-start.42 = (bf16[144,1024]{1,0:T(8,128)(2,1)S(1)}, bf16[144,1024]{1,0:T(8,128)(2,1)S(1)}, u32[]{:S(2)}, u32[]{:S(2)}) collective-permute-start(bf16[144,1024]{1,0:T(8,128)(2,1)S(1)} %copy-done.7), channel_id=1, source_target_pairs={{0,8},{1,17},{2,10},{3,19},{4,12},{5,21},{6,14},{7,23},{8,0},{9,25... | collective-permute-start | bytes 884744 | tf_op jit(solution)/shard_map/ppermute | solution.py:1022
  323.6 18.7 %collective-permute-start.44 = (bf16[2,128,512]{2,1,0:T(8,128)(2,1)S(1)}, bf16[2,128,512]{2,1,0:T(8,128)(2,1)S(1)}, u32[]{:S(2)}, u32[]{:S(2)}) collective-permute-start(bf16[2,128,512]{2,1,0:T(8,128)(2,1)S(1)} %pair.1.refs_4_.refs_1_), channel_id=1, source_target_pairs={{0,8},{1,17},{2,10},{3,19},{4,12},{5,21},{6,14},{7,23},{8,0},{9,25... | collective-permute-start | bytes 786440 | tf_op jit(solution)/shard_map/ppermute | solution.py:1022
  325.0 25.2 %collective-permute-start.45 = (bf16[2,128,512]{2,1,0:T(8,128)(2,1)S(1)}, bf16[2,128,512]{2,1,0:T(8,128)(2,1)S(1)}, u32[]{:S(2)}, u32[]{:S(2)}) collective-permute-start(bf16[2,128,512]{2,1,0:T(8,128)(2,1)S(1)} %pair.1.refs_4_.refs_1_), channel_id=1, source_target_pairs={{0,16},{1,9},{2,18},{3,11},{4,20},{5,13},{6,22},{7,15},{8,24},{9,1... | collective-permute-start | bytes 786440 | tf_op jit(solution)/shard_map/ppermute | solution.py:1022
  (77 other events, 579.7 us)
Sparse Core Ops, SparseCore 0:
  15.2 44.8 all-gather.8
  63.4 28.9 all-gather.6
  94.5 28.5 all-gather.4
  231.6 41.4 reduce-scatter.2
  314.5 33.3 reduce-scatter.4

commit v3 on v2

--- a/solution.py
+++ b/solution.py
@@ -111,14 +111,16 @@
 def project(places, blocks, weight, bias, scale):
     seqs, length, width = blocks[0].shape
     ranks = len(blocks)
-    out_width = weight.shape[1]
+    owners, _, out_width = weight.shape
+    rows = width // owners
 
     def kernel(place_ref, weight_ref, bias_ref, scale_ref, *refs):
         for q in range(ranks):
 
             @pl.when(pl.program_id(0) // seqs == q)
             def _(q=q):
-                product = dot(refs[q][0], weight_ref[...], 1, 0) + bias_ref[...]
+                whole = weight_ref[:, :rows, :].reshape(width, out_width)
+                product = dot(refs[q][0], whole, 1, 0) + bias_ref[...]
                 refs[ranks][0] = (product * scale_ref[...]).astype(jnp.bfloat16)
 
     def source(q):
@@ -371,7 +373,7 @@
 def up_grad(uppers, own, other, addends, waits=()):
     count, width = own.shape
     units = uppers[0].shape[1]
-    tile = min(TILE, width)
+    tile = min(2 * TILE, width)
     blocks = len(uppers)
     spread = [(q, a) for q in range(blocks) for a in addends[q]]
 
@@ -472,15 +474,17 @@
     )
 
 
-def hidden_grad(places, dqkv, weight, length, picks, addends, dtype, waits=()):
+def hidden_grad(places, dqkv, weight, width, length, picks, addends, dtype, waits=()):
     seqs, _, out_width = dqkv.shape
-    width = weight.shape[0]
+    owners = weight.shape[0]
+    rows = width // owners
     blocks = len(picks)
     spread = [(k, a) for k in range(blocks) for a in addends[k]]
 
     def kernel(place_ref, weight_ref, *refs):
+        whole = weight_ref[:, :rows, :].reshape(width, out_width)
         for k in range(blocks):
-            total = dot(refs[k][0], weight_ref[...], 1, 1)
+            total = dot(refs[k][0], whole, 1, 1)
             for j, (of, _) in enumerate(spread):
                 if of == k:
                     total = total + wide(refs[blocks + j][0])
@@ -1135,7 +1139,7 @@
     kind, start = plan_rows(segments)
     keep = wide(lax.dynamic_slice_in_dim(segments, here * length, length, 1) != 0)[:, :, None]
 
-    qkv_weight = gathered[:, :rows].reshape(width, out_width)
+    qkv_weight = gathered
     gathered = wide(gathered[:, rows:, :rows])
     vectors = gathered.transpose(1, 0, 2).reshape(EXTRA, width)
     biases = lax.dynamic_slice_in_dim(vectors, heads_at, head_width, 1)
@@ -1228,7 +1232,7 @@
         return [pieces[0]] + [ring.shift(pieces[d], d) for d in range(1, chips)]
 
     def hidden_made(turn, addends, waits=()):
-        return hidden_grad(places, dqkv, qkv_weight, length, turn, addends, jnp.bfloat16, waits or (up_pair,))
+        return hidden_grad(places, dqkv, qkv_weight, width, length, turn, addends, jnp.bfloat16, waits or (up_pair,))
 
     down_shard = total_rows(shifted(down_pieces), (dqkv, up_came[-1].array))
     down_parts = ring.gather(down_shard)
@@ -1248,7 +1252,7 @@
     up_pair = pair(core_index, keep_part, swap(take_part), (down_weight_grad,))
     hidden_came, hidden_hop = spread(hidden_made, hidden_sent)
     input_grad = hidden_grad(
-        places, dqkv, qkv_weight, length, [0], [[View(dbranch)] + hidden_came], jnp.float32
+        places, dqkv, qkv_weight, width, length, [0], [[View(dbranch)] + hidden_came], jnp.float32
     )[0]
 
     up_parts = ring.gather(up_pair)

time: 381 us -> 379 us (level)
    unnamed x116 -> x128, local copies, waits for them, and re-layouts: 23.8 us -> 23.1 us
  transfers between devices with their start and end apart: 52 -> 52, of which waited for: 18 -> 19; matrix products, arithmetic and copies ran while one was open for 4% -> 4% of each run, Pallas kernels for 41% -> 41%
where the time goes in v3:
time: 379 us; the launch traced here: 375 us
  Pallas kernels  169 us (45%)
  waiting for transfers between devices  95.6 us (25%)
  starting transfers between devices  57.5 us (15%)
  local copies, waits for them, and re-layouts  32.7 us (9%)
  between operations  14.8 us (4%)
  other arithmetic  5.8 us (2%)
    pallas_call x38, Pallas kernels, run(): pl.pallas_call(waiting, grid_spec=pltpu.PrefetchScalarGridSpec(num_scalar...  169 us
    ppermute x26, waiting for transfers between devices, hop(): return lax.ppermute(block, AXES, pairs)  45.3 us
    ppermute x26, starting transfers between devices, hop(): return lax.ppermute(block, AXES, pairs)  31.6 us
    ppermute x9, waiting for transfers between devices, shift(): lax.ppermute(block, 'z', [(z, (z + d) % self.chips) for z in range(self.c...  27.8 us
    unnamed x128, local copies, waits for them, and re-layouts  23.1 us
    ppermute x9, starting transfers between devices, shift(): lax.ppermute(block, 'z', [(z, (z + d) % self.chips) for z in range(self.c...  18 us
    ppermute x6, waiting for transfers between devices, exchange(): out.append(lax.ppermute(blocks[q], AXES, pairs))  10.8 us
    all_gather x1, waiting for transfers between devices, local(): lax.all_gather(hold(out_weight, (down_rows,)), ROWS, axis=0, tiled=True)  8.85 us
  transfers between devices with their start and end apart: 52, of which 19 were waited for; matrix products, arithmetic and copies ran while one was open for 4% of the time, Pallas kernels for 41%

profile of v3, /device:TPU:0, one launch (start us, length us, event | category | flops | bytes accessed | tf_op | source)
XLA Modules:
  0.0 375.3 jit_solution(7429557638524758410)
XLA Ops:
  18.1 3.7 collective-permute-start.6
  23.3 10.5 %collective-permute-done.refs_5_.refs_2_ = bf16[2,256,1024]{2,1,0:T(8,128)(2,1)} collective-permute-done((bf16[2,256,1024]{2,1,0:T(8,128)(2,1)}, bf16[2,256,1024]{2,1,0:T(8,128)(2,1)}, u32[]{:S(2)}, u32[]{:S(2)}) %collective-permute-start) | collective-permute-done | bytes 1048608 | tf_op jit(solution)/shard_map/ppermute | solution.py:1026
  35.5 23.5 %collective-permute-done.5.refs_3_ = bf16[256,512]{1,0:T(8,128)(2,1)S(1)} collective-permute-done((bf16[256,512]{1,0:T(8,128)(2,1)S(1)}, bf16[256,512]{1,0:T(8,128)(2,1)S(1)}, u32[]{:S(2)}, u32[]{:S(2)}) %collective-permute-start.5) | collective-permute-done | bytes 262176 | tf_op jit(solution)/shard_map/ppermute | solution.py:1047
  66.7 10.0 %project.1.refs_3_ = bf16[2,1024,768]{2,1,0:T(8,128)(2,1)} custom-call(s32[4]{0:T(128)S(1)} %pad_add_fusion.1.refs_0_.refs_2_, bf16[8,144,768]{2,1,0:T(8,128)(2,1)} %bitcast.80, f32[1,768]{1,0:T(1,128)S(1)} %broadcast_in_dim.133.refs_2_, f32[1,768]{1,0:T(1,128)S(1)} %compare_select_fusion.refs_3_, bf16[2,256,1024]{2,1,0:T(8,128)(2,1)S(1)} %copy-done.11, ...), custom_call_target="tpu_custom_call" | custom-call | flops 30000001024 | bytes 1000 | tf_op jit(solution)/shard_map/project/pallas_call | solution.py:36
  76.7 16.2 %attention_forward.1 = (bf16[2,1024,256]{2,1,0:T(8,128)(2,1)S(1)}, f32[2,4,1024]{2,1,0:T(4,128)S(1)}, bf16[2,256,256]{2,1,0:T(8,128)(2,1)S(1)}, bf16[2,256,256]{...) custom-call(s32[2]{0:T(128)S(1)} %select_select_fusion.refs_0_, ...), custom_call_target="tpu_custom_call" | custom-call | flops 299999985664 | bytes 1000 | tf_op jit(solution)/shard_map/attention_forward/pallas_call | solution.py:36
  99.4 3.7 collective-permute-done.7.refs_2_.refs_1_
  103.7 6.6 %collective-permute-done.9.refs_4_.refs_3_ = bf16[2,256,256]{2,1,0:T(8,128)(2,1)S(1)} collective-permute-done((bf16[2,256,256]{2,1,0:T(8,128)(2,1)S(1)}, bf16[2,256,256]{2,1,0:T(8,128)(2,1)S(1)}, u32[]{:S(2)}, u32[]{:S(2)}) %collective-permute-start.9) | collective-permute-done | bytes 262176 | tf_op jit(solution)/shard_map/ppermute | solution.py:1043
  114.3 8.9 %all-gather.5.cloned.1.call-done.refs_5_.refs_6_ = bf16[1024,1024]{1,0:T(8,128)(2,1)} async-done(((bf16[128,1024]{1,0:T(8,128)(2,1)}), bf16[1024,1024]{1,0:T(8,128)(2,1)}) %all-gather.5.cloned.1.call-update) | async-done | bytes 2097168 | tf_op jit(solution)/shard_map/all_gather | solution.py:1137
  123.2 4.5 %out_norm.1 = (bf16[2,256,1024]{2,1,0:T(8,128)(2,1)S(1)}, bf16[2,256,1024]{2,1,0:T(8,128)(2,1)S(1)}) custom-call(s32[4]{0:T(128)S(1)} %pad_add_fusion.1.refs_0_.refs_2_, bf16[2,256,256]{2,1,0:T(8,128)(2,1)S(1)} %get-tuple-element.64.refs_1_, bf16[2,256,256]{2,1,0:T(8,128)(2,1)S(1)} %collective-permute-done.7.refs_2_.refs_1_, ...), custom_call_target="tpu_custom_call" | custom-call | flops 30000001024 | bytes 1000 | tf_op jit(solution)/shard_map/out_norm/pallas_call | solution.py:36
  132.7 11.0 %up_forward.1 = (bf16[1024,512]{1,0:T(8,128)(2,1)S(1)}, bf16[1024,512]{1,0:T(8,128)(2,1)S(1)}, bf16[1024,512]{1,0:T(8,128)(2,1)S(1)}, bf16[1024,512]{1,0:T(8,128...) custom-call(bf16[512,1024]{1,0:T(8,128)(2,1)} %bitcast.86, ...), custom_call_target="tpu_custom_call" | custom-call | flops 30000001024 | bytes 1000 | tf_op jit(solution)/shard_map/up_forward/pallas_call | solution.py:36
  145.6 11.2 %collective-permute-done.16.refs_7_.refs_9_ = bf16[512,1024]{1,0:T(8,128)(2,1)S(1)} collective-permute-done((bf16[512,1024]{1,0:T(8,128)(2,1)}, bf16[512,1024]{1,0:T(8,128)(2,1)S(1)}, u32[]{:S(2)}, u32[]{:S(2)}) %collective-permute-start.16) | collective-permute-done | bytes 1048608 | tf_op jit(solution)/shard_map/ppermute | solution.py:1026
  157.8 4.9 %down_forward.2.refs_8_ = bf16[512,1024]{1,0:T(8,128)(2,1)S(1)} custom-call(bf16[1024,512]{1,0:T(8,128)(2,1)S(1)} %get-tuple-element.69.refs_0_.refs_2_, bf16[1024,512]{1,0:T(8,128)(2,1)S(1)} %get-tuple-element.70.refs_1_.refs_2_, bf16[1024,512]{1,0:T(8,128)(2,1)} %copy-done.48, bf16[1024,512]{1,0:T(8,128)(2,1)} %get-tuple-element.72.refs_3_, ...), custom_call_target="tpu_custom_call" | custom-call | flops 30000001024 | bytes 1000 | tf_op jit(solution)/shard_map/down_forward/pallas_call | solution.py:36
  163.7 4.9 %down_forward.3 = bf16[512,1024]{1,0:T(8,128)(2,1)S(1)} custom-call(bf16[1024,512]{1,0:T(8,128)(2,1)S(1)} %get-tuple-element.69.refs_0_.refs_2_, bf16[1024,512]{1,0:T(8,128)(2,1)S(1)} %get-tuple-element.70.refs_1_.refs_2_, bf16[1024,512]{1,0:T(8,128)(2,1)} %copy-done.48, bf16[1024,512]{1,0:T(8,128)(2,1)} %get-tuple-element.72.refs_3_, ...), custom_call_target="tpu_custom_call" | custom-call | flops 30000001024 | bytes 1000 | tf_op jit(solution)/shard_map/down_forward/pallas_call | solution.py:36
  168.6 4.8 %norm_two.1 = (bf16[2,256,1024]{2,1,0:T(8,128)(2,1)}, bf16[2,256,1024]{2,1,0:T(8,128)(2,1)S(1)}, f32[8,1024]{1,0:T(8,128)S(1)}) custom-call(bf16[2,256,1024]{2,1,0:T(8,128)(2,1)S(1)} %bitcast.97, bf16[2,256,1024]{2,1,0:T(8,128)(2,1)S(1)} %bitcast.95, bf16[2,256,1024]{2,1,0:T(8,128)(2,1)} %copy-done.51, f32[16,1024]{1,0:T(8,128)S(1)} %bitcast.77, ...), custom_call_target="tpu_custom_call" | custom-call | flops 30000001024 | bytes 1000 | tf_op jit(solution)/shard_map/norm_two/pallas_call | solution.py:36
  177.4 5.0 %down_grad.3.refs_0_ = bf16[2,512,1024]{2,1,0:T(8,128)(2,1)} custom-call(bf16[512,1024]{1,0:T(8,128)(2,1)S(1)} %bitcast.91, bf16[512,1024]{1,0:T(8,128)(2,1)} %collective-permute-done.18.refs_1_, bf16[1024,512]{1,0:T(8,128)(2,1)S(1)} %copy-done.50, bf16[1024,512]{1,0:T(8,128)(2,1)} %get-tuple-element.72.refs_3_), custom_call_target="tpu_custom_call" | custom-call | flops 30000001024 | bytes 1000 | tf_op jit(solution)/shard_map/down_grad/pallas_call | solution.py:36
  183.9 15.7 %feed_forward_back.1 = (bf16[1024,512]{1,0:T(8,128)(2,1)S(1)}, bf16[1024,512]{1,0:T(8,128)(2,1)S(1)}, bf16[1024,512]{1,0:T(8,128)(2,1)S(1)}, bf16[1024,512]{1,0:...) custom-call(bf16[512,1024]{1,0:T(8,128)(2,1)} %bitcast.92, ...), custom_call_target="tpu_custom_call" | custom-call | flops 30000001024 | bytes 1000 | tf_op jit(solution)/shard_map/feed_forward_back/pallas_call | solution.py:36
  203.6 6.6 %norm_one_back.1 = (bf16[2,256,1024]{2,1,0:T(8,128)(2,1)S(1)}, bf16[2,256,256]{2,1,0:T(8,128)(2,1)S(1)}, bf16[2,256,256]{2,1,0:T(8,128)(2,1)}, bf16[2,256,256]{2...) custom-call(s32[4]{0:T(128)S(1)} %pad_add_fusion.1.refs_0_.refs_2_, ...), custom_call_target="tpu_custom_call" | custom-call | flops 30000001024 | bytes 1000 | tf_op jit(solution)/shard_map/norm_one_back/pallas_call | solution.py:36
  215.7 3.9 %down_grad.4.refs_4_ = bf16[1,512,1024]{2,1,0:T(8,128)(2,1)} custom-call(bf16[512,1024]{1,0:T(8,128)(2,1)S(1)} %bitcast.93, bf16[512,1024]{1,0:T(8,128)(2,1)} %collective-permute-done.18.refs_1_, bf16[1024,512]{1,0:T(8,128)(2,1)} %copy-done.48, bf16[2,512,1024]{2,1,0:T(8,128)(2,1)} %collective-permute-done.23.refs_3_, f32[8,128]{1,0:T(8,128)S(1)} %tick.5.refs_4_), custom_call_target="tpu_custom_call" | custom-call | flops 30000001024 | bytes 1000 | tf_op jit(solution)/shard_map/down_grad/pallas_call | solution.py:36
  221.1 5.1 %up_grad.3.refs_7_ = bf16[2,1024,512]{2,1,0:T(8,128)(2,1)} custom-call(bf16[512,1024]{1,0:T(8,128)(2,1)S(1)} %bitcast.87, bf16[512,1024]{1,0:T(8,128)(2,1)} %collective-permute-done.10.refs_1_, bf16[1024,512]{1,0:T(8,128)(2,1)S(1)} %copy-done.43, bf16[1024,512]{1,0:T(8,128)(2,1)} %get-tuple-element.94.refs_3_, bf16[1,512,1024]{2,1,0:T(8,128)(2,1)} %down_grad.4.refs_4_), custom_call_target="tpu_custom_call" | custom-call | flops 30000001024 | bytes 1000 | tf_op jit(solution)/shard_map/up_grad/pallas_call | solution.py:36
  232.2 14.7 %attention_backward.2.refs_5_.refs_12_ = bf16[2,1024,768]{2,1,0:T(8,128)(2,1)} custom-call(s32[2]{0:T(128)S(1)} %copy-done.35, s32[2,4]{1,0:T(2,128)S(1)} %get-tuple-element.114.refs_1_, s32[4]{0:T(128)S(1)} %pad_add_fusion.1.refs_0_.refs_2_, bf16[2,1024,768]{2,1,0:T(8,128)(2,1)} %project.1.refs_3_, bf16[2,256,256]{2,1,0:T(8,128)(2,1)S(1)} %copy-done.53, ...), custom_call_target="tpu_custom_call" | custom-call | flops 30000001024 | bytes 1000 | tf_op jit(solution)/shard_map/attention_backward/pallas_call | solution.py:36
  247.3 3.5 down_grad.5
  256.2 3.5 collective-permute-done.24.refs_3_
  263.9 10.6 %attention_backward.3.refs_4_.refs_2_.refs_3_.refs_5_ = bf16[2,1024,768]{2,1,0:T(8,128)(2,1)} custom-call(s32[2]{0:T(128)S(1)} %copy-done.35, s32[2,4]{1,0:T(2,128)S(1)} %get-tuple-element.114.refs_1_, s32[4]{0:T(128)S(1)} %pad_add_fusion.1.refs_0_.refs_2_, bf16[2,1024,768]{2,1,0:T(8,128)(2,1)} %project.1.refs_3_, ...), custom_call_target="tpu_custom_call", output_to_operand_aliasing={{}: (12, {})} | custom-call | flops 30000001024 | bytes 1000 | tf_op jit(solution)/shard_map/attention_backward/pallas_call | solution.py:36
  274.5 4.3 %collective-permute-done.28.refs_2_ = bf16[128,1024]{1,0:T(8,128)(2,1)S(1)} collective-permute-done((bf16[128,1024]{1,0:T(8,128)(2,1)S(1)}, bf16[128,1024]{1,0:T(8,128)(2,1)S(1)}, u32[]{:S(2)}, u32[]{:S(2)}) %collective-permute-start.28) | collective-permute-done | bytes 262176 | tf_op jit(solution)/shard_map/ppermute | solution.py:1047
  287.3 5.9 %collective-permute-start.32 = (bf16[256,512]{1,0:T(8,128)(2,1)}, bf16[256,512]{1,0:T(8,128)(2,1)S(1)}, u32[]{:S(2)}, u32[]{:S(2)}) collective-permute-start(bf16[256,512]{1,0:T(8,128)(2,1)} %get-tuple-element.101), channel_id=1, source_target_pairs={{0,2},{2,4},{4,6},{6,0},{1,3},{3,5},{5,7},{7,1},{8,10},{10,12},{12... | collective-permute-start | bytes 786440 | tf_op jit(solution)/shard_map/ppermute | solution.py:1047
  296.5 4.7 %hidden_grad.3.refs_6_ = bf16[2,2,256,1024]{3,2,1,0:T(8,128)(2,1)} custom-call(s32[4]{0:T(128)S(1)} %copy-done.10, bf16[8,144,768]{2,1,0:T(8,128)(2,1)S(1)} %bitcast.82, bf16[2,1024,768]{2,1,0:T(8,128)(2,1)} %attention_backward.3.refs_4_.refs_2_.refs_3_.refs_5_, bf16[2,1024,768]{2,1,0:T(8,128)(2,1)} %attention_backward.3.refs_4_.refs_2_.refs_3_.refs_5_, ...), custom_call_target="tpu_custom_call" | custom-call | flops 6000000000 | bytes 1000 | tf_op jit(solution)/shard_map/hidden_grad/pallas_call | solution.py:36
  303.3 8.5 %project_grad_pack.1.refs_5_ = bf16[8,144,768]{2,1,0:T(8,128)(2,1)} custom-call(s32[4]{0:T(128)S(1)} %copy-done.10, bf16[2,256,1024]{2,1,0:T(8,128)(2,1)S(1)} %copy-done.12, bf16[2,256,1024]{2,1,0:T(8,128)(2,1)} %collective-permute-done.refs_5_.refs_2_, bf16[2,256,1024]{2,1,0:T(8,128)(2,1)} %collective-permute-done.1.refs_6_.refs_3_, ...), custom_call_target="tpu_custom_call" | custom-call | flops 6000000000 | bytes 1000 | tf_op jit(solution)/shard_map/project_grad_pack/pallas_call | solution.py:36
  325.1 9.4 %collective-permute-done.42 = bf16[144,1024]{1,0:T(8,128)(2,1)S(1)} collective-permute-done((bf16[144,1024]{1,0:T(8,128)(2,1)S(1)}, bf16[144,1024]{1,0:T(8,128)(2,1)S(1)}, u32[]{:S(2)}, u32[]{:S(2)}) %collective-permute-start.42) | collective-permute-done | bytes 294944 | tf_op jit(solution)/shard_map/ppermute | solution.py:1026
  336.6 3.7 collective-permute-done.44.refs_2_
  342.1 3.8 %hidden_grad.4.refs_5_ = bf16[1,2,256,1024]{3,2,1,0:T(8,128)(2,1)} custom-call(s32[4]{0:T(128)S(1)} %copy-done.10, bf16[8,144,768]{2,1,0:T(8,128)(2,1)S(1)} %bitcast.83, bf16[2,1024,768]{2,1,0:T(8,128)(2,1)} %attention_backward.3.refs_4_.refs_2_.refs_3_.refs_5_, bf16[2,2,256,1024]{3,2,1,0:T(8,128)(2,1)} %collective-permute-done.31.refs_3_.refs_4_, ...), custom_call_target="tpu_custom_call" | custom-call | flops 6000000000 | bytes 1000 | tf_op jit(solution)/shard_map/hidden_grad/pallas_call | solution.py:36
  354.3 3.4 collective-permute-done.39.refs_2_
  360.9 4.1 %hidden_grad.5 = f32[1,2,256,1024]{3,2,1,0:T(8,128)} custom-call(s32[4]{0:T(128)S(1)} %copy-done.10, bf16[8,144,768]{2,1,0:T(8,128)(2,1)S(1)} %bitcast.84, bf16[2,1024,768]{2,1,0:T(8,128)(2,1)} %attention_backward.3.refs_4_.refs_2_.refs_3_.refs_5_, bf16[2,256,1024]{2,1,0:T(8,128)(2,1)S(1)} %copy-done.37, ...), custom_call_target="tpu_custom_call" | custom-call | flops 6000000000 | bytes 1000 | tf_op jit(solution)/shard_map/hidden_grad/pallas_call | solution.py:36
  (302 shorter events, 120.0 us)
Async XLA Ops:
  7.2 53.8 %all-gather.9.cloned.1.call-start = ((), (), s32[]{:S(2)}) async-start(), calls=%async_computation.6 | async-start | bytes 1990656 | tf_op jit(solution)/shard_map/all_gather | solution.py:1134
  7.3 59.4 %collective-permute-start.1 = (bf16[2,256,1024]{2,1,0:T(8,128)(2,1)}, bf16[2,256,1024]{2,1,0:T(8,128)(2,1)}, u32[]{:S(2)}, u32[]{:S(2)}) collective-permute-start(bf16[2,256,1024]{2,1,0:T(8,128)(2,1)} %refs_1_.1), channel_id=1, source_target_pairs={{0,16},{1,9},{2,18},{3,11},{4,20},{5,13},{6,22},{7,15},{8,24},{9,1... | collective-permute-start | bytes 3145736 | tf_op jit(solution)/shard_map/ppermute | solution.py:1026
  10.3 23.4 %collective-permute-start = (bf16[2,256,1024]{2,1,0:T(8,128)(2,1)}, bf16[2,256,1024]{2,1,0:T(8,128)(2,1)}, u32[]{:S(2)}, u32[]{:S(2)}) collective-permute-start(bf16[2,256,1024]{2,1,0:T(8,128)(2,1)} %refs_1_.1), channel_id=1, source_target_pairs={{0,8},{1,17},{2,10},{3,19},{4,12},{5,21},{6,14},{7,23},{8,0},{9,25... | collective-permute-start | bytes 3145736 | tf_op jit(solution)/shard_map/ppermute | solution.py:1026
  15.1 95.2 %all-gather.7.cloned.1.call-start = ((), (), s32[]{:S(2)}) async-start(), calls=%async_computation.3 | async-start | bytes 1310720 | tf_op jit(solution)/shard_map/all_gather | solution.py:1136
  18.1 17.4 %collective-permute-start.6 = (bf16[256,512]{1,0:T(8,128)(2,1)S(1)}, bf16[256,512]{1,0:T(8,128)(2,1)S(1)}, u32[]{:S(2)}, u32[]{:S(2)}) collective-permute-start(bf16[256,512]{1,0:T(8,128)(2,1)S(1)} %pad_maximum_fusion.refs_1_), channel_id=1, source_target_pairs={{0,6},{2,0},{4,2},{6,4},{1,7},{3,1},{5,3},{7,5},{8,14},{10,8},{12,... | collective-permute-start | bytes 786440 | tf_op jit(solution)/shard_map/ppermute | solution.py:1047
  21.8 37.2 %collective-permute-start.5 = (bf16[256,512]{1,0:T(8,128)(2,1)S(1)}, bf16[256,512]{1,0:T(8,128)(2,1)S(1)}, u32[]{:S(2)}, u32[]{:S(2)}) collective-permute-start(bf16[256,512]{1,0:T(8,128)(2,1)S(1)} %pad_maximum_fusion.refs_1_), channel_id=1, source_target_pairs={{0,4},{2,6},{4,0},{6,2},{1,5},{3,7},{5,1},{7,3},{8,12},{10,14},{12... | collective-permute-start | bytes 786440 | tf_op jit(solution)/shard_map/ppermute | solution.py:1047
  21.8 37.2 %collective-permute-start.4 = (bf16[256,512]{1,0:T(8,128)(2,1)S(1)}, bf16[256,512]{1,0:T(8,128)(2,1)S(1)}, u32[]{:S(2)}, u32[]{:S(2)}) collective-permute-start(bf16[256,512]{1,0:T(8,128)(2,1)S(1)} %pad_maximum_fusion.refs_1_), channel_id=1, source_target_pairs={{0,2},{2,4},{4,6},{6,0},{1,3},{3,5},{5,7},{7,1},{8,10},{10,12},{12... | collective-permute-start | bytes 786440 | tf_op jit(solution)/shard_map/ppermute | solution.py:1047
  33.7 25.9 %collective-permute-start.2 = (bf16[2,256,1024]{2,1,0:T(8,128)(2,1)}, bf16[2,256,1024]{2,1,0:T(8,128)(2,1)}, u32[]{:S(2)}, u32[]{:S(2)}) collective-permute-start(bf16[2,256,1024]{2,1,0:T(8,128)(2,1)} %collective-permute-done.refs_5_.refs_2_), channel_id=1, source_target_pairs={{0,16},{1,9},{2,18},{3,11},{4,20},{5,13},{6,22},{7,15},{8,24},{9,1... | collective-permute-start | bytes 3145736 | tf_op jit(solution)/shard_map/ppermute | solution.py:1026
  60.6 38.8 %collective-permute-start.12 = (bf16[1024,512]{1,0:T(8,128)(2,1)}, bf16[1024,512]{1,0:T(8,128)(2,1)}, u32[]{:S(2)}, u32[]{:S(2)}) collective-permute-start(bf16[1024,512]{1,0:T(8,128)(2,1)} %hold.4.refs_6_.refs_2_.refs_10_), channel_id=1, source_target_pairs={{0,16},{1,9},{2,18},{3,11},{4,20},{5,13},{6,22},{7,15},{8,24},{9,1... | collective-permute-start | bytes 3145736 | tf_op jit(solution)/shard_map/ppermute | solution.py:1026
  61.0 36.6 %collective-permute-start.11 = (bf16[1024,512]{1,0:T(8,128)(2,1)}, bf16[1024,512]{1,0:T(8,128)(2,1)}, u32[]{:S(2)}, u32[]{:S(2)}) collective-permute-start(bf16[1024,512]{1,0:T(8,128)(2,1)} %hold.4.refs_6_.refs_2_.refs_10_), channel_id=1, source_target_pairs={{0,8},{1,17},{2,10},{3,19},{4,12},{5,21},{6,14},{7,23},{8,0},{9,25... | collective-permute-start | bytes 3145736 | tf_op jit(solution)/shard_map/ppermute | solution.py:1026
  63.3 59.9 %all-gather.5.cloned.1.call-start = ((), (), s32[]{:S(2)}) async-start(), calls=%async_computation.2 | async-start | bytes 2359296 | tf_op jit(solution)/shard_map/all_gather | solution.py:1137
  66.5 235.9 %reduce-scatter.3.cloned.1.call-start = ((), (), s32[]{:S(2)}) async-start(), calls=%async_computation.4 | async-start | bytes 2654208 | tf_op jit(solution)/shard_map/reduce_scatter | solution.py:1216
  97.6 35.1 %collective-permute-start.13 = (bf16[1024,512]{1,0:T(8,128)(2,1)}, bf16[1024,512]{1,0:T(8,128)(2,1)}, u32[]{:S(2)}, u32[]{:S(2)}) collective-permute-start(bf16[1024,512]{1,0:T(8,128)(2,1)} %collective-permute-done.11.refs_4_.refs_3_.refs_11_), channel_id=1, source_target_pairs={{0,16},{1,9},{2,18},{3,11},{4,20},{5,13},{6,22},{7,15},{8,24},{9,1... | collective-permute-start | bytes 3145736 | tf_op jit(solution)/shard_map/ppermute | solution.py:1026
  112.7 19.4 %collective-permute-start.14 = (bf16[512,1024]{1,0:T(8,128)(2,1)}, bf16[512,1024]{1,0:T(8,128)(2,1)}, u32[]{:S(2)}, u32[]{:S(2)}) collective-permute-start(bf16[512,1024]{1,0:T(8,128)(2,1)} %hold.7.refs_4_.refs_6_), channel_id=1, source_target_pairs={{0,8},{1,17},{2,10},{3,19},{4,12},{5,21},{6,14},{7,23},{8,0},{9,25... | collective-permute-start | bytes 3145736 | tf_op jit(solution)/shard_map/ppermute | solution.py:1026
  132.1 24.8 %collective-permute-start.16 = (bf16[512,1024]{1,0:T(8,128)(2,1)}, bf16[512,1024]{1,0:T(8,128)(2,1)S(1)}, u32[]{:S(2)}, u32[]{:S(2)}) collective-permute-start(bf16[512,1024]{1,0:T(8,128)(2,1)} %collective-permute-done.14.refs_10_.refs_5_.refs_7_), channel_id=1, source_target_pairs={{0,16},{1,9},{2,18},{3,11},{4,20},{5,13},{6,22},{7,15},{8,24},{9,1... | collective-permute-start | bytes 3145736 | tf_op jit(solution)/shard_map/ppermute | solution.py:1026
  182.4 32.1 %collective-permute-start.23 = (bf16[2,512,1024]{2,1,0:T(8,128)(2,1)}, bf16[2,512,1024]{2,1,0:T(8,128)(2,1)}, u32[]{:S(2)}, u32[]{:S(2)}) collective-permute-start(bf16[2,512,1024]{2,1,0:T(8,128)(2,1)} %down_grad.3.refs_0_), channel_id=1, source_target_pairs={{0,8},{1,17},{2,10},{3,19},{4,12},{5,21},{6,14},{7,23},{8,0},{9,25... | collective-permute-start | bytes 6291464 | tf_op jit(solution)/shard_map/ppermute | solution.py:1026
  210.9 19.3 %collective-permute-start.20 = (bf16[2,256,256]{2,1,0:T(8,128)(2,1)}, bf16[2,256,256]{2,1,0:T(8,128)(2,1)S(1)}, u32[]{:S(2)}, u32[]{:S(2)}) collective-permute-start(bf16[2,256,256]{2,1,0:T(8,128)(2,1)} %get-tuple-element.84), channel_id=1, source_target_pairs={{0,8},{1,17},{2,10},{3,19},{4,12},{5,21},{6,14},{7,23},{8,0},{9,25... | collective-permute-start | bytes 786440 | tf_op jit(solution)/shard_map/ppermute | solution.py:1043
  211.8 18.3 %collective-permute-start.21 = (bf16[2,256,256]{2,1,0:T(8,128)(2,1)}, bf16[2,256,256]{2,1,0:T(8,128)(2,1)S(1)}, u32[]{:S(2)}, u32[]{:S(2)}) collective-permute-start(bf16[2,256,256]{2,1,0:T(8,128)(2,1)} %get-tuple-element.85), channel_id=1, source_target_pairs={{0,16},{1,9},{2,18},{3,11},{4,20},{5,13},{6,22},{7,15},{8,24},{9,1... | collective-permute-start | bytes 786440 | tf_op jit(solution)/shard_map/ppermute | solution.py:1043
  212.9 17.3 %collective-permute-start.22 = (bf16[2,256,256]{2,1,0:T(8,128)(2,1)}, bf16[2,256,256]{2,1,0:T(8,128)(2,1)S(1)}, u32[]{:S(2)}, u32[]{:S(2)}) collective-permute-start(bf16[2,256,256]{2,1,0:T(8,128)(2,1)} %get-tuple-element.86), channel_id=1, source_target_pairs={{0,24},{1,25},{2,26},{3,27},{4,28},{5,29},{6,30},{7,31},{8,16},{9,... | collective-permute-start | bytes 786440 | tf_op jit(solution)/shard_map/ppermute | solution.py:1043
  219.6 27.7 %collective-permute-start.25 = (bf16[1,512,1024]{2,1,0:T(8,128)(2,1)}, bf16[1,512,1024]{2,1,0:T(8,128)(2,1)}, u32[]{:S(2)}, u32[]{:S(2)}) collective-permute-start(bf16[1,512,1024]{2,1,0:T(8,128)(2,1)} %down_grad.4.refs_4_), channel_id=1, source_target_pairs={{0,16},{1,9},{2,18},{3,11},{4,20},{5,13},{6,22},{7,15},{8,24},{9,1... | collective-permute-start | bytes 3145736 | tf_op jit(solution)/shard_map/ppermute | solution.py:1026
  226.1 33.6 %collective-permute-start.24 = (bf16[2,1024,512]{2,1,0:T(8,128)(2,1)}, bf16[2,1024,512]{2,1,0:T(8,128)(2,1)}, u32[]{:S(2)}, u32[]{:S(2)}) collective-permute-start(bf16[2,1024,512]{2,1,0:T(8,128)(2,1)} %up_grad.3.refs_7_), channel_id=1, source_target_pairs={{0,8},{1,17},{2,10},{3,19},{4,12},{5,21},{6,14},{7,23},{8,0},{9,25... | collective-permute-start | bytes 6291464 | tf_op jit(solution)/shard_map/ppermute | solution.py:1026
  230.1 119.0 %reduce-scatter.5.cloned.1.call-start = ((), (), s32[]{:S(2)}) async-start(), calls=%async_computation.5 | async-start | bytes 1990656 | tf_op jit(solution)/shard_map/reduce_scatter | solution.py:1245
  251.4 23.1 %collective-permute-start.27 = (bf16[128,1024]{1,0:T(8,128)(2,1)S(1)}, bf16[128,1024]{1,0:T(8,128)(2,1)S(1)}, u32[]{:S(2)}, u32[]{:S(2)}) collective-permute-start(bf16[128,1024]{1,0:T(8,128)(2,1)S(1)} %get-tuple-element.97), channel_id=1, source_target_pairs={{0,2},{2,4},{4,6},{6,0},{1,3},{3,5},{5,7},{7,1},{8,10},{10,12},{12... | collective-permute-start | bytes 786440 | tf_op jit(solution)/shard_map/ppermute | solution.py:1047
  252.9 25.8 %collective-permute-start.28 = (bf16[128,1024]{1,0:T(8,128)(2,1)S(1)}, bf16[128,1024]{1,0:T(8,128)(2,1)S(1)}, u32[]{:S(2)}, u32[]{:S(2)}) collective-permute-start(bf16[128,1024]{1,0:T(8,128)(2,1)S(1)} %get-tuple-element.98), channel_id=1, source_target_pairs={{0,4},{2,6},{4,0},{6,2},{1,5},{3,7},{5,1},{7,3},{8,12},{10,14},{12... | collective-permute-start | bytes 786440 | tf_op jit(solution)/shard_map/ppermute | solution.py:1047
  253.9 24.9 %collective-permute-start.29 = (bf16[128,1024]{1,0:T(8,128)(2,1)S(1)}, bf16[128,1024]{1,0:T(8,128)(2,1)S(1)}, u32[]{:S(2)}, u32[]{:S(2)}) collective-permute-start(bf16[128,1024]{1,0:T(8,128)(2,1)S(1)} %get-tuple-element.99), channel_id=1, source_target_pairs={{0,6},{2,0},{4,2},{6,4},{1,7},{3,1},{5,3},{7,5},{8,14},{10,8},{12,... | collective-permute-start | bytes 786440 | tf_op jit(solution)/shard_map/ppermute | solution.py:1047
  279.9 21.3 %collective-permute-start.35 = (bf16[128,1024]{1,0:T(8,128)(2,1)}, bf16[128,1024]{1,0:T(8,128)(2,1)}, u32[]{:S(2)}, u32[]{:S(2)}) collective-permute-start(bf16[128,1024]{1,0:T(8,128)(2,1)} %total_rows.1.refs_5_.refs_1_), channel_id=1, source_target_pairs={{0,16},{1,9},{2,18},{3,11},{4,20},{5,13},{6,22},{7,15},{8,24},{9,1... | collective-permute-start | bytes 786440 | tf_op jit(solution)/shard_map/ppermute | solution.py:1026
  287.3 24.6 %collective-permute-start.32 = (bf16[256,512]{1,0:T(8,128)(2,1)}, bf16[256,512]{1,0:T(8,128)(2,1)S(1)}, u32[]{:S(2)}, u32[]{:S(2)}) collective-permute-start(bf16[256,512]{1,0:T(8,128)(2,1)} %get-tuple-element.101), channel_id=1, source_target_pairs={{0,2},{2,4},{4,6},{6,0},{1,3},{3,5},{5,7},{7,1},{8,10},{10,12},{12... | collective-permute-start | bytes 786440 | tf_op jit(solution)/shard_map/ppermute | solution.py:1047
  293.2 19.4 %collective-permute-start.33 = (bf16[256,512]{1,0:T(8,128)(2,1)}, bf16[256,512]{1,0:T(8,128)(2,1)}, u32[]{:S(2)}, u32[]{:S(2)}) collective-permute-start(bf16[256,512]{1,0:T(8,128)(2,1)} %get-tuple-element.102), channel_id=1, source_target_pairs={{0,4},{2,6},{4,0},{6,2},{1,5},{3,7},{5,1},{7,3},{8,12},{10,14},{12... | collective-permute-start | bytes 786440 | tf_op jit(solution)/shard_map/ppermute | solution.py:1047
  295.4 17.2 %collective-permute-start.34 = (bf16[256,512]{1,0:T(8,128)(2,1)}, bf16[256,512]{1,0:T(8,128)(2,1)}, u32[]{:S(2)}, u32[]{:S(2)}) collective-permute-start(bf16[256,512]{1,0:T(8,128)(2,1)} %get-tuple-element.103), channel_id=1, source_target_pairs={{0,6},{2,0},{4,2},{6,4},{1,7},{3,1},{5,3},{7,5},{8,14},{10,8},{12,... | collective-permute-start | bytes 786440 | tf_op jit(solution)/shard_map/ppermute | solution.py:1047
  301.2 41.0 %collective-permute-start.31 = (bf16[2,2,256,1024]{3,2,1,0:T(8,128)(2,1)}, bf16[2,2,256,1024]{3,2,1,0:T(8,128)(2,1)}, u32[]{:S(2)}, u32[]{:S(2)}) collective-permute-start(bf16[2,2,256,1024]{3,2,1,0:T(8,128)(2,1)} %hidden_grad.3.refs_6_), channel_id=1, source_target_pairs={{0,8},{1,17},{2,10},{3,19},{4,12},{5,21},{6,14},{7,23},{8,0},{9,25... | collective-permute-start | bytes 6291464 | tf_op jit(solution)/shard_map/ppermute | solution.py:1026
  323.0 17.2 %collective-permute-start.44 = (bf16[2,128,512]{2,1,0:T(8,128)(2,1)S(1)}, bf16[2,128,512]{2,1,0:T(8,128)(2,1)}, u32[]{:S(2)}, u32[]{:S(2)}) collective-permute-start(bf16[2,128,512]{2,1,0:T(8,128)(2,1)S(1)} %pair.1.refs_4_.refs_1_), channel_id=1, source_target_pairs={{0,8},{1,17},{2,10},{3,19},{4,12},{5,21},{6,14},{7,23},{8,0},{9,25... | collective-permute-start | bytes 786440 | tf_op jit(solution)/shard_map/ppermute | solution.py:1026
  324.3 25.3 %collective-permute-start.45 = (bf16[2,128,512]{2,1,0:T(8,128)(2,1)S(1)}, bf16[2,128,512]{2,1,0:T(8,128)(2,1)}, u32[]{:S(2)}, u32[]{:S(2)}) collective-permute-start(bf16[2,128,512]{2,1,0:T(8,128)(2,1)S(1)} %pair.1.refs_4_.refs_1_), channel_id=1, source_target_pairs={{0,16},{1,9},{2,18},{3,11},{4,20},{5,13},{6,22},{7,15},{8,24},{9,1... | collective-permute-start | bytes 786440 | tf_op jit(solution)/shard_map/ppermute | solution.py:1026
  (83 other events, 866.0 us)
Sparse Core Ops, SparseCore 0:
  15.2 44.7 all-gather.8
  63.4 28.9 all-gather.6
  94.6 28.5 all-gather.4
  230.2 41.2 reduce-scatter.2
  312.0 33.8 reduce-scatter.4

commit v4 on v3

--- a/solution.py
+++ b/solution.py
@@ -117,22 +117,19 @@
     def kernel(place_ref, weight_ref, bias_ref, scale_ref, *refs):
         for q in range(ranks):
 
-            @pl.when(pl.program_id(0) // seqs == q)
+            @pl.when(pl.program_id(0) == q)
             def _(q=q):
                 whole = weight_ref[:, :rows, :].reshape(width, out_width)
-                product = dot(refs[q][0], whole, 1, 0) + bias_ref[...]
-                refs[ranks][0] = (product * scale_ref[...]).astype(jnp.bfloat16)
-
-    def source(q):
-        return lambda i, p: (jnp.clip(i - q * seqs, 0, seqs - 1), 0, 0)
+                product = dot(refs[q][...].reshape(seqs * length, width), whole, 1, 0) + bias_ref[...]
+                product = (product * scale_ref[...]).astype(jnp.bfloat16)
+                refs[ranks][...] = product.reshape(seqs, length, out_width)
 
     return run(
         kernel,
         "project",
-        (ranks * seqs,),
-        [fixed(weight), fixed(bias), fixed(scale)]
-        + [blocks[q].spec((1, length, width), source(q)) for q in range(ranks)],
-        pl.BlockSpec((1, length, out_width), lambda i, p: (i % seqs, p[i // seqs], 0)),
+        (ranks,),
+        [fixed(weight), fixed(bias), fixed(scale)] + [block.whole() for block in blocks],
+        pl.BlockSpec((seqs, length, out_width), lambda i, p: (0, p[i], 0)),
         kind_of((seqs, length * ranks, out_width)),
         [weight, bias, scale, *arrays(blocks)],
         prefetch=(places,),
@@ -276,7 +273,7 @@
     blocks = len(slopes)
     count, width = own.shape
     units = slopes[0].shape[1]
-    tile = min(TILE, count)
+    tile = min(2 * TILE, count)
     half = count // tile
 
     def kernel(own_ref, other_ref, *refs):
@@ -511,7 +508,7 @@
     ranks = len(blocks)
     out_width = dqkv.shape[2]
     rows = width // owners
-    group = max(1, TILE // rows)
+    group = max(1, min(owners, 2 * TILE // rows))
 
     def kernel(place_ref, *refs):
         dqkv_ref, out_ref, total_ref = refs[ranks:]

time: 379 us -> 381 us (level)
    ppermute x26, waiting for transfers between devices: 45.3 us -> 49.8 us  [hop(): return lax.ppermute(block, AXES, pairs)]
    ppermute x9, waiting for transfers between devices: 27.8 us -> 23.6 us  [shift(): lax.ppermute(block, 'z', [(z, (z + d) % self.chips) for z in range(self.c...]
  transfers between devices with their start and end apart: 52 -> 52, of which waited for: 19 -> 19; matrix products, arithmetic and copies ran while one was open for 4% -> 4% of each run, Pallas kernels for 41% -> 40%
where the time goes in v4:
time: 381 us; the launch traced here: 375 us
  Pallas kernels  167 us (44%)
  waiting for transfers between devices  98.1 us (26%)
  starting transfers between devices  56.6 us (15%)
  local copies, waits for them, and re-layouts  32.7 us (9%)
  between operations  14.7 us (4%)
  other arithmetic  5.79 us (2%)
    pallas_call x38, Pallas kernels, run(): pl.pallas_call(waiting, grid_spec=pltpu.PrefetchScalarGridSpec(num_scalar...  167 us
    ppermute x26, waiting for transfers between devices, hop(): return lax.ppermute(block, AXES, pairs)  49.8 us
    ppermute x26, starting transfers between devices, hop(): return lax.ppermute(block, AXES, pairs)  31.2 us
    ppermute x9, waiting for transfers between devices, shift(): lax.ppermute(block, 'z', [(z, (z + d) % self.chips) for z in range(self.c...  23.6 us
    unnamed x128, local copies, waits for them, and re-layouts  23.1 us
    ppermute x9, starting transfers between devices, shift(): lax.ppermute(block, 'z', [(z, (z + d) % self.chips) for z in range(self.c...  17.6 us
    all_gather x1, waiting for transfers between devices, local(): lax.all_gather(hold(out_weight, (down_rows,)), ROWS, axis=0, tiled=True)  11 us
    ppermute x6, waiting for transfers between devices, exchange(): out.append(lax.ppermute(blocks[q], AXES, pairs))  10.8 us
  transfers between devices with their start and end apart: 52, of which 19 were waited for; matrix products, arithmetic and copies ran while one was open for 4% of the time, Pallas kernels for 40%

profile of v4, /device:TPU:0, one launch (start us, length us, event | category | flops | bytes accessed | tf_op | source)
XLA Modules:
  0.0 375.0 jit_solution(11378644003177979008)
XLA Ops:
  18.1 3.7 collective-permute-start.6
  23.3 10.5 %collective-permute-done.refs_5_.refs_2_ = bf16[2,256,1024]{2,1,0:T(8,128)(2,1)} collective-permute-done((bf16[2,256,1024]{2,1,0:T(8,128)(2,1)}, bf16[2,256,1024]{2,1,0:T(8,128)(2,1)}, u32[]{:S(2)}, u32[]{:S(2)}) %collective-permute-start) | collective-permute-done | bytes 1048608 | tf_op jit(solution)/shard_map/ppermute | solution.py:1023
  35.5 23.5 %collective-permute-done.5.refs_3_ = bf16[256,512]{1,0:T(8,128)(2,1)S(1)} collective-permute-done((bf16[256,512]{1,0:T(8,128)(2,1)S(1)}, bf16[256,512]{1,0:T(8,128)(2,1)S(1)}, u32[]{:S(2)}, u32[]{:S(2)}) %collective-permute-start.5) | collective-permute-done | bytes 262176 | tf_op jit(solution)/shard_map/ppermute | solution.py:1044
  66.5 8.0 %project.1.refs_3_ = bf16[2,1024,768]{2,1,0:T(8,128)(2,1)} custom-call(s32[4]{0:T(128)S(1)} %pad_add_fusion.1.refs_0_.refs_2_, bf16[8,144,768]{2,1,0:T(8,128)(2,1)} %bitcast.80, f32[1,768]{1,0:T(1,128)S(1)} %broadcast_in_dim.133.refs_2_, f32[1,768]{1,0:T(1,128)S(1)} %compare_select_fusion.refs_3_, bf16[2,256,1024]{2,1,0:T(8,128)(2,1)S(1)} %copy-done.11, ...), custom_call_target="tpu_custom_call" | custom-call | flops 30000001024 | bytes 1000 | tf_op jit(solution)/shard_map/project/pallas_call | solution.py:36
  74.5 16.3 %attention_forward.1 = (bf16[2,1024,256]{2,1,0:T(8,128)(2,1)S(1)}, f32[2,4,1024]{2,1,0:T(4,128)S(1)}, bf16[2,256,256]{2,1,0:T(8,128)(2,1)S(1)}, bf16[2,256,256]{...) custom-call(s32[2]{0:T(128)S(1)} %select_select_fusion.refs_0_, ...), custom_call_target="tpu_custom_call" | custom-call | flops 299999985664 | bytes 1000 | tf_op jit(solution)/shard_map/attention_forward/pallas_call | solution.py:36
  97.3 3.7 collective-permute-done.7.refs_2_.refs_1_
  101.5 6.6 %collective-permute-done.9.refs_4_.refs_3_ = bf16[2,256,256]{2,1,0:T(8,128)(2,1)S(1)} collective-permute-done((bf16[2,256,256]{2,1,0:T(8,128)(2,1)S(1)}, bf16[2,256,256]{2,1,0:T(8,128)(2,1)S(1)}, u32[]{:S(2)}, u32[]{:S(2)}) %collective-permute-start.9) | collective-permute-done | bytes 262176 | tf_op jit(solution)/shard_map/ppermute | solution.py:1040
  112.2 11.0 %all-gather.5.cloned.1.call-done.refs_5_.refs_6_ = bf16[1024,1024]{1,0:T(8,128)(2,1)} async-done(((bf16[128,1024]{1,0:T(8,128)(2,1)}), bf16[1024,1024]{1,0:T(8,128)(2,1)}) %all-gather.5.cloned.1.call-update) | async-done | bytes 2097168 | tf_op jit(solution)/shard_map/all_gather | solution.py:1134
  123.3 4.5 %out_norm.1 = (bf16[2,256,1024]{2,1,0:T(8,128)(2,1)S(1)}, bf16[2,256,1024]{2,1,0:T(8,128)(2,1)S(1)}) custom-call(s32[4]{0:T(128)S(1)} %pad_add_fusion.1.refs_0_.refs_2_, bf16[2,256,256]{2,1,0:T(8,128)(2,1)S(1)} %get-tuple-element.64.refs_1_, bf16[2,256,256]{2,1,0:T(8,128)(2,1)S(1)} %collective-permute-done.7.refs_2_.refs_1_, ...), custom_call_target="tpu_custom_call" | custom-call | flops 30000001024 | bytes 1000 | tf_op jit(solution)/shard_map/out_norm/pallas_call | solution.py:36
  132.7 11.6 %up_forward.1 = (bf16[1024,512]{1,0:T(8,128)(2,1)S(1)}, bf16[1024,512]{1,0:T(8,128)(2,1)S(1)}, bf16[1024,512]{1,0:T(8,128)(2,1)S(1)}, bf16[1024,512]{1,0:T(8,128...) custom-call(bf16[512,1024]{1,0:T(8,128)(2,1)} %bitcast.86, ...), custom_call_target="tpu_custom_call" | custom-call | flops 30000001024 | bytes 1000 | tf_op jit(solution)/shard_map/up_forward/pallas_call | solution.py:36
  145.7 11.2 %collective-permute-done.16.refs_7_.refs_9_ = bf16[512,1024]{1,0:T(8,128)(2,1)S(1)} collective-permute-done((bf16[512,1024]{1,0:T(8,128)(2,1)}, bf16[512,1024]{1,0:T(8,128)(2,1)S(1)}, u32[]{:S(2)}, u32[]{:S(2)}) %collective-permute-start.16) | collective-permute-done | bytes 1048608 | tf_op jit(solution)/shard_map/ppermute | solution.py:1023
  157.9 4.9 %down_forward.2.refs_8_ = bf16[512,1024]{1,0:T(8,128)(2,1)S(1)} custom-call(bf16[1024,512]{1,0:T(8,128)(2,1)S(1)} %get-tuple-element.69.refs_0_.refs_2_, bf16[1024,512]{1,0:T(8,128)(2,1)S(1)} %get-tuple-element.70.refs_1_.refs_2_, bf16[1024,512]{1,0:T(8,128)(2,1)} %copy-done.48, bf16[1024,512]{1,0:T(8,128)(2,1)} %get-tuple-element.72.refs_3_, ...), custom_call_target="tpu_custom_call" | custom-call | flops 30000001024 | bytes 1000 | tf_op jit(solution)/shard_map/down_forward/pallas_call | solution.py:36
  163.8 4.9 %down_forward.3 = bf16[512,1024]{1,0:T(8,128)(2,1)S(1)} custom-call(bf16[1024,512]{1,0:T(8,128)(2,1)S(1)} %get-tuple-element.69.refs_0_.refs_2_, bf16[1024,512]{1,0:T(8,128)(2,1)S(1)} %get-tuple-element.70.refs_1_.refs_2_, bf16[1024,512]{1,0:T(8,128)(2,1)} %copy-done.48, bf16[1024,512]{1,0:T(8,128)(2,1)} %get-tuple-element.72.refs_3_, ...), custom_call_target="tpu_custom_call" | custom-call | flops 30000001024 | bytes 1000 | tf_op jit(solution)/shard_map/down_forward/pallas_call | solution.py:36
  168.7 4.8 %norm_two.1 = (bf16[2,256,1024]{2,1,0:T(8,128)(2,1)}, bf16[2,256,1024]{2,1,0:T(8,128)(2,1)S(1)}, f32[8,1024]{1,0:T(8,128)S(1)}) custom-call(bf16[2,256,1024]{2,1,0:T(8,128)(2,1)S(1)} %bitcast.97, bf16[2,256,1024]{2,1,0:T(8,128)(2,1)S(1)} %bitcast.95, bf16[2,256,1024]{2,1,0:T(8,128)(2,1)} %copy-done.51, f32[16,1024]{1,0:T(8,128)S(1)} %bitcast.77, ...), custom_call_target="tpu_custom_call" | custom-call | flops 30000001024 | bytes 1000 | tf_op jit(solution)/shard_map/norm_two/pallas_call | solution.py:36
  177.5 5.0 %down_grad.3.refs_0_ = bf16[2,512,1024]{2,1,0:T(8,128)(2,1)} custom-call(bf16[512,1024]{1,0:T(8,128)(2,1)S(1)} %bitcast.91, bf16[512,1024]{1,0:T(8,128)(2,1)} %collective-permute-done.18.refs_1_, bf16[1024,512]{1,0:T(8,128)(2,1)S(1)} %copy-done.50, bf16[1024,512]{1,0:T(8,128)(2,1)} %get-tuple-element.72.refs_3_), custom_call_target="tpu_custom_call" | custom-call | flops 30000001024 | bytes 1000 | tf_op jit(solution)/shard_map/down_grad/pallas_call | solution.py:36
  183.9 15.7 %feed_forward_back.1 = (bf16[1024,512]{1,0:T(8,128)(2,1)S(1)}, bf16[1024,512]{1,0:T(8,128)(2,1)S(1)}, bf16[1024,512]{1,0:T(8,128)(2,1)S(1)}, bf16[1024,512]{1,0:...) custom-call(bf16[512,1024]{1,0:T(8,128)(2,1)} %bitcast.92, ...), custom_call_target="tpu_custom_call" | custom-call | flops 30000001024 | bytes 1000 | tf_op jit(solution)/shard_map/feed_forward_back/pallas_call | solution.py:36
  203.6 6.6 %norm_one_back.1 = (bf16[2,256,1024]{2,1,0:T(8,128)(2,1)S(1)}, bf16[2,256,256]{2,1,0:T(8,128)(2,1)S(1)}, bf16[2,256,256]{2,1,0:T(8,128)(2,1)}, bf16[2,256,256]{2...) custom-call(s32[4]{0:T(128)S(1)} %pad_add_fusion.1.refs_0_.refs_2_, ...), custom_call_target="tpu_custom_call" | custom-call | flops 30000001024 | bytes 1000 | tf_op jit(solution)/shard_map/norm_one_back/pallas_call | solution.py:36
  215.7 3.9 %down_grad.4.refs_4_ = bf16[1,512,1024]{2,1,0:T(8,128)(2,1)} custom-call(bf16[512,1024]{1,0:T(8,128)(2,1)S(1)} %bitcast.93, bf16[512,1024]{1,0:T(8,128)(2,1)} %collective-permute-done.18.refs_1_, bf16[1024,512]{1,0:T(8,128)(2,1)} %copy-done.48, bf16[2,512,1024]{2,1,0:T(8,128)(2,1)} %collective-permute-done.23.refs_3_, f32[8,128]{1,0:T(8,128)S(1)} %tick.5.refs_4_), custom_call_target="tpu_custom_call" | custom-call | flops 30000001024 | bytes 1000 | tf_op jit(solution)/shard_map/down_grad/pallas_call | solution.py:36
  221.1 5.1 %up_grad.3.refs_7_ = bf16[2,1024,512]{2,1,0:T(8,128)(2,1)} custom-call(bf16[512,1024]{1,0:T(8,128)(2,1)S(1)} %bitcast.87, bf16[512,1024]{1,0:T(8,128)(2,1)} %collective-permute-done.10.refs_1_, bf16[1024,512]{1,0:T(8,128)(2,1)S(1)} %copy-done.43, bf16[1024,512]{1,0:T(8,128)(2,1)} %get-tuple-element.94.refs_3_, bf16[1,512,1024]{2,1,0:T(8,128)(2,1)} %down_grad.4.refs_4_), custom_call_target="tpu_custom_call" | custom-call | flops 30000001024 | bytes 1000 | tf_op jit(solution)/shard_map/up_grad/pallas_call | solution.py:36
  232.3 10.6 %attention_backward.2.refs_5_.refs_12_ = bf16[2,1024,768]{2,1,0:T(8,128)(2,1)} custom-call(s32[2]{0:T(128)S(1)} %copy-done.35, s32[2,4]{1,0:T(2,128)S(1)} %get-tuple-element.114.refs_1_, s32[4]{0:T(128)S(1)} %pad_add_fusion.1.refs_0_.refs_2_, bf16[2,1024,768]{2,1,0:T(8,128)(2,1)} %project.1.refs_3_, bf16[2,256,256]{2,1,0:T(8,128)(2,1)S(1)} %copy-done.53, ...), custom_call_target="tpu_custom_call" | custom-call | flops 30000001024 | bytes 1000 | tf_op jit(solution)/shard_map/attention_backward/pallas_call | solution.py:36
  242.8 4.5 %collective-permute-done.25.refs_4_ = bf16[1,512,1024]{2,1,0:T(8,128)(2,1)} collective-permute-done((bf16[1,512,1024]{2,1,0:T(8,128)(2,1)}, bf16[1,512,1024]{2,1,0:T(8,128)(2,1)}, u32[]{:S(2)}, u32[]{:S(2)}) %collective-permute-start.25) | collective-permute-done | bytes 1048608 | tf_op jit(solution)/shard_map/ppermute | solution.py:1023
  247.3 3.5 down_grad.5
  256.3 3.5 collective-permute-done.24.refs_3_
  264.0 14.9 %attention_backward.3.refs_4_.refs_2_.refs_3_.refs_5_ = bf16[2,1024,768]{2,1,0:T(8,128)(2,1)} custom-call(s32[2]{0:T(128)S(1)} %copy-done.35, s32[2,4]{1,0:T(2,128)S(1)} %get-tuple-element.114.refs_1_, s32[4]{0:T(128)S(1)} %pad_add_fusion.1.refs_0_.refs_2_, bf16[2,1024,768]{2,1,0:T(8,128)(2,1)} %project.1.refs_3_, ...), custom_call_target="tpu_custom_call", output_to_operand_aliasing={{}: (12, {})} | custom-call | flops 30000001024 | bytes 1000 | tf_op jit(solution)/shard_map/attention_backward/pallas_call | solution.py:36
  287.4 5.6 %collective-permute-start.32 = (bf16[256,512]{1,0:T(8,128)(2,1)}, bf16[256,512]{1,0:T(8,128)(2,1)S(1)}, u32[]{:S(2)}, u32[]{:S(2)}) collective-permute-start(bf16[256,512]{1,0:T(8,128)(2,1)} %get-tuple-element.101), channel_id=1, source_target_pairs={{0,2},{2,4},{4,6},{6,0},{1,3},{3,5},{5,7},{7,1},{8,10},{10,12},{12... | collective-permute-start | bytes 786440 | tf_op jit(solution)/shard_map/ppermute | solution.py:1044
  296.3 4.7 %hidden_grad.3.refs_6_ = bf16[2,2,256,1024]{3,2,1,0:T(8,128)(2,1)} custom-call(s32[4]{0:T(128)S(1)} %copy-done.10, bf16[8,144,768]{2,1,0:T(8,128)(2,1)S(1)} %bitcast.82, bf16[2,1024,768]{2,1,0:T(8,128)(2,1)} %attention_backward.3.refs_4_.refs_2_.refs_3_.refs_5_, bf16[2,1024,768]{2,1,0:T(8,128)(2,1)} %attention_backward.3.refs_4_.refs_2_.refs_3_.refs_5_, ...), custom_call_target="tpu_custom_call" | custom-call | flops 6000000000 | bytes 1000 | tf_op jit(solution)/shard_map/hidden_grad/pallas_call | solution.py:36
  303.6 8.2 %project_grad_pack.1.refs_5_ = bf16[8,144,768]{2,1,0:T(8,128)(2,1)} custom-call(s32[4]{0:T(128)S(1)} %copy-done.10, bf16[2,256,1024]{2,1,0:T(8,128)(2,1)S(1)} %copy-done.12, bf16[2,256,1024]{2,1,0:T(8,128)(2,1)} %collective-permute-done.refs_5_.refs_2_, bf16[2,256,1024]{2,1,0:T(8,128)(2,1)} %collective-permute-done.1.refs_6_.refs_3_, ...), custom_call_target="tpu_custom_call" | custom-call | flops 6000000000 | bytes 1000 | tf_op jit(solution)/shard_map/project_grad_pack/pallas_call | solution.py:36
  324.8 9.7 %collective-permute-done.42 = bf16[144,1024]{1,0:T(8,128)(2,1)S(1)} collective-permute-done((bf16[144,1024]{1,0:T(8,128)(2,1)S(1)}, bf16[144,1024]{1,0:T(8,128)(2,1)S(1)}, u32[]{:S(2)}, u32[]{:S(2)}) %collective-permute-start.42) | collective-permute-done | bytes 294944 | tf_op jit(solution)/shard_map/ppermute | solution.py:1023
  336.4 3.8 %collective-permute-done.44.refs_2_ = bf16[2,128,512]{2,1,0:T(8,128)(2,1)} collective-permute-done((bf16[2,128,512]{2,1,0:T(8,128)(2,1)S(1)}, bf16[2,128,512]{2,1,0:T(8,128)(2,1)}, u32[]{:S(2)}, u32[]{:S(2)}) %collective-permute-start.44) | collective-permute-done | bytes 262176 | tf_op jit(solution)/shard_map/ppermute | solution.py:1023
  342.0 3.8 %hidden_grad.4.refs_5_ = bf16[1,2,256,1024]{3,2,1,0:T(8,128)(2,1)} custom-call(s32[4]{0:T(128)S(1)} %copy-done.10, bf16[8,144,768]{2,1,0:T(8,128)(2,1)S(1)} %bitcast.83, bf16[2,1024,768]{2,1,0:T(8,128)(2,1)} %attention_backward.3.refs_4_.refs_2_.refs_3_.refs_5_, bf16[2,2,256,1024]{3,2,1,0:T(8,128)(2,1)} %collective-permute-done.31.refs_3_.refs_4_, ...), custom_call_target="tpu_custom_call" | custom-call | flops 6000000000 | bytes 1000 | tf_op jit(solution)/shard_map/hidden_grad/pallas_call | solution.py:36
  354.3 3.4 collective-permute-done.39.refs_2_
  360.7 4.1 %hidden_grad.5 = f32[1,2,256,1024]{3,2,1,0:T(8,128)} custom-call(s32[4]{0:T(128)S(1)} %copy-done.10, bf16[8,144,768]{2,1,0:T(8,128)(2,1)S(1)} %bitcast.84, bf16[2,1024,768]{2,1,0:T(8,128)(2,1)} %attention_backward.3.refs_4_.refs_2_.refs_3_.refs_5_, bf16[2,256,1024]{2,1,0:T(8,128)(2,1)S(1)} %copy-done.37, ...), custom_call_target="tpu_custom_call" | custom-call | flops 6000000000 | bytes 1000 | tf_op jit(solution)/shard_map/hidden_grad/pallas_call | solution.py:36
  (302 shorter events, 119.0 us)
Async XLA Ops:
  7.2 53.8 %all-gather.9.cloned.1.call-start = ((), (), s32[]{:S(2)}) async-start(), calls=%async_computation.6 | async-start | bytes 1990656 | tf_op jit(solution)/shard_map/all_gather | solution.py:1131
  7.3 59.3 %collective-permute-start.1 = (bf16[2,256,1024]{2,1,0:T(8,128)(2,1)}, bf16[2,256,1024]{2,1,0:T(8,128)(2,1)}, u32[]{:S(2)}, u32[]{:S(2)}) collective-permute-start(bf16[2,256,1024]{2,1,0:T(8,128)(2,1)} %refs_1_.1), channel_id=1, source_target_pairs={{0,16},{1,9},{2,18},{3,11},{4,20},{5,13},{6,22},{7,15},{8,24},{9,1... | collective-permute-start | bytes 3145736 | tf_op jit(solution)/shard_map/ppermute | solution.py:1023
  10.3 23.4 %collective-permute-start = (bf16[2,256,1024]{2,1,0:T(8,128)(2,1)}, bf16[2,256,1024]{2,1,0:T(8,128)(2,1)}, u32[]{:S(2)}, u32[]{:S(2)}) collective-permute-start(bf16[2,256,1024]{2,1,0:T(8,128)(2,1)} %refs_1_.1), channel_id=1, source_target_pairs={{0,8},{1,17},{2,10},{3,19},{4,12},{5,21},{6,14},{7,23},{8,0},{9,25... | collective-permute-start | bytes 3145736 | tf_op jit(solution)/shard_map/ppermute | solution.py:1023
  15.1 93.1 %all-gather.7.cloned.1.call-start = ((), (), s32[]{:S(2)}) async-start(), calls=%async_computation.3 | async-start | bytes 1310720 | tf_op jit(solution)/shard_map/all_gather | solution.py:1133
  18.1 17.4 %collective-permute-start.6 = (bf16[256,512]{1,0:T(8,128)(2,1)S(1)}, bf16[256,512]{1,0:T(8,128)(2,1)S(1)}, u32[]{:S(2)}, u32[]{:S(2)}) collective-permute-start(bf16[256,512]{1,0:T(8,128)(2,1)S(1)} %pad_maximum_fusion.refs_1_), channel_id=1, source_target_pairs={{0,6},{2,0},{4,2},{6,4},{1,7},{3,1},{5,3},{7,5},{8,14},{10,8},{12,... | collective-permute-start | bytes 786440 | tf_op jit(solution)/shard_map/ppermute | solution.py:1044
  21.8 37.2 %collective-permute-start.5 = (bf16[256,512]{1,0:T(8,128)(2,1)S(1)}, bf16[256,512]{1,0:T(8,128)(2,1)S(1)}, u32[]{:S(2)}, u32[]{:S(2)}) collective-permute-start(bf16[256,512]{1,0:T(8,128)(2,1)S(1)} %pad_maximum_fusion.refs_1_), channel_id=1, source_target_pairs={{0,4},{2,6},{4,0},{6,2},{1,5},{3,7},{5,1},{7,3},{8,12},{10,14},{12... | collective-permute-start | bytes 786440 | tf_op jit(solution)/shard_map/ppermute | solution.py:1044
  21.8 37.2 %collective-permute-start.4 = (bf16[256,512]{1,0:T(8,128)(2,1)S(1)}, bf16[256,512]{1,0:T(8,128)(2,1)S(1)}, u32[]{:S(2)}, u32[]{:S(2)}) collective-permute-start(bf16[256,512]{1,0:T(8,128)(2,1)S(1)} %pad_maximum_fusion.refs_1_), channel_id=1, source_target_pairs={{0,2},{2,4},{4,6},{6,0},{1,3},{3,5},{5,7},{7,1},{8,10},{10,12},{12... | collective-permute-start | bytes 786440 | tf_op jit(solution)/shard_map/ppermute | solution.py:1044
  33.7 25.9 %collective-permute-start.2 = (bf16[2,256,1024]{2,1,0:T(8,128)(2,1)}, bf16[2,256,1024]{2,1,0:T(8,128)(2,1)}, u32[]{:S(2)}, u32[]{:S(2)}) collective-permute-start(bf16[2,256,1024]{2,1,0:T(8,128)(2,1)} %collective-permute-done.refs_5_.refs_2_), channel_id=1, source_target_pairs={{0,16},{1,9},{2,18},{3,11},{4,20},{5,13},{6,22},{7,15},{8,24},{9,1... | collective-permute-start | bytes 3145736 | tf_op jit(solution)/shard_map/ppermute | solution.py:1023
  60.6 36.7 %collective-permute-start.12 = (bf16[1024,512]{1,0:T(8,128)(2,1)}, bf16[1024,512]{1,0:T(8,128)(2,1)}, u32[]{:S(2)}, u32[]{:S(2)}) collective-permute-start(bf16[1024,512]{1,0:T(8,128)(2,1)} %hold.4.refs_6_.refs_2_.refs_10_), channel_id=1, source_target_pairs={{0,16},{1,9},{2,18},{3,11},{4,20},{5,13},{6,22},{7,15},{8,24},{9,1... | collective-permute-start | bytes 3145736 | tf_op jit(solution)/shard_map/ppermute | solution.py:1023
  61.0 34.5 %collective-permute-start.11 = (bf16[1024,512]{1,0:T(8,128)(2,1)}, bf16[1024,512]{1,0:T(8,128)(2,1)}, u32[]{:S(2)}, u32[]{:S(2)}) collective-permute-start(bf16[1024,512]{1,0:T(8,128)(2,1)} %hold.4.refs_6_.refs_2_.refs_10_), channel_id=1, source_target_pairs={{0,8},{1,17},{2,10},{3,19},{4,12},{5,21},{6,14},{7,23},{8,0},{9,25... | collective-permute-start | bytes 3145736 | tf_op jit(solution)/shard_map/ppermute | solution.py:1023
  63.3 59.9 %all-gather.5.cloned.1.call-start = ((), (), s32[]{:S(2)}) async-start(), calls=%async_computation.2 | async-start | bytes 2359296 | tf_op jit(solution)/shard_map/all_gather | solution.py:1134
  66.5 236.2 %reduce-scatter.3.cloned.1.call-start = ((), (), s32[]{:S(2)}) async-start(), calls=%async_computation.4 | async-start | bytes 2654208 | tf_op jit(solution)/shard_map/reduce_scatter | solution.py:1213
  95.5 37.2 %collective-permute-start.13 = (bf16[1024,512]{1,0:T(8,128)(2,1)}, bf16[1024,512]{1,0:T(8,128)(2,1)}, u32[]{:S(2)}, u32[]{:S(2)}) collective-permute-start(bf16[1024,512]{1,0:T(8,128)(2,1)} %collective-permute-done.11.refs_4_.refs_3_.refs_11_), channel_id=1, source_target_pairs={{0,16},{1,9},{2,18},{3,11},{4,20},{5,13},{6,22},{7,15},{8,24},{9,1... | collective-permute-start | bytes 3145736 | tf_op jit(solution)/shard_map/ppermute | solution.py:1023
  110.6 21.6 %collective-permute-start.14 = (bf16[512,1024]{1,0:T(8,128)(2,1)}, bf16[512,1024]{1,0:T(8,128)(2,1)}, u32[]{:S(2)}, u32[]{:S(2)}) collective-permute-start(bf16[512,1024]{1,0:T(8,128)(2,1)} %hold.7.refs_4_.refs_6_), channel_id=1, source_target_pairs={{0,8},{1,17},{2,10},{3,19},{4,12},{5,21},{6,14},{7,23},{8,0},{9,25... | collective-permute-start | bytes 3145736 | tf_op jit(solution)/shard_map/ppermute | solution.py:1023
  132.2 24.8 %collective-permute-start.16 = (bf16[512,1024]{1,0:T(8,128)(2,1)}, bf16[512,1024]{1,0:T(8,128)(2,1)S(1)}, u32[]{:S(2)}, u32[]{:S(2)}) collective-permute-start(bf16[512,1024]{1,0:T(8,128)(2,1)} %collective-permute-done.14.refs_10_.refs_5_.refs_7_), channel_id=1, source_target_pairs={{0,16},{1,9},{2,18},{3,11},{4,20},{5,13},{6,22},{7,15},{8,24},{9,1... | collective-permute-start | bytes 3145736 | tf_op jit(solution)/shard_map/ppermute | solution.py:1023
  182.5 32.1 %collective-permute-start.23 = (bf16[2,512,1024]{2,1,0:T(8,128)(2,1)}, bf16[2,512,1024]{2,1,0:T(8,128)(2,1)}, u32[]{:S(2)}, u32[]{:S(2)}) collective-permute-start(bf16[2,512,1024]{2,1,0:T(8,128)(2,1)} %down_grad.3.refs_0_), channel_id=1, source_target_pairs={{0,8},{1,17},{2,10},{3,19},{4,12},{5,21},{6,14},{7,23},{8,0},{9,25... | collective-permute-start | bytes 6291464 | tf_op jit(solution)/shard_map/ppermute | solution.py:1023
  210.9 19.3 %collective-permute-start.20 = (bf16[2,256,256]{2,1,0:T(8,128)(2,1)}, bf16[2,256,256]{2,1,0:T(8,128)(2,1)S(1)}, u32[]{:S(2)}, u32[]{:S(2)}) collective-permute-start(bf16[2,256,256]{2,1,0:T(8,128)(2,1)} %get-tuple-element.84), channel_id=1, source_target_pairs={{0,8},{1,17},{2,10},{3,19},{4,12},{5,21},{6,14},{7,23},{8,0},{9,25... | collective-permute-start | bytes 786440 | tf_op jit(solution)/shard_map/ppermute | solution.py:1040
  211.8 18.3 %collective-permute-start.21 = (bf16[2,256,256]{2,1,0:T(8,128)(2,1)}, bf16[2,256,256]{2,1,0:T(8,128)(2,1)S(1)}, u32[]{:S(2)}, u32[]{:S(2)}) collective-permute-start(bf16[2,256,256]{2,1,0:T(8,128)(2,1)} %get-tuple-element.85), channel_id=1, source_target_pairs={{0,16},{1,9},{2,18},{3,11},{4,20},{5,13},{6,22},{7,15},{8,24},{9,1... | collective-permute-start | bytes 786440 | tf_op jit(solution)/shard_map/ppermute | solution.py:1040
  212.9 17.3 %collective-permute-start.22 = (bf16[2,256,256]{2,1,0:T(8,128)(2,1)}, bf16[2,256,256]{2,1,0:T(8,128)(2,1)S(1)}, u32[]{:S(2)}, u32[]{:S(2)}) collective-permute-start(bf16[2,256,256]{2,1,0:T(8,128)(2,1)} %get-tuple-element.86), channel_id=1, source_target_pairs={{0,24},{1,25},{2,26},{3,27},{4,28},{5,29},{6,30},{7,31},{8,16},{9,... | collective-permute-start | bytes 786440 | tf_op jit(solution)/shard_map/ppermute | solution.py:1040
  219.6 27.7 %collective-permute-start.25 = (bf16[1,512,1024]{2,1,0:T(8,128)(2,1)}, bf16[1,512,1024]{2,1,0:T(8,128)(2,1)}, u32[]{:S(2)}, u32[]{:S(2)}) collective-permute-start(bf16[1,512,1024]{2,1,0:T(8,128)(2,1)} %down_grad.4.refs_4_), channel_id=1, source_target_pairs={{0,16},{1,9},{2,18},{3,11},{4,20},{5,13},{6,22},{7,15},{8,24},{9,1... | collective-permute-start | bytes 3145736 | tf_op jit(solution)/shard_map/ppermute | solution.py:1023
  226.2 33.6 %collective-permute-start.24 = (bf16[2,1024,512]{2,1,0:T(8,128)(2,1)}, bf16[2,1024,512]{2,1,0:T(8,128)(2,1)}, u32[]{:S(2)}, u32[]{:S(2)}) collective-permute-start(bf16[2,1024,512]{2,1,0:T(8,128)(2,1)} %up_grad.3.refs_7_), channel_id=1, source_target_pairs={{0,8},{1,17},{2,10},{3,19},{4,12},{5,21},{6,14},{7,23},{8,0},{9,25... | collective-permute-start | bytes 6291464 | tf_op jit(solution)/shard_map/ppermute | solution.py:1023
  230.1 118.9 %reduce-scatter.5.cloned.1.call-start = ((), (), s32[]{:S(2)}) async-start(), calls=%async_computation.5 | async-start | bytes 1990656 | tf_op jit(solution)/shard_map/reduce_scatter | solution.py:1242
  251.5 27.5 %collective-permute-start.27 = (bf16[128,1024]{1,0:T(8,128)(2,1)S(1)}, bf16[128,1024]{1,0:T(8,128)(2,1)S(1)}, u32[]{:S(2)}, u32[]{:S(2)}) collective-permute-start(bf16[128,1024]{1,0:T(8,128)(2,1)S(1)} %get-tuple-element.97), channel_id=1, source_target_pairs={{0,2},{2,4},{4,6},{6,0},{1,3},{3,5},{5,7},{7,1},{8,10},{10,12},{12... | collective-permute-start | bytes 786440 | tf_op jit(solution)/shard_map/ppermute | solution.py:1044
  253.0 26.1 %collective-permute-start.28 = (bf16[128,1024]{1,0:T(8,128)(2,1)S(1)}, bf16[128,1024]{1,0:T(8,128)(2,1)S(1)}, u32[]{:S(2)}, u32[]{:S(2)}) collective-permute-start(bf16[128,1024]{1,0:T(8,128)(2,1)S(1)} %get-tuple-element.98), channel_id=1, source_target_pairs={{0,4},{2,6},{4,0},{6,2},{1,5},{3,7},{5,1},{7,3},{8,12},{10,14},{12... | collective-permute-start | bytes 786440 | tf_op jit(solution)/shard_map/ppermute | solution.py:1044
  254.0 25.1 %collective-permute-start.29 = (bf16[128,1024]{1,0:T(8,128)(2,1)S(1)}, bf16[128,1024]{1,0:T(8,128)(2,1)S(1)}, u32[]{:S(2)}, u32[]{:S(2)}) collective-permute-start(bf16[128,1024]{1,0:T(8,128)(2,1)S(1)} %get-tuple-element.99), channel_id=1, source_target_pairs={{0,6},{2,0},{4,2},{6,4},{1,7},{3,1},{5,3},{7,5},{8,14},{10,8},{12,... | collective-permute-start | bytes 786440 | tf_op jit(solution)/shard_map/ppermute | solution.py:1044
  280.1 20.9 %collective-permute-start.35 = (bf16[128,1024]{1,0:T(8,128)(2,1)}, bf16[128,1024]{1,0:T(8,128)(2,1)}, u32[]{:S(2)}, u32[]{:S(2)}) collective-permute-start(bf16[128,1024]{1,0:T(8,128)(2,1)} %total_rows.1.refs_5_.refs_1_), channel_id=1, source_target_pairs={{0,16},{1,9},{2,18},{3,11},{4,20},{5,13},{6,22},{7,15},{8,24},{9,1... | collective-permute-start | bytes 786440 | tf_op jit(solution)/shard_map/ppermute | solution.py:1023
  287.4 24.4 %collective-permute-start.32 = (bf16[256,512]{1,0:T(8,128)(2,1)}, bf16[256,512]{1,0:T(8,128)(2,1)S(1)}, u32[]{:S(2)}, u32[]{:S(2)}) collective-permute-start(bf16[256,512]{1,0:T(8,128)(2,1)} %get-tuple-element.101), channel_id=1, source_target_pairs={{0,2},{2,4},{4,6},{6,0},{1,3},{3,5},{5,7},{7,1},{8,10},{10,12},{12... | collective-permute-start | bytes 786440 | tf_op jit(solution)/shard_map/ppermute | solution.py:1044
  293.0 19.5 %collective-permute-start.33 = (bf16[256,512]{1,0:T(8,128)(2,1)}, bf16[256,512]{1,0:T(8,128)(2,1)}, u32[]{:S(2)}, u32[]{:S(2)}) collective-permute-start(bf16[256,512]{1,0:T(8,128)(2,1)} %get-tuple-element.102), channel_id=1, source_target_pairs={{0,4},{2,6},{4,0},{6,2},{1,5},{3,7},{5,1},{7,3},{8,12},{10,14},{12... | collective-permute-start | bytes 786440 | tf_op jit(solution)/shard_map/ppermute | solution.py:1044
  295.1 17.4 %collective-permute-start.34 = (bf16[256,512]{1,0:T(8,128)(2,1)}, bf16[256,512]{1,0:T(8,128)(2,1)}, u32[]{:S(2)}, u32[]{:S(2)}) collective-permute-start(bf16[256,512]{1,0:T(8,128)(2,1)} %get-tuple-element.103), channel_id=1, source_target_pairs={{0,6},{2,0},{4,2},{6,4},{1,7},{3,1},{5,3},{7,5},{8,14},{10,8},{12,... | collective-permute-start | bytes 786440 | tf_op jit(solution)/shard_map/ppermute | solution.py:1044
  301.1 40.9 %collective-permute-start.31 = (bf16[2,2,256,1024]{3,2,1,0:T(8,128)(2,1)}, bf16[2,2,256,1024]{3,2,1,0:T(8,128)(2,1)}, u32[]{:S(2)}, u32[]{:S(2)}) collective-permute-start(bf16[2,2,256,1024]{3,2,1,0:T(8,128)(2,1)} %hidden_grad.3.refs_6_), channel_id=1, source_target_pairs={{0,8},{1,17},{2,10},{3,19},{4,12},{5,21},{6,14},{7,23},{8,0},{9,25... | collective-permute-start | bytes 6291464 | tf_op jit(solution)/shard_map/ppermute | solution.py:1023
  322.5 17.6 %collective-permute-start.44 = (bf16[2,128,512]{2,1,0:T(8,128)(2,1)S(1)}, bf16[2,128,512]{2,1,0:T(8,128)(2,1)}, u32[]{:S(2)}, u32[]{:S(2)}) collective-permute-start(bf16[2,128,512]{2,1,0:T(8,128)(2,1)S(1)} %pair.1.refs_4_.refs_1_), channel_id=1, source_target_pairs={{0,8},{1,17},{2,10},{3,19},{4,12},{5,21},{6,14},{7,23},{8,0},{9,25... | collective-permute-start | bytes 786440 | tf_op jit(solution)/shard_map/ppermute | solution.py:1023
  324.1 25.6 %collective-permute-start.45 = (bf16[2,128,512]{2,1,0:T(8,128)(2,1)S(1)}, bf16[2,128,512]{2,1,0:T(8,128)(2,1)}, u32[]{:S(2)}, u32[]{:S(2)}) collective-permute-start(bf16[2,128,512]{2,1,0:T(8,128)(2,1)S(1)} %pair.1.refs_4_.refs_1_), channel_id=1, source_target_pairs={{0,16},{1,9},{2,18},{3,11},{4,20},{5,13},{6,22},{7,15},{8,24},{9,1... | collective-permute-start | bytes 786440 | tf_op jit(solution)/shard_map/ppermute | solution.py:1023
  (83 other events, 873.0 us)
Sparse Core Ops, SparseCore 0:
  15.2 44.7 all-gather.8
  63.4 28.9 all-gather.6
  94.5 28.6 all-gather.4
  230.2 41.7 reduce-scatter.2
  311.9 33.2 reduce-scatter.4
